TPU v7x, 32 devices: a whole 2x2x4 slice. The times are simulated.
32 devices in a mesh: tm: 2 (over core), space: 16 (over z, y, x).
Axes of the slice: x: 2, y: 2, z: 4, core: 2. Of those that a mesh axis runs over, the one named last changes fastest.
Arguments:
- start_states: float32 [2, 3, 128, 4096], P('tm', None, 'space'), may hold values from -6 to 6
- coarse_gain: float32 [3, 128, 4096], P(None, 'space'), may hold values from 0.55 to 0.95
- depth_level: int32 [128, 4096], P('space'), may hold values from 0 to 63
- depth_table: float32 [64], replicated, may hold values from 0.2 to 1
- wet: int32 [128, 4096], P('space'), may hold values 0 or 1
- block_count: int32 [16], P('space'), may hold values from 1 to 8, 80 in all
- neighbour: int32 [128, 4], P('space'), may hold values from -1 to 7
- coriolis: float32 [128, 4096], P('space'), may hold values from -0.5 to 0.5
- tide: float32 [2, 128, 4096], P(None, 'space'), may hold values from -2 to 2
Outputs:
- new_states: float32 [2, 3, 128, 4096], P('tm', None, 'space')
Inputs may be any that keep to these rules, and one draw needn't show every extreme that they name: `block_count`: each column's count is the number of its first slots that hold ocean blocks; some column holds 8. `neighbour`: entries 0 and 1 name slots of the same column, entries 2 and 3 slots of the next and the previous column along the periodic longitude; -1 is a closed face.
All inputs are finite; a program needn't handle non-finite values. No bound on the sum of `wet` on one device may be relied on, other than what follows from the above.
Results may differ from a plain program's by a relative error of at most 0.00007.
Values sent between devices are 32-bit elements; how exact they have to be, the bound alone decides.
No kernel may reach another device: no remote copies, remote signals or barrier semaphores. Data moves between devices by JAX's collectives and lax.ppermute only.
A program may use at most 64 MiB of HBM per device.

v0:
```python
import math

import jax
import jax.numpy as jnp
from jax import lax
from jax.sharding import PartitionSpec as P

BS = 64
STEPS = 6
LEVELS = 64


def padded(block, sides, width):
    for axis, dim in sides:
        count = lax.axis_size(axis)
        forward = [(i, i + 1) for i in range(count - 1)]
        forward.append((count - 1, 0))
        backward = [(target, source) for source, target in forward]
        low = lax.ppermute(
            lax.slice_in_dim(block, block.shape[dim] - width, None, axis=dim), axis, forward
        )
        high = lax.ppermute(lax.slice_in_dim(block, 0, width, axis=dim), axis, backward)
        block = jnp.concatenate([low, block, high], axis=dim)
    return block


def passed_along(shard, axis, by):
    size = lax.axis_size(axis)
    return lax.ppermute(shard, axis, [(i, (i + by) % size) for i in range(size)])


def take_edges(edges, index):
    select = (index[:, None] == jnp.arange(edges.shape[0])[None, :]).astype(edges.dtype)
    return jnp.dot(
        select, edges, precision=lax.Precision.HIGHEST, preferred_element_type=jnp.float32
    )


def across(field, west_ghost, east_ghost):
    column = jnp.arange(field.shape[-1]) % BS
    zero = jnp.zeros(field.shape[:-1] + (1,), field.dtype)
    east = jnp.where(
        column == BS - 1,
        jnp.repeat(east_ghost, BS, axis=-1),
        jnp.concatenate([field[:, 1:], zero], -1),
    )
    west = jnp.where(
        column == 0, jnp.repeat(west_ghost, BS, axis=-1), jnp.concatenate([zero, field[:, :-1]], -1)
    )
    return 0.5 * (east - west)


def along(field, north_ghost, south_ghost):
    north = jnp.concatenate([field[:, BS:], north_ghost], -1)
    south = jnp.concatenate([south_ghost, field[:, :-BS]], -1)
    return 0.5 * (north - south)


def edge_pair(field):
    return jnp.stack([field[:, 0::BS], field[:, BS - 1 :: BS]])


def body(
    start_states, coarse_gain, depth_level, depth_table, wet, block_count, neighbour, coriolis, tide
):
    slots_here = wet.shape[0]
    slot = jnp.arange(slots_here)
    live = wet.astype(jnp.float32) * (slot < block_count[0]).astype(jnp.float32)[:, None]
    level_ids = jnp.arange(LEVELS)[:, None]

    def depth_row(levels):
        return jnp.sum(
            jnp.where(levels[None, :] == level_ids, depth_table[:, None], jnp.float32(0.0)), axis=0
        )

    depth = lax.map(depth_row, depth_level)
    north_id = neighbour[:, 0]
    south_id = neighbour[:, 1]
    east_id = neighbour[:, 2]
    west_id = neighbour[:, 3]
    start = start_states * live
    slices = lax.axis_size("tm")
    omega = 2.0 * math.pi / (slices * STEPS)
    first_time = lax.axis_index("tm").astype(jnp.float32) * STEPS
    level, east_vel, north_vel = (start[0, 0], start[0, 1], start[0, 2])
    for step in range(STEPS):
        angle = (first_time + step) * omega
        source = tide[0] * jnp.cos(angle) + tide[1] * jnp.sin(angle)
        flux_x = depth * east_vel
        flux_y = depth * north_vel
        bordered = padded(edge_pair(flux_x), (("space", 0),), 1)
        div = across(flux_x, take_edges(bordered[0], west_id), take_edges(bordered[3], east_id))
        div = div + along(
            flux_y, take_edges(flux_y[:, :BS], north_id), take_edges(flux_y[:, -BS:], south_id)
        )
        level = (level + 0.3 * (source - div)) * live
        bordered = padded(edge_pair(level), (("space", 0),), 1)
        slope_x = across(level, take_edges(bordered[0], west_id), take_edges(bordered[3], east_id))
        slope_y = along(
            level, take_edges(level[:, :BS], north_id), take_edges(level[:, -BS:], south_id)
        )
        new_east = (east_vel + 0.3 * (coriolis * north_vel - slope_x - 0.05 * east_vel)) * live
        north_vel = (north_vel + 0.3 * (-coriolis * east_vel - slope_y - 0.05 * north_vel)) * live
        east_vel = new_east
    fine = jnp.stack([level, east_vel, north_vel])[None]
    defect = fine - coarse_gain * start

    def advance(turn, partial_sum):
        return defect + coarse_gain * passed_along(partial_sum, "tm", 1)

    partial_sum = lax.fori_loop(0, slices - 1, advance, defect)
    total = passed_along(partial_sum, "tm", 1)
    return total / (1.0 - coarse_gain**slices)


def solution(mesh):
    return jax.shard_map(
        body,
        mesh=mesh,
        in_specs=(
            P("tm", None, "space", None),
            P(None, "space", None),
            P("space", None),
            P(),
            P("space", None),
            P("space"),
            P("space", None),
            P("space", None),
            P(None, "space", None),
        ),
        out_specs=P("tm", None, "space", None),
        check_vma=False,
    )
```

profile of v0, /device:TPU:0, one launch (start us, length us, event | category | flops | bytes accessed | tf_op | source)
XLA Modules:
  0.0 134.5 jit_solution(13900898908548187878)
XLA Ops:
  0.7 12.7 %while.3 = (s32[]{:T(128)}, f32[8,4096]{1,0:T(8,128)S(1)}, s32[8,4096]{1,0:T(8,128)}, f32[64]{0:T(128)S(1)}, s32[]{:T(128)}, /*index=5*/s32[]{:T(128)}) while((s32[]{:T(128)}, f32[8,4096]{1,0:T(8,128)S(1)}, s32[8,4096]{1,0:T(8,128)}, f32[64]{0:T(128)S(1)}, s32[]{:T(128)}, /*index=5*/s32[]{:T(128)}) %tuple.76), condition=%wide.region_2.3_spmd.clone, body=%wide.region_0.2_spmd.clone.sunk | while | flops 782338 | bytes 98637 | solution.py:76
  0.7 1.0 constant_dynamic-slice_fusion.2
  2.3 0.9 constant_dynamic-slice_fusion.2
  3.9 0.9 constant_dynamic-slice_fusion.2
  5.5 0.9 constant_dynamic-slice_fusion.2
  7.1 0.9 constant_dynamic-slice_fusion.2
  8.6 0.9 constant_dynamic-slice_fusion.2
  10.2 0.9 constant_dynamic-slice_fusion.2
  11.8 0.9 constant_dynamic-slice_fusion.2
  13.5 1.0 broadcast_multiply_fusion
  14.7 7.0 %collective-permute-start = (f32[1,8,64]{2,1,0:T(8,128)S(1)}, f32[1,8,64]{2,1,0:T(8,128)S(1)}, u32[]{:S(2)}, u32[]{:S(2)}) collective-permute-start(f32[1,8,64]{2,1,0:T(8,128)S(1)} %bitcast.172), channel_id=1, source_target_pairs={{1,0},{2,1},{3,2},{4,3},{5,4},{6,5},{7,6},{8,7},{9,8},{10,9},{11,1... | collective-permute-start | bytes 6152 | tf_op jit(solution)/shard_map/ppermute | solution.py:22
  24.4 4.7 %collective-permute-done.1 = f32[1,8,64]{2,1,0:T(8,128)S(1)} collective-permute-done((f32[1,8,64]{2,1,0:T(8,128)S(1)}, f32[1,8,64]{2,1,0:T(8,128)S(1)}, u32[]{:S(2)}, u32[]{:S(2)}) %collective-permute-start.1) | collective-permute-done | bytes 2080 | tf_op jit(solution)/shard_map/ppermute | solution.py:19
  31.9 1.6 %collective-permute-start.3 = (f32[1,8,64]{2,1,0:T(8,128)S(1)}, f32[1,8,64]{2,1,0:T(8,128)S(1)}, u32[]{:S(2)}, u32[]{:S(2)}) collective-permute-start(f32[1,8,64]{2,1,0:T(8,128)S(1)} %bitcast.190), channel_id=1, source_target_pairs={{0,1},{1,2},{2,3},{3,4},{4,5},{5,6},{6,7},{7,8},{8,9},{9,10},{10,1... | collective-permute-start | bytes 6152 | tf_op jit(solution)/shard_map/ppermute | solution.py:19
  33.5 1.2 collective-permute-done.2
  35.2 4.0 %collective-permute-done.3 = f32[1,8,64]{2,1,0:T(8,128)S(1)} collective-permute-done((f32[1,8,64]{2,1,0:T(8,128)S(1)}, f32[1,8,64]{2,1,0:T(8,128)S(1)}, u32[]{:S(2)}, u32[]{:S(2)}) %collective-permute-start.3) | collective-permute-done | bytes 2080 | tf_op jit(solution)/shard_map/ppermute | solution.py:19
  41.5 2.0 %collective-permute-start.5 = (f32[1,8,64]{2,1,0:T(8,128)S(1)}, f32[1,8,64]{2,1,0:T(8,128)S(1)}, u32[]{:S(2)}, u32[]{:S(2)}) collective-permute-start(f32[1,8,64]{2,1,0:T(8,128)S(1)} %bitcast.184), channel_id=1, source_target_pairs={{0,1},{1,2},{2,3},{3,4},{4,5},{5,6},{6,7},{7,8},{8,9},{9,10},{10,1... | collective-permute-start | bytes 6152 | tf_op jit(solution)/shard_map/ppermute | solution.py:19
  43.5 1.2 collective-permute-done.4
  45.2 3.6 %collective-permute-done.5 = f32[1,8,64]{2,1,0:T(8,128)S(1)} collective-permute-done((f32[1,8,64]{2,1,0:T(8,128)S(1)}, f32[1,8,64]{2,1,0:T(8,128)S(1)}, u32[]{:S(2)}, u32[]{:S(2)}) %collective-permute-start.5) | collective-permute-done | bytes 2080 | tf_op jit(solution)/shard_map/ppermute | solution.py:19
  50.3 2.0 %collective-permute-start.7 = (f32[1,8,64]{2,1,0:T(8,128)S(1)}, f32[1,8,64]{2,1,0:T(8,128)S(1)}, u32[]{:S(2)}, u32[]{:S(2)}) collective-permute-start(f32[1,8,64]{2,1,0:T(8,128)S(1)} %bitcast.191), channel_id=1, source_target_pairs={{0,1},{1,2},{2,3},{3,4},{4,5},{5,6},{6,7},{7,8},{8,9},{9,10},{10,1... | collective-permute-start | bytes 6152 | tf_op jit(solution)/shard_map/ppermute | solution.py:19
  52.4 1.2 collective-permute-done.6
  54.0 3.6 %collective-permute-done.7 = f32[1,8,64]{2,1,0:T(8,128)S(1)} collective-permute-done((f32[1,8,64]{2,1,0:T(8,128)S(1)}, f32[1,8,64]{2,1,0:T(8,128)S(1)}, u32[]{:S(2)}, u32[]{:S(2)}) %collective-permute-start.7) | collective-permute-done | bytes 2080 | tf_op jit(solution)/shard_map/ppermute | solution.py:19
  59.2 2.0 %collective-permute-start.9 = (f32[1,8,64]{2,1,0:T(8,128)S(1)}, f32[1,8,64]{2,1,0:T(8,128)S(1)}, u32[]{:S(2)}, u32[]{:S(2)}) collective-permute-start(f32[1,8,64]{2,1,0:T(8,128)S(1)} %bitcast.185), channel_id=1, source_target_pairs={{0,1},{1,2},{2,3},{3,4},{4,5},{5,6},{6,7},{7,8},{8,9},{9,10},{10,1... | collective-permute-start | bytes 6152 | tf_op jit(solution)/shard_map/ppermute | solution.py:19
  61.2 1.2 collective-permute-done.8
  62.9 3.6 %collective-permute-done.9 = f32[1,8,64]{2,1,0:T(8,128)S(1)} collective-permute-done((f32[1,8,64]{2,1,0:T(8,128)S(1)}, f32[1,8,64]{2,1,0:T(8,128)S(1)}, u32[]{:S(2)}, u32[]{:S(2)}) %collective-permute-start.9) | collective-permute-done | bytes 2080 | tf_op jit(solution)/shard_map/ppermute | solution.py:19
  68.0 2.0 %collective-permute-start.11 = (f32[1,8,64]{2,1,0:T(8,128)S(1)}, f32[1,8,64]{2,1,0:T(8,128)S(1)}, u32[]{:S(2)}, u32[]{:S(2)}) collective-permute-start(f32[1,8,64]{2,1,0:T(8,128)S(1)} %bitcast.192), channel_id=1, source_target_pairs={{0,1},{1,2},{2,3},{3,4},{4,5},{5,6},{6,7},{7,8},{8,9},{9,10},{10,1... | collective-permute-start | bytes 6152 | tf_op jit(solution)/shard_map/ppermute | solution.py:19
  70.0 1.2 collective-permute-done.10
  71.7 3.6 %collective-permute-done.11 = f32[1,8,64]{2,1,0:T(8,128)S(1)} collective-permute-done((f32[1,8,64]{2,1,0:T(8,128)S(1)}, f32[1,8,64]{2,1,0:T(8,128)S(1)}, u32[]{:S(2)}, u32[]{:S(2)}) %collective-permute-start.11) | collective-permute-done | bytes 2080 | tf_op jit(solution)/shard_map/ppermute | solution.py:19
  76.9 2.0 %collective-permute-start.13 = (f32[1,8,64]{2,1,0:T(8,128)S(1)}, f32[1,8,64]{2,1,0:T(8,128)S(1)}, u32[]{:S(2)}, u32[]{:S(2)}) collective-permute-start(f32[1,8,64]{2,1,0:T(8,128)S(1)} %bitcast.186), channel_id=1, source_target_pairs={{0,1},{1,2},{2,3},{3,4},{4,5},{5,6},{6,7},{7,8},{8,9},{9,10},{10,1... | collective-permute-start | bytes 6152 | tf_op jit(solution)/shard_map/ppermute | solution.py:19
  78.9 1.2 collective-permute-done.12
  80.5 3.6 %collective-permute-done.13 = f32[1,8,64]{2,1,0:T(8,128)S(1)} collective-permute-done((f32[1,8,64]{2,1,0:T(8,128)S(1)}, f32[1,8,64]{2,1,0:T(8,128)S(1)}, u32[]{:S(2)}, u32[]{:S(2)}) %collective-permute-start.13) | collective-permute-done | bytes 2080 | tf_op jit(solution)/shard_map/ppermute | solution.py:19
  85.7 2.0 %collective-permute-start.15 = (f32[1,8,64]{2,1,0:T(8,128)S(1)}, f32[1,8,64]{2,1,0:T(8,128)S(1)}, u32[]{:S(2)}, u32[]{:S(2)}) collective-permute-start(f32[1,8,64]{2,1,0:T(8,128)S(1)} %bitcast.193), channel_id=1, source_target_pairs={{0,1},{1,2},{2,3},{3,4},{4,5},{5,6},{6,7},{7,8},{8,9},{9,10},{10,1... | collective-permute-start | bytes 6152 | tf_op jit(solution)/shard_map/ppermute | solution.py:19
  87.7 1.2 collective-permute-done.14
  89.4 3.6 %collective-permute-done.15 = f32[1,8,64]{2,1,0:T(8,128)S(1)} collective-permute-done((f32[1,8,64]{2,1,0:T(8,128)S(1)}, f32[1,8,64]{2,1,0:T(8,128)S(1)}, u32[]{:S(2)}, u32[]{:S(2)}) %collective-permute-start.15) | collective-permute-done | bytes 2080 | tf_op jit(solution)/shard_map/ppermute | solution.py:19
  94.6 2.0 %collective-permute-start.17 = (f32[1,8,64]{2,1,0:T(8,128)S(1)}, f32[1,8,64]{2,1,0:T(8,128)S(1)}, u32[]{:S(2)}, u32[]{:S(2)}) collective-permute-start(f32[1,8,64]{2,1,0:T(8,128)S(1)} %bitcast.187), channel_id=1, source_target_pairs={{0,1},{1,2},{2,3},{3,4},{4,5},{5,6},{6,7},{7,8},{8,9},{9,10},{10,1... | collective-permute-start | bytes 6152 | tf_op jit(solution)/shard_map/ppermute | solution.py:19
  96.6 1.2 collective-permute-done.16
  98.2 3.6 %collective-permute-done.17 = f32[1,8,64]{2,1,0:T(8,128)S(1)} collective-permute-done((f32[1,8,64]{2,1,0:T(8,128)S(1)}, f32[1,8,64]{2,1,0:T(8,128)S(1)}, u32[]{:S(2)}, u32[]{:S(2)}) %collective-permute-start.17) | collective-permute-done | bytes 2080 | tf_op jit(solution)/shard_map/ppermute | solution.py:19
  103.4 2.0 %collective-permute-start.19 = (f32[1,8,64]{2,1,0:T(8,128)S(1)}, f32[1,8,64]{2,1,0:T(8,128)S(1)}, u32[]{:S(2)}, u32[]{:S(2)}) collective-permute-start(f32[1,8,64]{2,1,0:T(8,128)S(1)} %bitcast.194), channel_id=1, source_target_pairs={{0,1},{1,2},{2,3},{3,4},{4,5},{5,6},{6,7},{7,8},{8,9},{9,10},{10,1... | collective-permute-start | bytes 6152 | tf_op jit(solution)/shard_map/ppermute | solution.py:19
  105.4 1.2 collective-permute-done.18
  107.0 3.6 %collective-permute-done.19 = f32[1,8,64]{2,1,0:T(8,128)S(1)} collective-permute-done((f32[1,8,64]{2,1,0:T(8,128)S(1)}, f32[1,8,64]{2,1,0:T(8,128)S(1)}, u32[]{:S(2)}, u32[]{:S(2)}) %collective-permute-start.19) | collective-permute-done | bytes 2080 | tf_op jit(solution)/shard_map/ppermute | solution.py:19
  112.3 2.0 %collective-permute-start.21 = (f32[1,8,64]{2,1,0:T(8,128)S(1)}, f32[1,8,64]{2,1,0:T(8,128)S(1)}, u32[]{:S(2)}, u32[]{:S(2)}) collective-permute-start(f32[1,8,64]{2,1,0:T(8,128)S(1)} %bitcast.188), channel_id=1, source_target_pairs={{0,1},{1,2},{2,3},{3,4},{4,5},{5,6},{6,7},{7,8},{8,9},{9,10},{10,1... | collective-permute-start | bytes 6152 | tf_op jit(solution)/shard_map/ppermute | solution.py:19
  114.3 1.2 collective-permute-done.20
  115.9 3.6 %collective-permute-done.21 = f32[1,8,64]{2,1,0:T(8,128)S(1)} collective-permute-done((f32[1,8,64]{2,1,0:T(8,128)S(1)}, f32[1,8,64]{2,1,0:T(8,128)S(1)}, u32[]{:S(2)}, u32[]{:S(2)}) %collective-permute-start.21) | collective-permute-done | bytes 2080 | tf_op jit(solution)/shard_map/ppermute | solution.py:19
  121.1 2.0 %collective-permute-start.23 = (f32[1,8,64]{2,1,0:T(8,128)S(1)}, f32[1,8,64]{2,1,0:T(8,128)S(1)}, u32[]{:S(2)}, u32[]{:S(2)}) collective-permute-start(f32[1,8,64]{2,1,0:T(8,128)S(1)} %bitcast.189), channel_id=1, source_target_pairs={{0,1},{1,2},{2,3},{3,4},{4,5},{5,6},{6,7},{7,8},{8,9},{9,10},{10,1... | collective-permute-start | bytes 6152 | tf_op jit(solution)/shard_map/ppermute | solution.py:19
  123.1 1.2 collective-permute-done.22
  124.7 3.6 %collective-permute-done.23 = f32[1,8,64]{2,1,0:T(8,128)S(1)} collective-permute-done((f32[1,8,64]{2,1,0:T(8,128)S(1)}, f32[1,8,64]{2,1,0:T(8,128)S(1)}, u32[]{:S(2)}, u32[]{:S(2)}) %collective-permute-start.23) | collective-permute-done | bytes 2080 | tf_op jit(solution)/shard_map/ppermute | solution.py:19
  130.0 1.7 %collective-permute-done.24 = f32[1,3,8,4096]{3,2,1,0:T(8,128)S(1)} collective-permute-done((f32[1,3,8,4096]{3,2,1,0:T(8,128)S(1)}, f32[1,3,8,4096]{3,2,1,0:T(8,128)S(1)}, u32[]{:S(2)}, u32[]{:S(2)}) %collective-permute-start.24) | collective-permute-done | bytes 393248 | tf_op jit(solution)/shard_map/while/body/eval_jaxpr/ppermute | solution.py:29
  132.0 1.6 %collective-permute-done.25 = f32[1,3,8,4096]{3,2,1,0:T(8,128)S(1)} collective-permute-done((f32[1,3,8,4096]{3,2,1,0:T(8,128)S(1)}, f32[1,3,8,4096]{3,2,1,0:T(8,128)S(1)}, u32[]{:S(2)}, u32[]{:S(2)}) %collective-permute-start.25) | collective-permute-done | bytes 393248 | tf_op jit(solution)/shard_map/ppermute | solution.py:29
  133.6 0.8 bitcast_divide_fusion
  (209 shorter events, 32.8 us)
Async XLA Ops:
  0.0 0.7 copy-start.5
  0.7 12.7 %copy-start = (s32[8,4096]{1,0:T(8,128)S(1)}, s32[8,4096]{1,0:T(8,128)}, u32[]{:S(2)}) copy-start(s32[8,4096]{1,0:T(8,128)} %param.15) | copy-start | bytes 393220
  14.7 9.3 %collective-permute-start = (f32[1,8,64]{2,1,0:T(8,128)S(1)}, f32[1,8,64]{2,1,0:T(8,128)S(1)}, u32[]{:S(2)}, u32[]{:S(2)}) collective-permute-start(f32[1,8,64]{2,1,0:T(8,128)S(1)} %bitcast.172), channel_id=1, source_target_pairs={{1,0},{2,1},{3,2},{4,3},{5,4},{6,5},{7,6},{8,7},{9,8},{10,9},{11,1... | collective-permute-start | bytes 6152 | tf_op jit(solution)/shard_map/ppermute | solution.py:22
  21.8 0.7 copy-start.6
  21.8 7.3 %collective-permute-start.1 = (f32[1,8,64]{2,1,0:T(8,128)S(1)}, f32[1,8,64]{2,1,0:T(8,128)S(1)}, u32[]{:S(2)}, u32[]{:S(2)}) collective-permute-start(f32[1,8,64]{2,1,0:T(8,128)S(1)} %bitcast.171), channel_id=1, source_target_pairs={{0,1},{1,2},{2,3},{3,4},{4,5},{5,6},{6,7},{7,8},{8,9},{9,10},{10,1... | collective-permute-start | bytes 6152 | tf_op jit(solution)/shard_map/ppermute | solution.py:19
  29.4 1.0 copy-start.1
  31.1 3.7 %collective-permute-start.2 = (f32[1,8,64]{2,1,0:T(8,128)S(1)}, f32[1,8,64]{2,1,0:T(8,128)S(1)}, u32[]{:S(2)}, u32[]{:S(2)}) collective-permute-start(f32[1,8,64]{2,1,0:T(8,128)S(1)} %bitcast.179), channel_id=1, source_target_pairs={{1,0},{2,1},{3,2},{4,3},{5,4},{6,5},{7,6},{8,7},{9,8},{10,9},{11,1... | collective-permute-start | bytes 6152 | tf_op jit(solution)/shard_map/ppermute | solution.py:22
  31.9 7.3 %collective-permute-start.3 = (f32[1,8,64]{2,1,0:T(8,128)S(1)}, f32[1,8,64]{2,1,0:T(8,128)S(1)}, u32[]{:S(2)}, u32[]{:S(2)}) collective-permute-start(f32[1,8,64]{2,1,0:T(8,128)S(1)} %bitcast.190), channel_id=1, source_target_pairs={{0,1},{1,2},{2,3},{3,4},{4,5},{5,6},{6,7},{7,8},{8,9},{9,10},{10,1... | collective-permute-start | bytes 6152 | tf_op jit(solution)/shard_map/ppermute | solution.py:19
  39.5 0.9 copy-start.2
  41.1 3.6 %collective-permute-start.4 = (f32[1,8,64]{2,1,0:T(8,128)S(1)}, f32[1,8,64]{2,1,0:T(8,128)S(1)}, u32[]{:S(2)}, u32[]{:S(2)}) collective-permute-start(f32[1,8,64]{2,1,0:T(8,128)S(1)} %bitcast.173), channel_id=1, source_target_pairs={{1,0},{2,1},{3,2},{4,3},{5,4},{6,5},{7,6},{8,7},{9,8},{10,9},{11,1... | collective-permute-start | bytes 6152 | tf_op jit(solution)/shard_map/ppermute | solution.py:22
  41.5 7.3 %collective-permute-start.5 = (f32[1,8,64]{2,1,0:T(8,128)S(1)}, f32[1,8,64]{2,1,0:T(8,128)S(1)}, u32[]{:S(2)}, u32[]{:S(2)}) collective-permute-start(f32[1,8,64]{2,1,0:T(8,128)S(1)} %bitcast.184), channel_id=1, source_target_pairs={{0,1},{1,2},{2,3},{3,4},{4,5},{5,6},{6,7},{7,8},{8,9},{9,10},{10,1... | collective-permute-start | bytes 6152 | tf_op jit(solution)/shard_map/ppermute | solution.py:19
  49.9 3.6 %collective-permute-start.6 = (f32[1,8,64]{2,1,0:T(8,128)S(1)}, f32[1,8,64]{2,1,0:T(8,128)S(1)}, u32[]{:S(2)}, u32[]{:S(2)}) collective-permute-start(f32[1,8,64]{2,1,0:T(8,128)S(1)} %bitcast.180), channel_id=1, source_target_pairs={{1,0},{2,1},{3,2},{4,3},{5,4},{6,5},{7,6},{8,7},{9,8},{10,9},{11,1... | collective-permute-start | bytes 6152 | tf_op jit(solution)/shard_map/ppermute | solution.py:22
  50.3 7.3 %collective-permute-start.7 = (f32[1,8,64]{2,1,0:T(8,128)S(1)}, f32[1,8,64]{2,1,0:T(8,128)S(1)}, u32[]{:S(2)}, u32[]{:S(2)}) collective-permute-start(f32[1,8,64]{2,1,0:T(8,128)S(1)} %bitcast.191), channel_id=1, source_target_pairs={{0,1},{1,2},{2,3},{3,4},{4,5},{5,6},{6,7},{7,8},{8,9},{9,10},{10,1... | collective-permute-start | bytes 6152 | tf_op jit(solution)/shard_map/ppermute | solution.py:19
  58.8 3.6 %collective-permute-start.8 = (f32[1,8,64]{2,1,0:T(8,128)S(1)}, f32[1,8,64]{2,1,0:T(8,128)S(1)}, u32[]{:S(2)}, u32[]{:S(2)}) collective-permute-start(f32[1,8,64]{2,1,0:T(8,128)S(1)} %bitcast.174), channel_id=1, source_target_pairs={{1,0},{2,1},{3,2},{4,3},{5,4},{6,5},{7,6},{8,7},{9,8},{10,9},{11,1... | collective-permute-start | bytes 6152 | tf_op jit(solution)/shard_map/ppermute | solution.py:22
  59.2 7.3 %collective-permute-start.9 = (f32[1,8,64]{2,1,0:T(8,128)S(1)}, f32[1,8,64]{2,1,0:T(8,128)S(1)}, u32[]{:S(2)}, u32[]{:S(2)}) collective-permute-start(f32[1,8,64]{2,1,0:T(8,128)S(1)} %bitcast.185), channel_id=1, source_target_pairs={{0,1},{1,2},{2,3},{3,4},{4,5},{5,6},{6,7},{7,8},{8,9},{9,10},{10,1... | collective-permute-start | bytes 6152 | tf_op jit(solution)/shard_map/ppermute | solution.py:19
  67.6 3.6 %collective-permute-start.10 = (f32[1,8,64]{2,1,0:T(8,128)S(1)}, f32[1,8,64]{2,1,0:T(8,128)S(1)}, u32[]{:S(2)}, u32[]{:S(2)}) collective-permute-start(f32[1,8,64]{2,1,0:T(8,128)S(1)} %bitcast.181), channel_id=1, source_target_pairs={{1,0},{2,1},{3,2},{4,3},{5,4},{6,5},{7,6},{8,7},{9,8},{10,9},{11,1... | collective-permute-start | bytes 6152 | tf_op jit(solution)/shard_map/ppermute | solution.py:22
  68.0 7.3 %collective-permute-start.11 = (f32[1,8,64]{2,1,0:T(8,128)S(1)}, f32[1,8,64]{2,1,0:T(8,128)S(1)}, u32[]{:S(2)}, u32[]{:S(2)}) collective-permute-start(f32[1,8,64]{2,1,0:T(8,128)S(1)} %bitcast.192), channel_id=1, source_target_pairs={{0,1},{1,2},{2,3},{3,4},{4,5},{5,6},{6,7},{7,8},{8,9},{9,10},{10,1... | collective-permute-start | bytes 6152 | tf_op jit(solution)/shard_map/ppermute | solution.py:19
  76.5 3.6 %collective-permute-start.12 = (f32[1,8,64]{2,1,0:T(8,128)S(1)}, f32[1,8,64]{2,1,0:T(8,128)S(1)}, u32[]{:S(2)}, u32[]{:S(2)}) collective-permute-start(f32[1,8,64]{2,1,0:T(8,128)S(1)} %bitcast.175), channel_id=1, source_target_pairs={{1,0},{2,1},{3,2},{4,3},{5,4},{6,5},{7,6},{8,7},{9,8},{10,9},{11,1... | collective-permute-start | bytes 6152 | tf_op jit(solution)/shard_map/ppermute | solution.py:22
  76.9 7.3 %collective-permute-start.13 = (f32[1,8,64]{2,1,0:T(8,128)S(1)}, f32[1,8,64]{2,1,0:T(8,128)S(1)}, u32[]{:S(2)}, u32[]{:S(2)}) collective-permute-start(f32[1,8,64]{2,1,0:T(8,128)S(1)} %bitcast.186), channel_id=1, source_target_pairs={{0,1},{1,2},{2,3},{3,4},{4,5},{5,6},{6,7},{7,8},{8,9},{9,10},{10,1... | collective-permute-start | bytes 6152 | tf_op jit(solution)/shard_map/ppermute | solution.py:19
  85.3 3.6 %collective-permute-start.14 = (f32[1,8,64]{2,1,0:T(8,128)S(1)}, f32[1,8,64]{2,1,0:T(8,128)S(1)}, u32[]{:S(2)}, u32[]{:S(2)}) collective-permute-start(f32[1,8,64]{2,1,0:T(8,128)S(1)} %bitcast.182), channel_id=1, source_target_pairs={{1,0},{2,1},{3,2},{4,3},{5,4},{6,5},{7,6},{8,7},{9,8},{10,9},{11,1... | collective-permute-start | bytes 6152 | tf_op jit(solution)/shard_map/ppermute | solution.py:22
  85.7 7.3 %collective-permute-start.15 = (f32[1,8,64]{2,1,0:T(8,128)S(1)}, f32[1,8,64]{2,1,0:T(8,128)S(1)}, u32[]{:S(2)}, u32[]{:S(2)}) collective-permute-start(f32[1,8,64]{2,1,0:T(8,128)S(1)} %bitcast.193), channel_id=1, source_target_pairs={{0,1},{1,2},{2,3},{3,4},{4,5},{5,6},{6,7},{7,8},{8,9},{9,10},{10,1... | collective-permute-start | bytes 6152 | tf_op jit(solution)/shard_map/ppermute | solution.py:19
  94.2 3.6 %collective-permute-start.16 = (f32[1,8,64]{2,1,0:T(8,128)S(1)}, f32[1,8,64]{2,1,0:T(8,128)S(1)}, u32[]{:S(2)}, u32[]{:S(2)}) collective-permute-start(f32[1,8,64]{2,1,0:T(8,128)S(1)} %bitcast.176), channel_id=1, source_target_pairs={{1,0},{2,1},{3,2},{4,3},{5,4},{6,5},{7,6},{8,7},{9,8},{10,9},{11,1... | collective-permute-start | bytes 6152 | tf_op jit(solution)/shard_map/ppermute | solution.py:22
  94.6 7.3 %collective-permute-start.17 = (f32[1,8,64]{2,1,0:T(8,128)S(1)}, f32[1,8,64]{2,1,0:T(8,128)S(1)}, u32[]{:S(2)}, u32[]{:S(2)}) collective-permute-start(f32[1,8,64]{2,1,0:T(8,128)S(1)} %bitcast.187), channel_id=1, source_target_pairs={{0,1},{1,2},{2,3},{3,4},{4,5},{5,6},{6,7},{7,8},{8,9},{9,10},{10,1... | collective-permute-start | bytes 6152 | tf_op jit(solution)/shard_map/ppermute | solution.py:19
  103.0 3.6 %collective-permute-start.18 = (f32[1,8,64]{2,1,0:T(8,128)S(1)}, f32[1,8,64]{2,1,0:T(8,128)S(1)}, u32[]{:S(2)}, u32[]{:S(2)}) collective-permute-start(f32[1,8,64]{2,1,0:T(8,128)S(1)} %bitcast.183), channel_id=1, source_target_pairs={{1,0},{2,1},{3,2},{4,3},{5,4},{6,5},{7,6},{8,7},{9,8},{10,9},{11,1... | collective-permute-start | bytes 6152 | tf_op jit(solution)/shard_map/ppermute | solution.py:22
  103.4 7.3 %collective-permute-start.19 = (f32[1,8,64]{2,1,0:T(8,128)S(1)}, f32[1,8,64]{2,1,0:T(8,128)S(1)}, u32[]{:S(2)}, u32[]{:S(2)}) collective-permute-start(f32[1,8,64]{2,1,0:T(8,128)S(1)} %bitcast.194), channel_id=1, source_target_pairs={{0,1},{1,2},{2,3},{3,4},{4,5},{5,6},{6,7},{7,8},{8,9},{9,10},{10,1... | collective-permute-start | bytes 6152 | tf_op jit(solution)/shard_map/ppermute | solution.py:19
  111.8 3.6 %collective-permute-start.20 = (f32[1,8,64]{2,1,0:T(8,128)S(1)}, f32[1,8,64]{2,1,0:T(8,128)S(1)}, u32[]{:S(2)}, u32[]{:S(2)}) collective-permute-start(f32[1,8,64]{2,1,0:T(8,128)S(1)} %bitcast.177), channel_id=1, source_target_pairs={{1,0},{2,1},{3,2},{4,3},{5,4},{6,5},{7,6},{8,7},{9,8},{10,9},{11,1... | collective-permute-start | bytes 6152 | tf_op jit(solution)/shard_map/ppermute | solution.py:22
  112.3 7.3 %collective-permute-start.21 = (f32[1,8,64]{2,1,0:T(8,128)S(1)}, f32[1,8,64]{2,1,0:T(8,128)S(1)}, u32[]{:S(2)}, u32[]{:S(2)}) collective-permute-start(f32[1,8,64]{2,1,0:T(8,128)S(1)} %bitcast.188), channel_id=1, source_target_pairs={{0,1},{1,2},{2,3},{3,4},{4,5},{5,6},{6,7},{7,8},{8,9},{9,10},{10,1... | collective-permute-start | bytes 6152 | tf_op jit(solution)/shard_map/ppermute | solution.py:19
  120.7 3.6 %collective-permute-start.22 = (f32[1,8,64]{2,1,0:T(8,128)S(1)}, f32[1,8,64]{2,1,0:T(8,128)S(1)}, u32[]{:S(2)}, u32[]{:S(2)}) collective-permute-start(f32[1,8,64]{2,1,0:T(8,128)S(1)} %bitcast.178), channel_id=1, source_target_pairs={{1,0},{2,1},{3,2},{4,3},{5,4},{6,5},{7,6},{8,7},{9,8},{10,9},{11,1... | collective-permute-start | bytes 6152 | tf_op jit(solution)/shard_map/ppermute | solution.py:22
  121.1 7.3 %collective-permute-start.23 = (f32[1,8,64]{2,1,0:T(8,128)S(1)}, f32[1,8,64]{2,1,0:T(8,128)S(1)}, u32[]{:S(2)}, u32[]{:S(2)}) collective-permute-start(f32[1,8,64]{2,1,0:T(8,128)S(1)} %bitcast.189), channel_id=1, source_target_pairs={{0,1},{1,2},{2,3},{3,4},{4,5},{5,6},{6,7},{7,8},{8,9},{9,10},{10,1... | collective-permute-start | bytes 6152 | tf_op jit(solution)/shard_map/ppermute | solution.py:19
  128.8 1.0 copy-start.3
  128.8 1.1 copy-start.4
  130.0 1.8 %collective-permute-start.24 = (f32[1,3,8,4096]{3,2,1,0:T(8,128)S(1)}, f32[1,3,8,4096]{3,2,1,0:T(8,128)S(1)}, u32[]{:S(2)}, u32[]{:S(2)}) collective-permute-start(f32[1,3,8,4096]{3,2,1,0:T(8,128)S(1)} %fusion.2), channel_id=1, source_target_pairs={{0,16},{16,0},{1,17},{17,1},{2,18},{18,2},{3,19},{19,3},{4,20},{20... | collective-permute-start | bytes 1179656 | tf_op jit(solution)/shard_map/while/body/eval_jaxpr/ppermute | solution.py:29
  131.8 1.8 %collective-permute-start.25 = (f32[1,3,8,4096]{3,2,1,0:T(8,128)S(1)}, f32[1,3,8,4096]{3,2,1,0:T(8,128)S(1)}, u32[]{:S(2)}, u32[]{:S(2)}) collective-permute-start(f32[1,3,8,4096]{3,2,1,0:T(8,128)S(1)} %fusion.3), channel_id=1, source_target_pairs={{0,16},{16,0},{1,17},{17,1},{2,18},{18,2},{3,19},{19,3},{4,20},{20... | collective-permute-start | bytes 1179656 | tf_op jit(solution)/shard_map/ppermute | solution.py:29
where the time goes:
time: 135 us; the launch traced here: 134 us
  waiting for transfers between devices  61.2 us (45%)
  starting transfers between devices  30.4 us (23%)
  local copies, waits for them, and re-layouts  25.2 us (19%)
  matrix products  8.83 us (7%)
  other arithmetic  6.27 us (5%)
  between operations  2.34 us (2%)
    ppermute x12, waiting for transfers between devices, padded(): lax.ppermute(lax.slice_in_dim(block, block.shape[dim] - width, None, axis...  44.7 us
    ppermute x12, starting transfers between devices, padded(): lax.ppermute(lax.slice_in_dim(block, block.shape[dim] - width, None, axis...  21.7 us
    ppermute x12, waiting for transfers between devices, padded(): lax.ppermute(lax.slice_in_dim(block, 0, width, axis=dim), axis, backward)  13.2 us
    dot_general x48, matrix products, take_edges(): jnp.dot(select, edges, precision=lax.Precision.HIGHEST, preferred_element...  8.83 us
    ppermute x12, starting transfers between devices, padded(): lax.ppermute(lax.slice_in_dim(block, 0, width, axis=dim), axis, backward)  8.37 us
    dynamic_slice x8, local copies, waits for them, and re-layouts, body(): depth = lax.map(depth_row, depth_level)  7.41 us
    slice x24, local copies, waits for them, and re-layouts, edge_pair(): return jnp.stack([field[:, 0::BS], field[:, BS - 1::BS]])  3.33 us
    ppermute x2, waiting for transfers between devices, passed_along(): lax.ppermute(shard, axis, [(i, (i + by) % size) for i in range(size)])  3.3 us
  transfers between devices with their start and end apart: 26, of which 25 were waited for; matrix products, arithmetic and copies ran while one was open for 7% of the time, Pallas kernels for 0%

commit v1 on v0

v1 whole, which is shorter than its diff:
```python
import functools
import math

import jax
import jax.numpy as jnp
from jax import lax
from jax.experimental import pallas as pl
from jax.experimental.pallas import tpu as pltpu
from jax.sharding import PartitionSpec as P

BS = 64
STEPS = 6
HALF = 2 * STEPS
SENT = STEPS // 2
OUT = STEPS
LANES = 128
USED = 8 * OUT
F32 = jnp.float32
VMEM_LIMIT = 24 * 1024 * 1024


def roll(x, by):
    by = by % LANES
    return x if by == 0 else pltpu.roll(x, by, 1)


def take(x, index):
    return jnp.take_along_axis(x, index, axis=0)


def lane_ids():
    lane = lax.broadcasted_iota(jnp.int32, (8, LANES), 1)
    return lane, lane % BS


def spread(column):
    return jnp.broadcast_to(column, (8, LANES))


def ghost_index(entry):
    return jnp.maximum(entry, 0), (entry >= 0).astype(F32)


class Field:
    def __init__(self, ref, lead=()):
        self.ref, self.lead = ref, tuple(lead)

    def __getitem__(self, v):
        return self.ref[self.lead + (slice(None), pl.ds(v * LANES, LANES))]

    def __setitem__(self, v, value):
        self.ref[self.lead + (slice(None), pl.ds(v * LANES, LANES))] = value


def phase(count, step):
    omega = 2.0 * math.pi / (count * STEPS)
    here = lax.axis_index("tm")
    ca, sa = F32(0), F32(0)
    for n in range(count):
        for j in range(STEPS):
            hit = jnp.logical_and(here == n, step == j)
            angle = (n * STEPS + j) * omega
            ca = jnp.where(hit, F32(0.3 * math.cos(angle)), ca)
            sa = jnp.where(hit, F32(0.3 * math.sin(angle)), sa)
    return ca, sa


def along(tile, count, lower, north, south):
    first, last = roll(tile(0), BS), roll(tile(count - 1), BS)
    (north_at, north_on), (south_at, south_on) = north, south
    before, here = take(last, south_at) * south_on, first
    for v in range(count):
        if v == count - 1:
            after = take(first, north_at) * north_on
        elif v == count - 2:
            after = last
        else:
            after = roll(tile(v + 1), BS)
        yield jnp.where(lower, here, after) - jnp.where(lower, before, here)
        before, here = here, after


def across_open(x):
    return roll(x, -1) - roll(x, 1)


def level_half(s, count, ca, sa, update, lower, north, south, across):
    depth, level, east, northv = s["depth"], s["level"], s["east"], s["north"]
    slope = along(lambda v: depth[v] * northv[v], count, lower, north, south)
    for v, dy in enumerate(slope):
        div = across(depth[v] * east[v]) + dy
        old = level[v]
        new = (old + (s["tide0"][v] * ca + s["tide1"][v] * sa) - div) * s["live"][v]
        level[v] = jnp.where(update, new, old)


def velocity_half(s, count, update, lower, north, south, across):
    level = s["level"]
    slope = along(lambda v: level[v], count, lower, north, south)
    for v, dy in enumerate(slope):
        dx = across(level[v])
        u, w = s["east"][v], s["north"][v]
        cor, live = s["cor"](v), s["live"][v]
        new_u = (F32(0.985) * u + cor * w - F32(0.15) * dx) * live
        new_w = (F32(0.985) * w - cor * u - F32(0.15) * dy) * live
        s["east"][v] = jnp.where(update, new_u, u)
        s["north"][v] = jnp.where(update, new_w, w)


def own_ghosts(nb_ref):
    nb = nb_ref[...]
    return ghost_index(spread(nb[:, 0:1])), ghost_index(spread(nb[:, 1:2]))


def interior_steps(s, count, slices, steps, nb_ref):
    lane, cell = lane_ids()
    lower = lane < BS
    edge = jnp.minimum(cell, BS - 1 - cell) + 1
    north, south = own_ghosts(nb_ref)
    for step in steps:
        ca, sa = phase(slices, step)
        level_half(s, count, ca, sa, edge > 2 * step + 1, lower, north, south, across_open)
        velocity_half(s, count, edge > 2 * step + 2, lower, north, south, across_open)


def window(cell, f):
    return jnp.logical_and(cell >= OUT * f, cell < OUT * f + OUT)


def before_kernel(
    slices, start, level_id, table, wet, count_ref, nb_ref, cor, tide,
    state, depth_out, live_out, pe, pw,
):
    tiles = wet.shape[1] // LANES
    lane, cell = lane_ids()
    slot = lax.broadcasted_iota(jnp.int32, (8, LANES), 0)
    held = (slot < count_ref[0]).astype(F32)
    row = F32(0.15) * table[...].reshape(1, table.shape[0])
    row = jnp.broadcast_to(jnp.concatenate([row] * (LANES // row.shape[1]), axis=1), (8, LANES))
    depth, live = Field(depth_out), Field(live_out)
    fields = [Field(state, (i,)) for i in range(3)]
    ids, land = Field(level_id), Field(wet)
    for v in range(tiles):
        depth[v] = jnp.take_along_axis(row, ids[v], axis=1)
        live[v] = land[v].astype(F32) * held
        for i in range(3):
            fields[i][v] = Field(start, (0, i))[v] * live[v]
    cor_f = Field(cor)
    s = dict(
        depth=depth, live=live, level=fields[0], east=fields[1], north=fields[2],
        tide0=Field(tide, (0,)), tide1=Field(tide, (1,)), cor=lambda v: F32(0.3) * cor_f[v],
    )
    interior_steps(s, tiles, slices, range(SENT), nb_ref)

    nb = nb_ref[...].astype(F32)
    masks = [window(cell, f) for f in range(8)]

    def packed(v, going_east):
        items = [
            s["level"][v], s["east"][v], s["north"][v], depth[v], live[v],
            s["cor"](v), s["tide0"][v], s["tide1"][v],
        ]
        if going_east:
            shift, spare, far = -(BS - OUT), 0, -(BS - OUT - 1)
        else:
            shift, spare, far = BS, OUT - 1, BS - 1
        out = jnp.zeros((8, LANES), F32)
        for f, item in enumerate(items):
            out = jnp.where(masks[f], roll(item, OUT * f + shift), out)
        out = jnp.where(cell == 6 * OUT + spare, roll(items[0], 6 * OUT + far), out)
        if v < 2:
            at = 7 * OUT + spare + (0 if going_east else BS)
            for h in range(2):
                put = lane == (at + BS * h) % LANES
                out = jnp.where(put, spread(nb[:, 2 * v + h : 2 * v + h + 1]), out)
        return out

    full = tiles * 3 // 4
    for ref, going_east in ((pe, True), (pw, False)):
        for i in range(tiles - full):
            extra = packed(full + i, going_east)
            for q in range(3):
                own = packed(3 * i + q, going_east)
                ref[3 * i + q] = jnp.where(cell < USED, own, roll(extra, USED - 16 * q))


def strip_of(tile, cell):
    return jnp.where(cell < BS // 2, roll(tile, OUT), roll(tile, -OUT))


def during_kernel(slices, state, depth_in, live_in, nb_ref, cor, tide, last, strips):
    tiles = depth_in.shape[1] // LANES
    lane, cell = lane_ids()
    fields = [Field(last, (i,)) for i in range(3)]
    for v in range(tiles):
        for i in range(3):
            fields[i][v] = Field(state, (i,))[v]
    cor_f = Field(cor)
    s = dict(
        depth=Field(depth_in), live=Field(live_in), level=fields[0], east=fields[1],
        north=fields[2], tide0=Field(tide, (0,)), tide1=Field(tide, (1,)),
        cor=lambda v: F32(0.3) * cor_f[v],
    )
    interior_steps(s, tiles, slices, range(SENT, STEPS), nb_ref)
    for v in range(tiles):
        items = [
            s["level"][v], s["east"][v], s["north"][v], s["depth"][v], s["live"][v],
            s["cor"](v), s["tide0"][v], s["tide1"][v],
        ]
        for f, item in enumerate(items):
            Field(strips, (f,))[v] = strip_of(item, cell)


def after_kernel(slices, pe, pw, strips, nb_ref, last, start, live_in, gain, defect, work):
    tiles = live_in.shape[1] // LANES
    lane, cell = lane_ids()
    lower = lane < BS
    full = tiles * 3 // 4
    odd = (cell // OUT) % 2 == 1
    even = jnp.logical_and(jnp.logical_not(odd), cell < USED)
    odd = jnp.logical_and(odd, cell < USED)
    outer = jnp.logical_or(cell < OUT, cell >= BS - OUT)

    def opened(ref, v):
        if v < full:
            return ref[v]
        out = None
        for q in range(3):
            part = roll(ref[3 * (v - full) + q], 16 * q - USED)
            out = part if out is None else jnp.where(cell >= 16 * q, part, out)
        return out

    for v in range(tiles):
        west, east = opened(pe, v), roll(opened(pw, v), -OUT)
        pair = (jnp.where(even, west, east), jnp.where(odd, west, east))
        for f in range(8):
            Field(work, (f,))[v] = jnp.where(outer, roll(pair[f % 2], -OUT * f), Field(strips, (f,))[v])

    names = ("level", "east", "north", "depth", "live", "cor", "tide0", "tide1")
    s = {name: Field(work, (f,)) for f, name in enumerate(names)}
    cor_f = s["cor"]
    s["cor"] = lambda v: cor_f[v]

    nb = nb_ref[...]
    t1 = s["tide1"]
    sent = [t1[0], t1[1]]

    def entry(j):
        tile, base = sent[j // 2], BS * (j % 2)
        west = spread(tile[:, base : base + 1]).astype(jnp.int32)
        east = spread(tile[:, base + BS - 1 : base + BS]).astype(jnp.int32)
        return west, spread(nb[:, j : j + 1]), east

    west_side, east_side = cell < OUT, cell >= BS - OUT

    def row_ghost(j):
        west, own, east = entry(j)
        return ghost_index(jnp.where(west_side, west, jnp.where(east_side, east, own)))

    north, south = row_ghost(0), row_ghost(1)
    slot = lax.broadcasted_iota(jnp.int32, (8, LANES), 0)
    west_e, own_e, _ = entry(2)
    _, own_w, east_w = entry(3)
    join_e = jnp.where(cell == OUT - 1, west_e, jnp.where(cell == BS - OUT - 1, own_e, slot))
    join_w = jnp.where(cell == OUT, own_w, jnp.where(cell == BS - OUT, east_w, slot))
    (to_e, on_e), (to_w, on_w) = ghost_index(join_e), ghost_index(join_w)

    def across(x):
        return take(roll(x, -1), to_e) * on_e - take(roll(x, 1), to_w) * on_w

    depth_of = jnp.minimum(cell, BS - 1 - cell)

    def update(k):
        low = OUT - jnp.minimum(k, HALF - k)
        return jnp.logical_and(depth_of >= low, depth_of <= k + OUT - 1)

    far = s["tide0"]
    far_w, far_e = cell == 0, cell == BS - 1

    def step_of(step, carry):
        ca, sa = phase(slices, step)
        level_half(s, tiles, ca, sa, update(2 * step + 1), lower, north, south, across)
        level = s["level"]
        slope = along(lambda v: level[v], tiles, lower, north, south)
        now = update(2 * step + 2)
        for v, dy in enumerate(slope):
            x, beyond = level[v], far[v]
            e = jnp.where(far_e, beyond, roll(x, -1))
            w = jnp.where(far_w, beyond, roll(x, 1))
            dx = take(e, to_e) * on_e - take(w, to_w) * on_w
            u, n = s["east"][v], s["north"][v]
            cor, live = s["cor"](v), s["live"][v]
            new_u = (F32(0.985) * u + cor * n - F32(0.15) * dx) * live
            new_n = (F32(0.985) * n - cor * u - F32(0.15) * dy) * live
            s["east"][v] = jnp.where(now, new_u, u)
            s["north"][v] = jnp.where(now, new_n, n)
        return carry

    lax.fori_loop(0, STEPS, step_of, 0)

    head, tail = cell < HALF, cell >= BS - HALF
    for v in range(tiles):
        live = Field(live_in)[v]
        for i in range(3):
            x = Field(work, (i,))[v]
            fine = jnp.where(head, roll(x, -OUT), jnp.where(tail, roll(x, OUT), Field(last, (i,))[v]))
            Field(defect, (i,))[v] = fine - Field(gain, (i,))[v] * (Field(start, (0, i))[v] * live)


def call(kernel, out_shape, operands, smem=(), scratch=(), flops=0):
    vmem = pl.BlockSpec(memory_space=pltpu.VMEM)
    size = sum(4 * x.size for x in operands)
    return pl.pallas_call(
        kernel,
        out_shape=out_shape,
        in_specs=[
            pl.BlockSpec(memory_space=pltpu.SMEM) if i in smem else vmem
            for i in range(len(operands))
        ],
        out_specs=jax.tree.map(lambda _: vmem, out_shape),
        scratch_shapes=scratch,
        cost_estimate=pl.CostEstimate(flops=flops, bytes_accessed=2 * size, transcendentals=0),
        compiler_params=pltpu.CompilerParams(vmem_limit_bytes=VMEM_LIMIT),
    )(*operands)


def shape(*dims):
    return jax.ShapeDtypeStruct(dims, F32)


def passed_along(shard, axis, by):
    size = lax.axis_size(axis)
    return lax.ppermute(shard, axis, [(i, (i + by) % size) for i in range(size)])


def body(
    start_states, coarse_gain, depth_level, depth_table, wet, block_count, neighbour, coriolis, tide
):
    slots, cells = wet.shape
    tiles = cells // LANES
    slices = lax.axis_size("tm")
    state, depth, live, pe, pw = call(
        functools.partial(before_kernel, slices),
        [shape(3, slots, cells), shape(slots, cells), shape(slots, cells)]
        + [shape(tiles * 3 // 4, slots, LANES)] * 2,
        [start_states, depth_level, depth_table, wet, block_count, neighbour, coriolis, tide],
        smem=(4,),
    )
    from_west = passed_along(pe, "space", 1)
    from_east = passed_along(pw, "space", -1)
    last, strips = call(
        functools.partial(during_kernel, slices),
        [shape(3, slots, cells), shape(8, slots, cells)],
        [state, depth, live, neighbour, coriolis, tide],
    )
    defect = call(
        functools.partial(after_kernel, slices),
        shape(3, slots, cells),
        [from_west, from_east, strips, neighbour, last, start_states, live, coarse_gain],
        scratch=[pltpu.VMEM((8, slots, cells), F32)],
    )
    total, power = passed_along(defect, "tm", 1), coarse_gain
    for _ in range(slices - 2):
        total = passed_along(defect + coarse_gain * total, "tm", 1)
        power = power * coarse_gain
    total = total + power * defect
    return (total / (1.0 - power * coarse_gain))[None]


def solution(mesh):
    return jax.shard_map(
        body,
        mesh=mesh,
        in_specs=(
            P("tm", None, "space", None),
            P(None, "space", None),
            P("space", None),
            P(),
            P("space", None),
            P("space"),
            P("space", None),
            P("space", None),
            P(None, "space", None),
        ),
        out_specs=P("tm", None, "space", None),
        check_vma=False,
    )
```

time: 135 us -> 25.9 us (0.19)
  waiting for transfers between devices: 61.2 us -> 2.95 us
  starting transfers between devices: 30.4 us -> 7.12 us
  local copies, waits for them, and re-layouts: 25.2 us -> 5.44 us
  matrix products: 8.83 us -> 0 us
  Pallas kernels: 0 us -> 8.55 us
  other arithmetic: 6.27 us -> 0.84 us
  between operations: 2.34 us -> 0.7 us
    ppermute x24 -> x0, waiting for transfers between devices: 57.9 us -> none  [the longest x12 44.7 us: padded(): lax.ppermute(lax.slice_in_dim(block, block.shape[dim] - width, None, axis...]
    ppermute x24 -> x0, starting transfers between devices: 30.1 us -> none  [the longest x12 21.7 us: padded(): lax.ppermute(lax.slice_in_dim(block, block.shape[dim] - width, None, axis...]
    dot_general x48 -> x0, matrix products: 8.83 us -> none  [take_edges(): jnp.dot(select, edges, precision=lax.Precision.HIGHEST, preferred_element...]
    pallas_call x0 -> x3, Pallas kernels: none -> 8.55 us  [call(): pl.pallas_call(kernel, out_shape=out_shape, in_specs=[pl.BlockSpec(memory...]
    dynamic_slice x8 -> x0, local copies, waits for them, and re-layouts: 7.41 us -> none  [body(): depth = lax.map(depth_row, depth_level)]
    ppermute x2 -> x3, starting transfers between devices: 0.27 us -> 7.12 us  [passed_along(): lax.ppermute(shard, axis, [(i, (i + by) % size) for i in range(size)])]
    slice x48 -> x0, local copies, waits for them, and re-layouts: 5.6 us -> none  [the longest x24 3.33 us: edge_pair(): return jnp.stack([field[:, 0::BS], field[:, BS - 1::BS]])]
    broadcast_in_dim x24 -> x0, local copies, waits for them, and re-layouts: 3.2 us -> none  [the longest x12 1.6 us: across(): jnp.repeat(west_ghost, BS, axis=-1)]
  transfers between devices with their start and end apart: 26 -> 3, of which waited for: 25 -> 2; matrix products, arithmetic and copies ran while one was open for 7% -> 0% of each run, Pallas kernels for 0% -> 6%
where the time goes in v1:
time: 25.9 us; the launch traced here: 25.6 us
  Pallas kernels  8.55 us (33%)
  starting transfers between devices  7.12 us (27%)
  local copies, waits for them, and re-layouts  5.44 us (21%)
  waiting for transfers between devices  2.95 us (11%)
  other arithmetic  0.84 us (3%)
  between operations  0.7 us (3%)
    pallas_call x3, Pallas kernels, call(): pl.pallas_call(kernel, out_shape=out_shape, in_specs=[pl.BlockSpec(memory...  8.55 us
    ppermute x3, starting transfers between devices, passed_along(): lax.ppermute(shard, axis, [(i, (i + by) % size) for i in range(size)])  7.12 us
    unnamed x21, local copies, waits for them, and re-layouts  5.44 us
    ppermute x3, waiting for transfers between devices, passed_along(): lax.ppermute(shard, axis, [(i, (i + by) % size) for i in range(size)])  2.95 us
    broadcast_in_dim x1, other arithmetic, body(): return (total / (1.0 - power * coarse_gain))[None]  0.84 us
  transfers between devices with their start and end apart: 3, of which 2 were waited for; matrix products, arithmetic and copies ran while one was open for 0% of the time, Pallas kernels for 6%

profile of v1, /device:TPU:0, one launch (start us, length us, event | category | flops | bytes accessed | tf_op | source)
XLA Modules:
  0.0 25.6 jit_solution(1341470588115140055)
XLA Ops:
  0.7 0.0 copy-start.9
  0.7 0.8 %copy.10.nb_ref = s32[8,4]{1,0:T(8,128)S(1)} copy(s32[8,4]{0,1:T(4,128)} %param.15) | data formatting | bytes 256 | tf_op args[6]
  1.4 0.0 copy-done.9
  1.4 0.0 copy-start
  1.4 1.0 %copy-done = f32[1,3,8,4096]{3,2,1,0:T(8,128)S(1)} copy-done((f32[1,3,8,4096]{3,2,1,0:T(8,128)S(1)}, f32[1,3,8,4096]{3,2,1,0:T(8,128)}, u32[]{:S(2)}) %copy-start) | copy-done | bytes 393240
  2.4 0.0 copy-start.3
  2.4 0.9 %copy-done.3 = f32[2,8,4096]{2,1,0:T(8,128)S(1)} copy-done((f32[2,8,4096]{2,1,0:T(8,128)S(1)}, f32[2,8,4096]{2,1,0:T(8,128)}, u32[]{:S(2)}) %copy-start.3) | copy-done | bytes 262168
  3.4 0.0 copy-start.5
  3.4 0.9 %copy-done.5 = f32[8,4096]{1,0:T(8,128)S(1)} copy-done((f32[8,4096]{1,0:T(8,128)S(1)}, f32[8,4096]{1,0:T(8,128)}, u32[]{:S(2)}) %copy-start.5) | copy-done | bytes 131096
  4.3 0.0 copy-start.7
  4.3 0.9 %copy-done.7 = s32[8,4096]{1,0:T(8,128)S(1)} copy-done((s32[8,4096]{1,0:T(8,128)S(1)}, s32[8,4096]{1,0:T(8,128)}, u32[]{:S(2)}) %copy-start.7) | copy-done | bytes 131096
  5.2 0.0 copy-start.8
  5.2 0.9 %copy-done.8 = s32[8,4096]{1,0:T(8,128)S(1)} copy-done((s32[8,4096]{1,0:T(8,128)S(1)}, s32[8,4096]{1,0:T(8,128)}, u32[]{:S(2)}) %copy-start.8) | copy-done | bytes 131096
  6.1 0.0 copy-start.4
  6.1 0.0 copy-start.6
  6.1 2.6 %shard_map.91 = (f32[3,8,4096]{2,1,0:T(8,128)S(1)}, f32[8,4096]{1,0:T(8,128)S(1)}, f32[8,4096]{1,0:T(8,128)S(1)}, f32[24,8,128]{2,1,0:T(8,128)S(1)}, f32[24,8,128]{2,1,0:T(8,128)S(1)}) custom-call(f32[1,3,8,4096]{3,2,1,0:T(8,128)S(1)} %copy-done, s32[8,4096]{1,0:T(8,128)S(1)} %copy-done.7, f32[64]{0:T(128)S(1)} %copy-done.9, s32[8,4096]{1,0:T(8,128)S(1)} %copy-done.8, ...), custom_call_target="tpu_custom_call" | custom-call | bytes 2097928 | tf_op jit(solution)/shard_map/pallas_call | solution.py:313
  8.7 3.0 %collective-permute-start = (f32[24,8,128]{2,1,0:T(8,128)S(1)}, f32[24,8,128]{2,1,0:T(8,128)S(1)}, u32[]{:S(2)}, u32[]{:S(2)}) collective-permute-start(f32[24,8,128]{2,1,0:T(8,128)S(1)} %get-tuple-element.12), channel_id=1, source_target_pairs={{0,1},{1,2},{2,3},{3,4},{4,5},{5,6},{6,7},{7,8},{8,9},{9,10},{10,1... | collective-permute-start | bytes 294920 | tf_op jit(solution)/shard_map/ppermute | solution.py:333
  11.7 4.1 %collective-permute-start.1 = (f32[24,8,128]{2,1,0:T(8,128)S(1)}, f32[24,8,128]{2,1,0:T(8,128)S(1)}, u32[]{:S(2)}, u32[]{:S(2)}) collective-permute-start(f32[24,8,128]{2,1,0:T(8,128)S(1)} %get-tuple-element.13), channel_id=1, source_target_pairs={{0,15},{1,0},{2,1},{3,2},{4,3},{5,4},{6,5},{7,6},{8,7},{9,8},{10,9... | collective-permute-start | bytes 294920 | tf_op jit(solution)/shard_map/ppermute | solution.py:333
  15.7 0.0 copy-done.4
  15.7 0.0 copy-done.6
  15.7 0.0 copy-start.1
  15.7 0.0 copy-start.2
  15.8 1.6 %shard_map.92 = (f32[3,8,4096]{2,1,0:T(8,128)S(1)}, f32[8,8,4096]{2,1,0:T(8,128)S(1)}) custom-call(f32[3,8,4096]{2,1,0:T(8,128)S(1)} %get-tuple-element.14.state, f32[8,4096]{1,0:T(8,128)S(1)} %get-tuple-element.15.depth_in, f32[8,4096]{1,0:T(8,128)S(1)} %get-tuple-element.16.live_in, s32[8,4]{1,0:T(8,128)S(1)} %copy.10.nb_ref, f32[8,4096]{1,0:T(8,128)S(1)} %copy-done.6, ...), custom_call_target="tpu_custom_call" | custom-call | bytes 2097408 | tf_op jit(solution)/shard_map/pallas_call | solution.py:313
  17.3 1.2 %collective-permute-done.pe = f32[24,8,128]{2,1,0:T(8,128)S(1)} collective-permute-done((f32[24,8,128]{2,1,0:T(8,128)S(1)}, f32[24,8,128]{2,1,0:T(8,128)S(1)}, u32[]{:S(2)}, u32[]{:S(2)}) %collective-permute-start) | collective-permute-done | bytes 98336 | tf_op jit(solution)/shard_map/ppermute | solution.py:333
  18.6 0.0 collective-permute-done.1.pw
  18.6 0.0 copy-done.1
  18.6 0.0 copy-done.2
  18.6 4.4 %shard_map.93 = f32[3,8,4096]{2,1,0:T(8,128)S(1)} custom-call(f32[24,8,128]{2,1,0:T(8,128)S(1)} %collective-permute-done.pe, f32[24,8,128]{2,1,0:T(8,128)S(1)} %collective-permute-done.1.pw, f32[8,8,4096]{2,1,0:T(8,128)S(1)} %get-tuple-element.17.strips, s32[8,4]{1,0:T(8,128)S(1)} %copy.10.nb_ref, f32[3,8,4096]{2,1,0:T(8,128)S(1)} %get-tuple-element.18.last, ...), custom_call_target="tpu_custom_call" | custom-call | bytes 5112064 | tf_op jit(solution)/shard_map/pallas_call | solution.py:313
  23.0 0.1 collective-permute-start.2
  23.0 1.7 %collective-permute-done.2 = f32[3,8,4096]{2,1,0:T(8,128)S(1)} collective-permute-done((f32[3,8,4096]{2,1,0:T(8,128)S(1)}, f32[3,8,4096]{2,1,0:T(8,128)S(1)}, u32[]{:S(2)}, u32[]{:S(2)}) %collective-permute-start.2) | collective-permute-done | bytes 393248 | tf_op jit(solution)/shard_map/ppermute | solution.py:333
  24.8 0.8 %divide_bitcast_fusion = f32[1,3,8,4096]{3,2,1,0:T(8,128)} fusion(f32[3,8,4096]{2,1,0:T(8,128)S(1)} %copy-done.2, f32[3,8,4096]{2,1,0:T(8,128)S(1)} %collective-permute-done.2, f32[3,8,4096]{2,1,0:T(8,128)S(1)} %shard_map.93), kind=kLoop, calls=%fused_computation | loop fusion | flops 491520 | bytes 1572864 | tf_op jit(solution)/shard_map/broadcast_in_dim | solution.py:367
Async XLA Ops:
  0.7 0.8 %copy-start.9 = (f32[64]{0:T(128)S(1)}, f32[64]{0:T(128)}, u32[]{:S(2)}) copy-start(f32[64]{0:T(128)} %table.1) | copy-start | bytes 772
  1.4 1.0 %copy-start = (f32[1,3,8,4096]{3,2,1,0:T(8,128)S(1)}, f32[1,3,8,4096]{3,2,1,0:T(8,128)}, u32[]{:S(2)}) copy-start(f32[1,3,8,4096]{3,2,1,0:T(8,128)} %start.3) | copy-start | bytes 1179652
  2.4 0.9 %copy-start.3 = (f32[2,8,4096]{2,1,0:T(8,128)S(1)}, f32[2,8,4096]{2,1,0:T(8,128)}, u32[]{:S(2)}) copy-start(f32[2,8,4096]{2,1,0:T(8,128)} %tide.3) | copy-start | bytes 786436
  3.4 0.9 %copy-start.5 = (f32[8,4096]{1,0:T(8,128)S(1)}, f32[8,4096]{1,0:T(8,128)}, u32[]{:S(2)}) copy-start(f32[8,4096]{1,0:T(8,128)} %cor.3) | copy-start | bytes 393220
  4.3 0.9 %copy-start.7 = (s32[8,4096]{1,0:T(8,128)S(1)}, s32[8,4096]{1,0:T(8,128)}, u32[]{:S(2)}) copy-start(s32[8,4096]{1,0:T(8,128)} %level_id.1) | copy-start | bytes 393220
  5.2 0.9 %copy-start.8 = (s32[8,4096]{1,0:T(8,128)S(1)}, s32[8,4096]{1,0:T(8,128)}, u32[]{:S(2)}) copy-start(s32[8,4096]{1,0:T(8,128)} %wet.1) | copy-start | bytes 393220
  6.1 9.7 %copy-start.4 = (f32[2,8,4096]{2,1,0:T(8,128)S(1)}, f32[2,8,4096]{2,1,0:T(8,128)}, u32[]{:S(2)}) copy-start(f32[2,8,4096]{2,1,0:T(8,128)} %tide.3) | copy-start | bytes 786436
  6.1 9.7 %copy-start.6 = (f32[8,4096]{1,0:T(8,128)S(1)}, f32[8,4096]{1,0:T(8,128)}, u32[]{:S(2)}) copy-start(f32[8,4096]{1,0:T(8,128)} %cor.3) | copy-start | bytes 393220
  8.7 9.9 %collective-permute-start = (f32[24,8,128]{2,1,0:T(8,128)S(1)}, f32[24,8,128]{2,1,0:T(8,128)S(1)}, u32[]{:S(2)}, u32[]{:S(2)}) collective-permute-start(f32[24,8,128]{2,1,0:T(8,128)S(1)} %get-tuple-element.12), channel_id=1, source_target_pairs={{0,1},{1,2},{2,3},{3,4},{4,5},{5,6},{6,7},{7,8},{8,9},{9,10},{10,1... | collective-permute-start | bytes 294920 | tf_op jit(solution)/shard_map/ppermute | solution.py:333
  11.7 6.9 %collective-permute-start.1 = (f32[24,8,128]{2,1,0:T(8,128)S(1)}, f32[24,8,128]{2,1,0:T(8,128)S(1)}, u32[]{:S(2)}, u32[]{:S(2)}) collective-permute-start(f32[24,8,128]{2,1,0:T(8,128)S(1)} %get-tuple-element.13), channel_id=1, source_target_pairs={{0,15},{1,0},{2,1},{3,2},{4,3},{5,4},{6,5},{7,6},{8,7},{9,8},{10,9... | collective-permute-start | bytes 294920 | tf_op jit(solution)/shard_map/ppermute | solution.py:333
  15.7 2.8 %copy-start.1 = (f32[1,3,8,4096]{3,2,1,0:T(8,128)S(1)}, f32[1,3,8,4096]{3,2,1,0:T(8,128)}, u32[]{:S(2)}) copy-start(f32[1,3,8,4096]{3,2,1,0:T(8,128)} %start.3) | copy-start | bytes 1179652
  15.7 2.8 %copy-start.2 = (f32[3,8,4096]{2,1,0:T(8,128)S(1)}, f32[3,8,4096]{2,1,0:T(8,128)}, u32[]{:S(2)}) copy-start(f32[3,8,4096]{2,1,0:T(8,128)} %gain.1) | copy-start | bytes 1179652
  23.0 1.8 %collective-permute-start.2 = (f32[3,8,4096]{2,1,0:T(8,128)S(1)}, f32[3,8,4096]{2,1,0:T(8,128)S(1)}, u32[]{:S(2)}, u32[]{:S(2)}) collective-permute-start(f32[3,8,4096]{2,1,0:T(8,128)S(1)} %shard_map.93), channel_id=1, source_target_pairs={{0,16},{16,0},{1,17},{17,1},{2,18},{18,2},{3,19},{19,3},{4,20},{20... | collective-permute-start | bytes 1179656 | tf_op jit(solution)/shard_map/ppermute | solution.py:333

commit v2 on v1

--- a/solution.py
+++ b/solution.py
@@ -25,7 +25,7 @@
 
 
 def take(x, index):
-    return jnp.take_along_axis(x, index, axis=0)
+    return jnp.take_along_axis(x, index, axis=0, mode="promise_in_bounds")
 
 
 def lane_ids():
@@ -107,16 +107,15 @@
         s["north"][v] = jnp.where(update, new_w, w)
 
 
-def own_ghosts(nb_ref):
-    nb = nb_ref[...]
-    return ghost_index(spread(nb[:, 0:1])), ghost_index(spread(nb[:, 1:2]))
-
-
-def interior_steps(s, count, slices, steps, nb_ref):
+def own_ghosts(face):
+    return ghost_index(face[0]), ghost_index(face[1])
+
+
+def interior_steps(s, count, slices, steps, face):
     lane, cell = lane_ids()
     lower = lane < BS
     edge = jnp.minimum(cell, BS - 1 - cell) + 1
-    north, south = own_ghosts(nb_ref)
+    north, south = own_ghosts(face)
     for step in steps:
         ca, sa = phase(slices, step)
         level_half(s, count, ca, sa, edge > 2 * step + 1, lower, north, south, across_open)
@@ -128,31 +127,50 @@
 
 
 def before_kernel(
-    slices, start, level_id, table, wet, count_ref, nb_ref, cor, tide,
-    state, depth_out, live_out, pe, pw,
+    slices, count_ref, level_h, table_h, wet_h, nb_h, start_h, tide_h, cor_h,
+    state, depth_out, live_out, face, pe, pw,
+    level_id, table, wet, nb_ref, start, tide, cor, sems,
 ):
+    loads = [
+        pltpu.make_async_copy(src, dst, sems.at[i])
+        for i, (src, dst) in enumerate(
+            [
+                (level_h, level_id), (table_h, table), (wet_h, wet), (nb_h, nb_ref),
+                (start_h, start), (tide_h, tide), (cor_h, cor),
+            ]
+        )
+    ]
+    for load in loads:
+        load.start()
     tiles = wet.shape[1] // LANES
     lane, cell = lane_ids()
     slot = lax.broadcasted_iota(jnp.int32, (8, LANES), 0)
     held = (slot < count_ref[0]).astype(F32)
+    for load in loads[:5]:
+        load.wait()
+    for j in range(4):
+        entry = jnp.broadcast_to(nb_ref[j : j + 1, :], (8, 8))
+        here = lax.broadcasted_iota(jnp.int32, (8, 8), 0) == lax.broadcasted_iota(jnp.int32, (8, 8), 1)
+        face[j] = spread(jnp.sum(jnp.where(here, entry, 0), axis=1, keepdims=True))
     row = F32(0.15) * table[...].reshape(1, table.shape[0])
     row = jnp.broadcast_to(jnp.concatenate([row] * (LANES // row.shape[1]), axis=1), (8, LANES))
     depth, live = Field(depth_out), Field(live_out)
     fields = [Field(state, (i,)) for i in range(3)]
     ids, land = Field(level_id), Field(wet)
     for v in range(tiles):
-        depth[v] = jnp.take_along_axis(row, ids[v], axis=1)
+        depth[v] = jnp.take_along_axis(row, ids[v], axis=1, mode="promise_in_bounds")
         live[v] = land[v].astype(F32) * held
         for i in range(3):
             fields[i][v] = Field(start, (0, i))[v] * live[v]
+    for load in loads[5:]:
+        load.wait()
     cor_f = Field(cor)
     s = dict(
         depth=depth, live=live, level=fields[0], east=fields[1], north=fields[2],
         tide0=Field(tide, (0,)), tide1=Field(tide, (1,)), cor=lambda v: F32(0.3) * cor_f[v],
     )
-    interior_steps(s, tiles, slices, range(SENT), nb_ref)
-
-    nb = nb_ref[...].astype(F32)
+    interior_steps(s, tiles, slices, range(SENT), face)
+
     masks = [window(cell, f) for f in range(8)]
 
     def packed(v, going_east):
@@ -172,7 +190,7 @@
             at = 7 * OUT + spare + (0 if going_east else BS)
             for h in range(2):
                 put = lane == (at + BS * h) % LANES
-                out = jnp.where(put, spread(nb[:, 2 * v + h : 2 * v + h + 1]), out)
+                out = jnp.where(put, face[2 * v + h].astype(F32), out)
         return out
 
     full = tiles * 3 // 4
@@ -188,7 +206,7 @@
     return jnp.where(cell < BS // 2, roll(tile, OUT), roll(tile, -OUT))
 
 
-def during_kernel(slices, state, depth_in, live_in, nb_ref, cor, tide, last, strips):
+def during_kernel(slices, state, depth_in, live_in, face, cor, tide, last, strips):
     tiles = depth_in.shape[1] // LANES
     lane, cell = lane_ids()
     fields = [Field(last, (i,)) for i in range(3)]
@@ -201,7 +219,7 @@
         north=fields[2], tide0=Field(tide, (0,)), tide1=Field(tide, (1,)),
         cor=lambda v: F32(0.3) * cor_f[v],
     )
-    interior_steps(s, tiles, slices, range(SENT, STEPS), nb_ref)
+    interior_steps(s, tiles, slices, range(SENT, STEPS), face)
     for v in range(tiles):
         items = [
             s["level"][v], s["east"][v], s["north"][v], s["depth"][v], s["live"][v],
@@ -211,7 +229,7 @@
             Field(strips, (f,))[v] = strip_of(item, cell)
 
 
-def after_kernel(slices, pe, pw, strips, nb_ref, last, start, live_in, gain, defect, work):
+def after_kernel(slices, pe, pw, strips, face, last, start, live_in, gain, defect, work):
     tiles = live_in.shape[1] // LANES
     lane, cell = lane_ids()
     lower = lane < BS
@@ -241,7 +259,6 @@
     cor_f = s["cor"]
     s["cor"] = lambda v: cor_f[v]
 
-    nb = nb_ref[...]
     t1 = s["tide1"]
     sent = [t1[0], t1[1]]
 
@@ -249,7 +266,7 @@
         tile, base = sent[j // 2], BS * (j % 2)
         west = spread(tile[:, base : base + 1]).astype(jnp.int32)
         east = spread(tile[:, base + BS - 1 : base + BS]).astype(jnp.int32)
-        return west, spread(nb[:, j : j + 1]), east
+        return west, face[j], east
 
     west_side, east_side = cell < OUT, cell >= BS - OUT
 
@@ -307,16 +324,14 @@
             Field(defect, (i,))[v] = fine - Field(gain, (i,))[v] * (Field(start, (0, i))[v] * live)
 
 
-def call(kernel, out_shape, operands, smem=(), scratch=(), flops=0):
+def call(kernel, out_shape, operands, spaces=None, scratch=(), flops=0):
     vmem = pl.BlockSpec(memory_space=pltpu.VMEM)
+    spaces = spaces or [pltpu.VMEM] * len(operands)
     size = sum(4 * x.size for x in operands)
     return pl.pallas_call(
         kernel,
         out_shape=out_shape,
-        in_specs=[
-            pl.BlockSpec(memory_space=pltpu.SMEM) if i in smem else vmem
-            for i in range(len(operands))
-        ],
+        in_specs=[pl.BlockSpec(memory_space=space) for space in spaces],
         out_specs=jax.tree.map(lambda _: vmem, out_shape),
         scratch_shapes=scratch,
         cost_estimate=pl.CostEstimate(flops=flops, bytes_accessed=2 * size, transcendentals=0),
@@ -339,24 +354,28 @@
     slots, cells = wet.shape
     tiles = cells // LANES
     slices = lax.axis_size("tm")
-    state, depth, live, pe, pw = call(
+    loaded = [depth_level, depth_table, wet, neighbour.T, start_states, tide, coriolis]
+    state, depth, live, face, pe, pw = call(
         functools.partial(before_kernel, slices),
         [shape(3, slots, cells), shape(slots, cells), shape(slots, cells)]
+        + [jax.ShapeDtypeStruct((4, slots, LANES), jnp.int32)]
         + [shape(tiles * 3 // 4, slots, LANES)] * 2,
-        [start_states, depth_level, depth_table, wet, block_count, neighbour, coriolis, tide],
-        smem=(4,),
+        [block_count] + [pltpu.with_memory_space_constraint(x, pltpu.HBM) for x in loaded],
+        spaces=[pltpu.SMEM] + [pltpu.HBM] * len(loaded),
+        scratch=[pltpu.VMEM(x.shape, x.dtype) for x in loaded]
+        + [pltpu.SemaphoreType.DMA((len(loaded),))],
     )
     from_west = passed_along(pe, "space", 1)
     from_east = passed_along(pw, "space", -1)
     last, strips = call(
         functools.partial(during_kernel, slices),
         [shape(3, slots, cells), shape(8, slots, cells)],
-        [state, depth, live, neighbour, coriolis, tide],
+        [state, depth, live, face, coriolis, tide],
     )
     defect = call(
         functools.partial(after_kernel, slices),
         shape(3, slots, cells),
-        [from_west, from_east, strips, neighbour, last, start_states, live, coarse_gain],
+        [from_west, from_east, strips, face, last, start_states, live, coarse_gain],
         scratch=[pltpu.VMEM((8, slots, cells), F32)],
     )
     total, power = passed_along(defect, "tm", 1), coarse_gain

time: 25.9 us -> 21.8 us (0.84)
  local copies, waits for them, and re-layouts: 5.44 us -> 0.02 us
  Pallas kernels: 8.55 us -> 9.99 us
    unnamed x21 -> x8, local copies, waits for them, and re-layouts: 5.44 us -> 0.02 us
    pallas_call x3, Pallas kernels: 8.55 us -> 9.99 us  [call(): pl.pallas_call(kernel, out_shape=out_shape, in_specs=[pl.BlockSpec(memory...]
  transfers between devices with their start and end apart: 3 -> 3, of which waited for: 2 -> 2; matrix products, arithmetic and copies ran while one was open for 0% -> 0% of each run, Pallas kernels for 6% -> 7%
where the time goes in v2:
time: 21.8 us; the launch traced here: 21.6 us
  Pallas kernels  9.99 us (46%)
  starting transfers between devices  7.12 us (33%)
  waiting for transfers between devices  2.97 us (14%)
  other arithmetic  0.83 us (4%)
  between operations  0.71 us (3%)
    pallas_call x3, Pallas kernels, call(): pl.pallas_call(kernel, out_shape=out_shape, in_specs=[pl.BlockSpec(memory...  9.99 us
    ppermute x3, starting transfers between devices, passed_along(): lax.ppermute(shard, axis, [(i, (i + by) % size) for i in range(size)])  7.12 us
    ppermute x3, waiting for transfers between devices, passed_along(): lax.ppermute(shard, axis, [(i, (i + by) % size) for i in range(size)])  2.97 us
    broadcast_in_dim x1, other arithmetic, body(): return (total / (1.0 - power * coarse_gain))[None]  0.83 us
  transfers between devices with their start and end apart: 3, of which 2 were waited for; matrix products, arithmetic and copies ran while one was open for 0% of the time, Pallas kernels for 7%

profile of v2, /device:TPU:0, one launch (start us, length us, event | category | flops | bytes accessed | tf_op | source)
XLA Modules:
  0.0 21.6 jit_solution(4385223356830999660)
XLA Ops:
  0.7 0.0 copy-start.2
  0.7 0.0 copy-start.3
  0.7 4.1 %shard_map.91 = (f32[3,8,4096]{2,1,0:T(8,128)S(1)}, f32[8,4096]{1,0:T(8,128)S(1)}, f32[8,4096]{1,0:T(8,128)S(1)}, s32[4,8,128]{2,1,0:T(8,128)S(1)}, f32[24,8,128...) custom-call(s32[1]{0:T(128)S(6)} %copy.10.count_ref, s32[8,4096]{1,0:T(8,128)} %level_h.1, f32[64]{0:T(128)} %table_h.1, ...), custom_call_target="tpu_custom_call" | custom-call | bytes 2097928 | tf_op jit(solution)/shard_map/pallas_call | solution.py:331
  4.8 3.0 %collective-permute-start = (f32[24,8,128]{2,1,0:T(8,128)S(1)}, f32[24,8,128]{2,1,0:T(8,128)S(1)}, u32[]{:S(2)}, u32[]{:S(2)}) collective-permute-start(f32[24,8,128]{2,1,0:T(8,128)S(1)} %get-tuple-element.13), channel_id=1, source_target_pairs={{0,1},{1,2},{2,3},{3,4},{4,5},{5,6},{6,7},{7,8},{8,9},{9,10},{10,1... | collective-permute-start | bytes 294920 | tf_op jit(solution)/shard_map/ppermute | solution.py:348
  7.8 4.1 %collective-permute-start.1 = (f32[24,8,128]{2,1,0:T(8,128)S(1)}, f32[24,8,128]{2,1,0:T(8,128)S(1)}, u32[]{:S(2)}, u32[]{:S(2)}) collective-permute-start(f32[24,8,128]{2,1,0:T(8,128)S(1)} %get-tuple-element.14), channel_id=1, source_target_pairs={{0,15},{1,0},{2,1},{3,2},{4,3},{5,4},{6,5},{7,6},{8,7},{9,8},{10,9... | collective-permute-start | bytes 294920 | tf_op jit(solution)/shard_map/ppermute | solution.py:348
  11.9 0.0 copy-done.2
  11.9 0.0 copy-done.3
  11.9 0.0 copy-start
  11.9 0.0 copy-start.1
  11.9 1.6 %shard_map.92 = (f32[3,8,4096]{2,1,0:T(8,128)S(1)}, f32[8,8,4096]{2,1,0:T(8,128)S(1)}) custom-call(f32[3,8,4096]{2,1,0:T(8,128)S(1)} %get-tuple-element.15.state, f32[8,4096]{1,0:T(8,128)S(1)} %get-tuple-element.16.depth_in, f32[8,4096]{1,0:T(8,128)S(1)} %get-tuple-element.17.live_in, s32[4,8,128]{2,1,0:T(8,128)S(1)} %get-tuple-element.18.face, ...), custom_call_target="tpu_custom_call" | custom-call | bytes 2129920 | tf_op jit(solution)/shard_map/pallas_call | solution.py:331
  13.5 1.3 %collective-permute-done.pe = f32[24,8,128]{2,1,0:T(8,128)S(1)} collective-permute-done((f32[24,8,128]{2,1,0:T(8,128)S(1)}, f32[24,8,128]{2,1,0:T(8,128)S(1)}, u32[]{:S(2)}, u32[]{:S(2)}) %collective-permute-start) | collective-permute-done | bytes 98336 | tf_op jit(solution)/shard_map/ppermute | solution.py:348
  14.7 0.0 collective-permute-done.1.pw
  14.7 0.0 copy-done
  14.7 0.0 copy-done.1
  14.7 4.3 %shard_map.93 = f32[3,8,4096]{2,1,0:T(8,128)S(1)} custom-call(f32[24,8,128]{2,1,0:T(8,128)S(1)} %collective-permute-done.pe, f32[24,8,128]{2,1,0:T(8,128)S(1)} %collective-permute-done.1.pw, f32[8,8,4096]{2,1,0:T(8,128)S(1)} %get-tuple-element.19.strips, s32[4,8,128]{2,1,0:T(8,128)S(1)} %get-tuple-element.18.face, f32[3,8,4096]{2,1,0:T(8,128)S(1)} %get-tuple-element.20.last, ...), custom_call_target="tpu_custom_call" | custom-call | bytes 5144576 | tf_op jit(solution)/shard_map/pallas_call | solution.py:331
  19.0 0.1 collective-permute-start.2
  19.1 1.7 %collective-permute-done.2 = f32[3,8,4096]{2,1,0:T(8,128)S(1)} collective-permute-done((f32[3,8,4096]{2,1,0:T(8,128)S(1)}, f32[3,8,4096]{2,1,0:T(8,128)S(1)}, u32[]{:S(2)}, u32[]{:S(2)}) %collective-permute-start.2) | collective-permute-done | bytes 393248 | tf_op jit(solution)/shard_map/ppermute | solution.py:348
  20.8 0.8 %divide_bitcast_fusion = f32[1,3,8,4096]{3,2,1,0:T(8,128)} fusion(f32[3,8,4096]{2,1,0:T(8,128)S(1)} %copy-done.1, f32[3,8,4096]{2,1,0:T(8,128)S(1)} %collective-permute-done.2, f32[3,8,4096]{2,1,0:T(8,128)S(1)} %shard_map.93), kind=kLoop, calls=%fused_computation | loop fusion | flops 491520 | bytes 1572864 | tf_op jit(solution)/shard_map/broadcast_in_dim | solution.py:386
Async XLA Ops:
  0.7 11.2 %copy-start.2 = (f32[2,8,4096]{2,1,0:T(8,128)S(1)}, f32[2,8,4096]{2,1,0:T(8,128)}, u32[]{:S(2)}) copy-start(f32[2,8,4096]{2,1,0:T(8,128)} %tide.1) | copy-start | bytes 786436
  0.7 11.2 %copy-start.3 = (f32[8,4096]{1,0:T(8,128)S(1)}, f32[8,4096]{1,0:T(8,128)}, u32[]{:S(2)}) copy-start(f32[8,4096]{1,0:T(8,128)} %cor.1) | copy-start | bytes 393220
  4.8 9.9 %collective-permute-start = (f32[24,8,128]{2,1,0:T(8,128)S(1)}, f32[24,8,128]{2,1,0:T(8,128)S(1)}, u32[]{:S(2)}, u32[]{:S(2)}) collective-permute-start(f32[24,8,128]{2,1,0:T(8,128)S(1)} %get-tuple-element.13), channel_id=1, source_target_pairs={{0,1},{1,2},{2,3},{3,4},{4,5},{5,6},{6,7},{7,8},{8,9},{9,10},{10,1... | collective-permute-start | bytes 294920 | tf_op jit(solution)/shard_map/ppermute | solution.py:348
  7.8 6.9 %collective-permute-start.1 = (f32[24,8,128]{2,1,0:T(8,128)S(1)}, f32[24,8,128]{2,1,0:T(8,128)S(1)}, u32[]{:S(2)}, u32[]{:S(2)}) collective-permute-start(f32[24,8,128]{2,1,0:T(8,128)S(1)} %get-tuple-element.14), channel_id=1, source_target_pairs={{0,15},{1,0},{2,1},{3,2},{4,3},{5,4},{6,5},{7,6},{8,7},{9,8},{10,9... | collective-permute-start | bytes 294920 | tf_op jit(solution)/shard_map/ppermute | solution.py:348
  11.9 2.8 %copy-start = (f32[1,3,8,4096]{3,2,1,0:T(8,128)S(1)}, f32[1,3,8,4096]{3,2,1,0:T(8,128)}, u32[]{:S(2)}) copy-start(f32[1,3,8,4096]{3,2,1,0:T(8,128)} %start.1) | copy-start | bytes 1179652
  11.9 2.8 %copy-start.1 = (f32[3,8,4096]{2,1,0:T(8,128)S(1)}, f32[3,8,4096]{2,1,0:T(8,128)}, u32[]{:S(2)}) copy-start(f32[3,8,4096]{2,1,0:T(8,128)} %gain.1) | copy-start | bytes 1179652
  19.0 1.8 %collective-permute-start.2 = (f32[3,8,4096]{2,1,0:T(8,128)S(1)}, f32[3,8,4096]{2,1,0:T(8,128)S(1)}, u32[]{:S(2)}, u32[]{:S(2)}) collective-permute-start(f32[3,8,4096]{2,1,0:T(8,128)S(1)} %shard_map.93), channel_id=1, source_target_pairs={{0,16},{16,0},{1,17},{17,1},{2,18},{18,2},{3,19},{19,3},{4,20},{20... | collective-permute-start | bytes 1179656 | tf_op jit(solution)/shard_map/ppermute | solution.py:348

commit v3 on v0

v3 whole, which is shorter than its diff:
```python
import functools
import math

import jax
import jax.numpy as jnp
from jax import lax
from jax.experimental import pallas as pl
from jax.experimental.pallas import tpu as pltpu
from jax.sharding import PartitionSpec as P

BS = 64
STEPS = 6
HALF = 2 * STEPS
SENT = STEPS // 2
OUT = STEPS
LANES = 128
SUB = 8
ROWS = 4
GROUPS = BS // SUB
F32 = jnp.float32
VMEM_LIMIT = 24 * 1024 * 1024


def shifted(x, by):
    return pltpu.roll(x, by % SUB, 0)


def lanes_of(x, index):
    return jnp.take_along_axis(x, index, axis=1, mode="promise_in_bounds")


def tile_iota(dim):
    return lax.broadcasted_iota(jnp.int32, (SUB, LANES), dim)


def lane_tile(ref, v, lead=()):
    return ref[tuple(lead) + (slice(None), pl.ds(v * LANES, LANES))]


def to_columns(tiles):
    out = []
    for part in (tiles[0::2], tiles[1::2]):
        turned = jnp.concatenate(part, axis=0).T
        out += [turned[:BS], turned[BS:]]
    return out


def to_tiles(columns):
    out = {}
    for part in range(2):
        turned = jnp.concatenate(columns[2 * part : 2 * part + 2], axis=0).T
        for c in range(LANES // SUB):
            out[2 * c + part] = turned[SUB * c : SUB * c + SUB]
    return [out[v] for v in range(len(out))]


def phase(count, step):
    omega = 2.0 * math.pi / (count * STEPS)
    here = lax.axis_index("tm")
    ca, sa = F32(0), F32(0)
    for n in range(count):
        angle = (n * STEPS + step) * omega
        ca = jnp.where(here == n, F32(0.3 * math.cos(angle)), ca)
        sa = jnp.where(here == n, F32(0.3 * math.sin(angle)), sa)
    return ca, sa


def chunk_ghosts(north, south):
    lane = tile_iota(1)
    top, bottom = lane >= LANES - SUB, lane < SUB
    up = jnp.where(top, jnp.maximum(north, 0), (lane + SUB) % LANES)
    down = jnp.where(bottom, LANES - SUB + jnp.maximum(south, 0), (lane + LANES - SUB) % LANES)
    up_on = jnp.where(jnp.logical_and(top, north < 0), F32(0), F32(1))
    down_on = jnp.where(jnp.logical_and(bottom, south < 0), F32(0), F32(1))
    return up, up_on, down, down_on


def face_rows(nb):
    wide = jnp.concatenate([nb] * (LANES // SUB), axis=1)
    return [jnp.broadcast_to(wide[j : j + 1], (SUB, LANES)) for j in range(4)]


def y_slopes(t, ghosts):
    up, up_on, down, down_on = ghosts
    above = lanes_of(t[0], up) * up_on
    below = lanes_of(t[3], down) * down_on
    return [t[1] - below, t[2] - t[0], t[3] - t[1], above - t[2]]


def x_slopes(columns):
    sub = tile_iota(0)
    first, last = sub == 0, sub == SUB - 1
    get = [columns(q) for q in range(GROUPS)]
    easts = [[shifted(x, -1) for x in t] for t in get]
    wests = [[shifted(x, 1) for x in t] for t in get]
    for q in range(GROUPS):
        east, west = easts[q], wests[q]
        if q + 1 < GROUPS:
            east = [jnp.where(last, b, a) for a, b in zip(east, easts[q + 1])]
        if q > 0:
            west = [jnp.where(first, b, a) for a, b in zip(west, wests[q - 1])]
        yield [e - w for e, w in zip(east, west)]


def new_level(level, t0, t1, ca, sa, dx, dy, live):
    return (level + (t0 * ca + t1 * sa) - (dx + dy)) * live


def new_velocity(u, w, cor, dx, dy, live):
    return (
        (F32(0.985) * u + cor * w - F32(0.15) * dx) * live,
        (F32(0.985) * w - cor * u - F32(0.15) * dy) * live,
    )


NAMES = ("level", "east", "north", "depth", "live", "cor", "tide0", "tide1")


def fields_of(state, still):
    return {
        name: (state, f) if f < 3 else (still, f - 3) for f, name in enumerate(NAMES)
    }


def interior_steps(s, slices, steps, ghosts):
    sub = tile_iota(0)

    def tiles(name, q):
        ref, f = s[name]
        return [ref[f, i, pl.ds(SUB * q, SUB), :] for i in range(ROWS)]

    def put(name, q, k, new, old):
        ref, f = s[name]
        least = min(SUB * q, BS - SUB - SUB * q) + 1
        if k >= least + SUB - 1:
            return
        if k >= least:
            edge = (sub if q < GROUPS // 2 else SUB - 1 - sub) + least
            new = [jnp.where(edge > k, a, b) for a, b in zip(new, old)]
        for i in range(ROWS):
            ref[f, i, pl.ds(SUB * q, SUB), :] = new[i]

    def product(a, b):
        return [x * y for x, y in zip(a, b)]

    for step in steps:
        ca, sa = phase(slices, step)
        slope = x_slopes(lambda q: product(tiles("depth", q), tiles("east", q)))
        for q, dx in enumerate(slope):
            dy = y_slopes(product(tiles("depth", q), tiles("north", q)), ghosts)
            old = tiles("level", q)
            t0, t1, live = tiles("tide0", q), tiles("tide1", q), tiles("live", q)
            new = [
                new_level(old[i], t0[i], t1[i], ca, sa, dx[i], dy[i], live[i]) for i in range(ROWS)
            ]
            put("level", q, 2 * step + 1, new, old)
        slope = x_slopes(lambda q: tiles("level", q))
        for q, dx in enumerate(slope):
            dy = y_slopes(tiles("level", q), ghosts)
            u, w, cor, live = (tiles(n, q) for n in ("east", "north", "cor", "live"))
            new = [new_velocity(u[i], w[i], cor[i], dx[i], dy[i], live[i]) for i in range(ROWS)]
            put("east", q, 2 * step + 2, [a for a, _ in new], u)
            put("north", q, 2 * step + 2, [b for _, b in new], w)


def before_kernel(
    slices, count_ref, level_h, table_h, wet_h, nb_h, start_h, tide_h, cor_h,
    state, still, begin, face, pe, pw,
    level_id, table, wet, nb_ref, start, tide, cor, sems,
):
    loads = [
        pltpu.make_async_copy(src, dst, sems.at[i])
        for i, (src, dst) in enumerate(
            [
                (level_h, level_id), (table_h, table), (wet_h, wet), (nb_h, nb_ref),
                (start_h, start), (tide_h, tide), (cor_h, cor),
            ]
        )
    ]
    for load in loads:
        load.start()
    tiles = wet.shape[1] // LANES
    held = (tile_iota(0) < count_ref[0]).astype(F32)

    def store(ref, f, columns):
        for i in range(ROWS):
            ref[f, i] = columns[i]

    for load in loads[:4]:
        load.wait()
    row = F32(0.15) * table[...].reshape(1, table.shape[0])
    row = jnp.broadcast_to(jnp.concatenate([row] * (LANES // row.shape[1]), axis=1), (SUB, LANES))
    live = [lane_tile(wet, v).astype(F32) * held for v in range(tiles)]
    store(still, 1, to_columns(live))
    store(still, 0, to_columns([lanes_of(row, lane_tile(level_id, v)) for v in range(tiles)]))
    rows = face_rows(nb_ref[...])
    for j in range(4):
        face[j] = rows[j]
    loads[4].wait()
    for f in range(3):
        own = [lane_tile(start, v, (0, f)) * live[v] for v in range(tiles)]
        for v in range(tiles):
            begin[f, :, pl.ds(v * LANES, LANES)] = own[v]
        store(state, f, to_columns(own))
    loads[5].wait()
    for f in range(2):
        store(still, 3 + f, to_columns([lane_tile(tide, v, (f,)) for v in range(tiles)]))
    loads[6].wait()
    store(still, 2, to_columns([F32(0.3) * lane_tile(cor, v) for v in range(tiles)]))

    s = fields_of(state, still)
    interior_steps(s, slices, range(SENT), chunk_ghosts(rows[0], rows[1]))

    for f, name in enumerate(NAMES):
        ref, at = s[name]
        for i in range(ROWS):
            pe[i, pl.ds(OUT * f, OUT), :] = ref[at, i, pl.ds(BS - OUT, OUT), :]
            pw[i, pl.ds(OUT * f, OUT), :] = ref[at, i, pl.ds(0, OUT), :]
    for i in range(ROWS):
        pe[i, pl.ds(6 * OUT, 1), :] = state[0, i, pl.ds(BS - OUT - 1, 1), :]
        pw[i, pl.ds(6 * OUT + OUT - 1, 1), :] = state[0, i, pl.ds(OUT, 1), :]
        entry = rows[i][:1].astype(F32)
        pe[i, pl.ds(7 * OUT, 1), :] = entry
        pw[i, pl.ds(7 * OUT + OUT - 1, 1), :] = entry


def during_kernel(slices, state, still, face, last):
    last[...] = state[...]
    ghosts = chunk_ghosts(face[0], face[1])
    interior_steps(fields_of(last, still), slices, range(SENT, STEPS), ghosts)


def after_kernel(slices, pe, pw, last, still, face, begin, gain, defect, joined):
    tiles = begin.shape[-1] // LANES
    sub, lane = tile_iota(0), tile_iota(1)
    s = fields_of(last, still)

    for f, name in enumerate(NAMES):
        ref, at = s[name]
        for i in range(ROWS):
            joined[f, i, 0, pl.ds(0, OUT), :] = pe[i, pl.ds(OUT * f, OUT), :]
            joined[f, i, 0, pl.ds(OUT, 2), :] = ref[at, i, pl.ds(0, 2), :]
            joined[f, i, 1, pl.ds(0, 2), :] = ref[at, i, pl.ds(BS - 2, 2), :]
            joined[f, i, 1, pl.ds(2, OUT), :] = pw[i, pl.ds(OUT * f, OUT), :]

    def load(name, side, g):
        f = NAMES.index(name)
        if g == 0:
            return [joined[f, i, side] for i in range(ROWS)]
        ref, at = s[name]
        low = SUB * g - OUT
        low = low if side == 0 else BS - SUB - low
        return [ref[at, i, pl.ds(low, SUB), :] for i in range(ROWS)]

    own = [face[j] for j in range(4)]
    ghosts, joins, far = [], [], []
    for side in range(2):
        row = 0 if side == 0 else SUB - 1
        sent = [
            jnp.broadcast_to(joined[7, j, side, pl.ds(row, 1), :].astype(jnp.int32), (SUB, LANES))
            for j in range(4)
        ]
        outer = sub < OUT if side == 0 else sub >= 2
        mixed = [jnp.where(outer, sent[j], own[j]) for j in range(4)]
        here = chunk_ghosts(own[0], own[1])
        ghosts.append([chunk_ghosts(mixed[0], mixed[1]), here, here])
        to = jnp.where(outer, own[3 - side], sent[2 + side])
        joins.append((lane - lane % SUB + jnp.maximum(to, 0), (to >= 0).astype(F32)))
    inner_row = (OUT, 1)
    outer_row = (OUT - 1, 2)

    def x_side(side, t, beyond=None):
        index, on = joins[side]
        looked = [lanes_of(x, index) * on for x in t[0]]
        inner = [jnp.where(sub == inner_row[side], b, a) for a, b in zip(t[0], looked)]
        outer = [jnp.where(sub == outer_row[side], b, a) for a, b in zip(t[0], looked)]
        sign = -1 if side == 0 else 1
        end_in, end_out = (SUB - 1, 0) if side == 0 else (0, SUB - 1)
        inward = [[shifted(x, sign) for x in inner]]
        outward = [[shifted(x, -sign) for x in outer]]
        if beyond is not None:
            outward[0] = [jnp.where(sub == end_out, b, a) for a, b in zip(outward[0], beyond)]
        plain_out = [[shifted(x, -sign) for x in t[0]]]
        for g in range(1, len(t)):
            inward.append([shifted(x, sign) for x in t[g]])
            plain_out.append([shifted(x, -sign) for x in t[g]])
        for g in range(1, len(t)):
            outward.append(
                [jnp.where(sub == end_out, b, a) for a, b in zip(plain_out[g], plain_out[g - 1])]
            )
        for g in range(len(t) - 1):
            inward[g] = [
                jnp.where(sub == end_in, b, a) for a, b in zip(inward[g], inward[g + 1])
            ]
        return [
            [(a - b) if side == 0 else (b - a) for a, b in zip(inward[g], outward[g])]
            for g in range(len(t))
        ]

    def changed(side, g, k):
        place = sub if side == 0 else SUB - 1 - sub
        if g == 0:
            reach = min(k, HALF - k)
            mask = place >= OUT - reach
            return mask if k >= 2 else jnp.logical_and(mask, place <= OUT)
        least = SUB * g - OUT + 1
        if k < least:
            return False
        return None if k >= least + SUB - 1 else place + least <= k

    cells = {
        (n, side, g): load(n, side, g)
        for n in ("level", "east", "north") for side in range(2) for g in range(3)
    }

    def put(name, side, g, mask, new):
        key = (name, side, g)
        if mask is not None:
            new = [jnp.where(mask, a, b) for a, b in zip(new, cells[key])]
        cells[key] = new

    def product(a, b):
        return [x * y for x, y in zip(a, b)]

    for k in range(1, HALF + 1):
        ca, sa = phase(slices, (k - 1) // 2)
        active = [g for g in range(3) if changed(0, g, k) is not False]
        reach = min(3, len(active) + 1)
        for side in range(2):
            if k % 2 == 1:
                depth = [load("depth", side, g) for g in range(reach)]
                dx = x_side(
                    side, [product(depth[g], cells["east", side, g]) for g in range(reach)]
                )
                for g in active:
                    flux = product(depth[g], cells["north", side, g])
                    dy = y_slopes(flux, ghosts[side][g])
                    t0, t1, live = (load(n, side, g) for n in ("tide0", "tide1", "live"))
                    old = cells["level", side, g]
                    new = [
                        new_level(old[i], t0[i], t1[i], ca, sa, dx[g][i], dy[i], live[i])
                        for i in range(ROWS)
                    ]
                    put("level", side, g, changed(side, g, k), new)
            else:
                beyond = load("tide0", side, 0) if k == OUT else None
                dx = x_side(side, [cells["level", side, g] for g in range(reach)], beyond)
                for g in active:
                    dy = y_slopes(cells["level", side, g], ghosts[side][g])
                    cor, live = load("cor", side, g), load("live", side, g)
                    u, w = cells["east", side, g], cells["north", side, g]
                    new = [
                        new_velocity(u[i], w[i], cor[i], dx[g][i], dy[i], live[i])
                        for i in range(ROWS)
                    ]
                    mask = changed(side, g, k)
                    put("east", side, g, mask, [a for a, _ in new])
                    put("north", side, g, mask, [b for _, b in new])

    for f, name in enumerate(NAMES[:3]):
        fine = []
        for i in range(ROWS):
            a, b, c = (shifted(cells[name, 0, g][i], 2) for g in range(3))
            d, e, h = (shifted(cells[name, 1, g][i], -2) for g in range(3))
            q = [last[f, i, pl.ds(SUB * n, SUB), :] for n in range(GROUPS)]
            q[0] = jnp.where(sub < 2, a, b)
            q[1] = jnp.where(sub < 2, b, jnp.where(sub < 4, c, q[1]))
            q[6] = jnp.where(sub >= 6, e, jnp.where(sub >= 4, h, q[6]))
            q[7] = jnp.where(sub >= 6, d, e)
            fine.append(jnp.concatenate(q, axis=0))
        for v, x in enumerate(to_tiles(fine)):
            at = pl.ds(v * LANES, LANES)
            defect[f, :, at] = x - gain[f, :, at] * begin[f, :, at]


def call(kernel, out_shape, operands, spaces=None, scratch=()):
    vmem = pl.BlockSpec(memory_space=pltpu.VMEM)
    spaces = spaces or [pltpu.VMEM] * len(operands)
    size = sum(4 * x.size for x in operands)
    return pl.pallas_call(
        kernel,
        out_shape=out_shape,
        in_specs=[pl.BlockSpec(memory_space=space) for space in spaces],
        out_specs=jax.tree.map(lambda _: vmem, out_shape),
        scratch_shapes=scratch,
        cost_estimate=pl.CostEstimate(flops=0, bytes_accessed=2 * size, transcendentals=0),
        compiler_params=pltpu.CompilerParams(vmem_limit_bytes=VMEM_LIMIT),
    )(*operands)


def shape(*dims):
    return jax.ShapeDtypeStruct(dims, F32)


def passed_along(shard, axis, by):
    size = lax.axis_size(axis)
    return lax.ppermute(shard, axis, [(i, (i + by) % size) for i in range(size)])


def body(
    start_states, coarse_gain, depth_level, depth_table, wet, block_count, neighbour, coriolis, tide
):
    slots, cells = wet.shape
    slices = lax.axis_size("tm")
    loaded = [depth_level, depth_table, wet, neighbour.T, start_states, tide, coriolis]
    state, still, begin, face, pe, pw = call(
        functools.partial(before_kernel, slices),
        [shape(3, ROWS, BS, LANES), shape(5, ROWS, BS, LANES), shape(3, slots, cells)]
        + [jax.ShapeDtypeStruct((4, SUB, LANES), jnp.int32)]
        + [shape(ROWS, len(NAMES) * OUT, LANES)] * 2,
        [block_count] + [pltpu.with_memory_space_constraint(x, pltpu.HBM) for x in loaded],
        spaces=[pltpu.SMEM] + [pltpu.HBM] * len(loaded),
        scratch=[pltpu.VMEM(x.shape, x.dtype) for x in loaded]
        + [pltpu.SemaphoreType.DMA((len(loaded),))],
    )
    from_west = passed_along(pe, "space", 1)
    from_east = passed_along(pw, "space", -1)
    last = call(
        functools.partial(during_kernel, slices),
        shape(3, ROWS, BS, LANES),
        [state, still, face],
    )
    defect = call(
        functools.partial(after_kernel, slices),
        shape(3, slots, cells),
        [from_west, from_east, last, still, face, begin, coarse_gain],
        scratch=[pltpu.VMEM((len(NAMES), ROWS, 2, SUB, LANES), F32)],
    )
    total, power = passed_along(defect, "tm", 1), coarse_gain
    for _ in range(slices - 2):
        total = passed_along(defect + coarse_gain * total, "tm", 1)
        power = power * coarse_gain
    total = total + power * defect
    return (total / (1.0 - power * coarse_gain))[None]


def solution(mesh):
    return jax.shard_map(
        body,
        mesh=mesh,
        in_specs=(
            P("tm", None, "space", None),
            P(None, "space", None),
            P("space", None),
            P(),
            P("space", None),
            P("space"),
            P("space", None),
            P("space", None),
            P(None, "space", None),
        ),
        out_specs=P("tm", None, "space", None),
        check_vma=False,
    )
```

time: 135 us -> 16.8 us (0.12)
  waiting for transfers between devices: 61.2 us -> 4.05 us
  local copies, waits for them, and re-layouts: 25.2 us -> 0.01 us
  starting transfers between devices: 30.4 us -> 7.12 us
  matrix products: 8.83 us -> 0 us
  other arithmetic: 6.27 us -> 0.85 us
  Pallas kernels: 0 us -> 3.98 us
  between operations: 2.34 us -> 0.68 us
    ppermute x24 -> x0, waiting for transfers between devices: 57.9 us -> none  [the longest x12 44.7 us: padded(): lax.ppermute(lax.slice_in_dim(block, block.shape[dim] - width, None, axis...]
    ppermute x24 -> x0, starting transfers between devices: 30.1 us -> none  [the longest x12 21.7 us: padded(): lax.ppermute(lax.slice_in_dim(block, block.shape[dim] - width, None, axis...]
    dot_general x48 -> x0, matrix products: 8.83 us -> none  [take_edges(): jnp.dot(select, edges, precision=lax.Precision.HIGHEST, preferred_element...]
    dynamic_slice x8 -> x0, local copies, waits for them, and re-layouts: 7.41 us -> none  [body(): depth = lax.map(depth_row, depth_level)]
    ppermute x2 -> x3, starting transfers between devices: 0.27 us -> 7.12 us  [passed_along(): lax.ppermute(shard, axis, [(i, (i + by) % size) for i in range(size)])]
    slice x48 -> x0, local copies, waits for them, and re-layouts: 5.6 us -> none  [the longest x24 3.33 us: edge_pair(): return jnp.stack([field[:, 0::BS], field[:, BS - 1::BS]])]
    pallas_call x0 -> x3, Pallas kernels: none -> 3.98 us  [call(): pl.pallas_call(kernel, out_shape=out_shape, in_specs=[pl.BlockSpec(memory...]
    broadcast_in_dim x24 -> x0, local copies, waits for them, and re-layouts: 3.2 us -> none  [the longest x12 1.6 us: across(): jnp.repeat(west_ghost, BS, axis=-1)]
  transfers between devices with their start and end apart: 26 -> 3, of which waited for: 25 -> 2; matrix products, arithmetic and copies ran while one was open for 7% -> 0% of each run, Pallas kernels for 0% -> 3%
where the time goes in v3:
time: 16.8 us; the launch traced here: 16.7 us
  starting transfers between devices  7.12 us (42%)
  waiting for transfers between devices  4.05 us (24%)
  Pallas kernels  3.98 us (24%)
  other arithmetic  0.85 us (5%)
  between operations  0.68 us (4%)
    ppermute x3, starting transfers between devices, passed_along(): lax.ppermute(shard, axis, [(i, (i + by) % size) for i in range(size)])  7.12 us
    ppermute x3, waiting for transfers between devices, passed_along(): lax.ppermute(shard, axis, [(i, (i + by) % size) for i in range(size)])  4.05 us
    pallas_call x3, Pallas kernels, call(): pl.pallas_call(kernel, out_shape=out_shape, in_specs=[pl.BlockSpec(memory...  3.98 us
    broadcast_in_dim x1, other arithmetic, body(): return (total / (1.0 - power * coarse_gain))[None]  0.85 us
  transfers between devices with their start and end apart: 3, of which 2 were waited for; matrix products, arithmetic and copies ran while one was open for 0% of the time, Pallas kernels for 3%

profile of v3, /device:TPU:0, one launch (start us, length us, event | category | flops | bytes accessed | tf_op | source)
XLA Modules:
  0.0 16.7 jit_solution(10409969081711945313)
XLA Ops:
  0.7 2.3 %shard_map.91 = (f32[3,4,64,128]{3,2,1,0:T(8,128)S(1)}, f32[5,4,64,128]{3,2,1,0:T(8,128)S(1)}, f32[3,8,4096]{2,1,0:T(8,128)S(1)}, s32[4,8,128]{2,1,0:T(8,128)S(1...) custom-call(s32[1]{0:T(128)S(6)} %copy.10.count_ref, s32[8,4096]{1,0:T(8,128)} %level_h.1, f32[64]{0:T(128)} %table_h.1, ...), custom_call_target="tpu_custom_call" | custom-call | bytes 2097928 | tf_op jit(solution)/shard_map/pallas_call | solution.py:380
  2.9 3.0 %collective-permute-start = (f32[4,48,128]{2,1,0:T(8,128)S(1)}, f32[4,48,128]{2,1,0:T(8,128)S(1)}, u32[]{:S(2)}, u32[]{:S(2)}) collective-permute-start(f32[4,48,128]{2,1,0:T(8,128)S(1)} %get-tuple-element.11), channel_id=1, source_target_pairs={{0,1},{1,2},{2,3},{3,4},{4,5},{5,6},{6,7},{7,8},{8,9},{9,10},{10,1... | collective-permute-start | bytes 294920 | tf_op jit(solution)/shard_map/ppermute | solution.py:397
  5.9 4.1 %collective-permute-start.1 = (f32[4,48,128]{2,1,0:T(8,128)S(1)}, f32[4,48,128]{2,1,0:T(8,128)S(1)}, u32[]{:S(2)}, u32[]{:S(2)}) collective-permute-start(f32[4,48,128]{2,1,0:T(8,128)S(1)} %get-tuple-element.12), channel_id=1, source_target_pairs={{0,15},{1,0},{2,1},{3,2},{4,3},{5,4},{6,5},{7,6},{8,7},{9,8},{10,9... | collective-permute-start | bytes 294920 | tf_op jit(solution)/shard_map/ppermute | solution.py:397
  10.0 0.0 copy-start
  10.0 0.5 %shard_map.92.last = f32[3,4,64,128]{3,2,1,0:T(8,128)S(1)} custom-call(f32[3,4,64,128]{3,2,1,0:T(8,128)S(1)} %get-tuple-element.13.state, f32[5,4,64,128]{3,2,1,0:T(8,128)S(1)} %get-tuple-element.14.still, s32[4,8,128]{2,1,0:T(8,128)S(1)} %get-tuple-element.15.face), custom_call_target="tpu_custom_call" | custom-call | bytes 2129920 | tf_op jit(solution)/shard_map/pallas_call | solution.py:380
  10.5 2.3 %collective-permute-done.pe = f32[4,48,128]{2,1,0:T(8,128)S(1)} collective-permute-done((f32[4,48,128]{2,1,0:T(8,128)S(1)}, f32[4,48,128]{2,1,0:T(8,128)S(1)}, u32[]{:S(2)}, u32[]{:S(2)}) %collective-permute-start) | collective-permute-done | bytes 98336 | tf_op jit(solution)/shard_map/ppermute | solution.py:397
  12.8 0.0 collective-permute-done.1.pw
  12.8 0.0 copy-done
  12.8 1.2 %shard_map.93 = f32[3,8,4096]{2,1,0:T(8,128)S(1)} custom-call(f32[4,48,128]{2,1,0:T(8,128)S(1)} %collective-permute-done.pe, f32[4,48,128]{2,1,0:T(8,128)S(1)} %collective-permute-done.1.pw, f32[3,4,64,128]{3,2,1,0:T(8,128)S(1)} %shard_map.92.last, f32[5,4,64,128]{3,2,1,0:T(8,128)S(1)} %get-tuple-element.14.still, s32[4,8,128]{2,1,0:T(8,128)S(1)} %get-tuple-element.15.face, ...), custom_call_target="tpu_custom_call" | custom-call | bytes 4096000 | tf_op jit(solution)/shard_map/pallas_call | solution.py:380
  14.0 0.1 collective-permute-start.2
  14.1 1.7 %collective-permute-done.2 = f32[3,8,4096]{2,1,0:T(8,128)S(1)} collective-permute-done((f32[3,8,4096]{2,1,0:T(8,128)S(1)}, f32[3,8,4096]{2,1,0:T(8,128)S(1)}, u32[]{:S(2)}, u32[]{:S(2)}) %collective-permute-start.2) | collective-permute-done | bytes 393248 | tf_op jit(solution)/shard_map/ppermute | solution.py:397
  15.8 0.8 %divide_bitcast_fusion = f32[1,3,8,4096]{3,2,1,0:T(8,128)} fusion(f32[3,8,4096]{2,1,0:T(8,128)S(1)} %copy-done, f32[3,8,4096]{2,1,0:T(8,128)S(1)} %collective-permute-done.2, f32[3,8,4096]{2,1,0:T(8,128)S(1)} %shard_map.93), kind=kLoop, calls=%fused_computation | loop fusion | flops 491520 | bytes 1572864 | tf_op jit(solution)/shard_map/broadcast_in_dim | solution.py:434
Async XLA Ops:
  2.9 9.9 %collective-permute-start = (f32[4,48,128]{2,1,0:T(8,128)S(1)}, f32[4,48,128]{2,1,0:T(8,128)S(1)}, u32[]{:S(2)}, u32[]{:S(2)}) collective-permute-start(f32[4,48,128]{2,1,0:T(8,128)S(1)} %get-tuple-element.11), channel_id=1, source_target_pairs={{0,1},{1,2},{2,3},{3,4},{4,5},{5,6},{6,7},{7,8},{8,9},{9,10},{10,1... | collective-permute-start | bytes 294920 | tf_op jit(solution)/shard_map/ppermute | solution.py:397
  5.9 6.9 %collective-permute-start.1 = (f32[4,48,128]{2,1,0:T(8,128)S(1)}, f32[4,48,128]{2,1,0:T(8,128)S(1)}, u32[]{:S(2)}, u32[]{:S(2)}) collective-permute-start(f32[4,48,128]{2,1,0:T(8,128)S(1)} %get-tuple-element.12), channel_id=1, source_target_pairs={{0,15},{1,0},{2,1},{3,2},{4,3},{5,4},{6,5},{7,6},{8,7},{9,8},{10,9... | collective-permute-start | bytes 294920 | tf_op jit(solution)/shard_map/ppermute | solution.py:397
  10.0 2.8 %copy-start = (f32[3,8,4096]{2,1,0:T(8,128)S(1)}, f32[3,8,4096]{2,1,0:T(8,128)}, u32[]{:S(2)}) copy-start(f32[3,8,4096]{2,1,0:T(8,128)} %gain.1) | copy-start | bytes 1179652
  14.0 1.8 %collective-permute-start.2 = (f32[3,8,4096]{2,1,0:T(8,128)S(1)}, f32[3,8,4096]{2,1,0:T(8,128)S(1)}, u32[]{:S(2)}, u32[]{:S(2)}) collective-permute-start(f32[3,8,4096]{2,1,0:T(8,128)S(1)} %shard_map.93), channel_id=1, source_target_pairs={{0,16},{16,0},{1,17},{17,1},{2,18},{18,2},{3,19},{19,3},{4,20},{20... | collective-permute-start | bytes 1179656 | tf_op jit(solution)/shard_map/ppermute | solution.py:397

commit v4 on v3

--- a/solution.py
+++ b/solution.py
@@ -75,6 +75,11 @@
     return up, up_on, down, down_on
 
 
+def two_way_ghosts(ghosts):
+    up, up_on, down, down_on = ghosts
+    return lanes_of(down, up), lanes_of(down_on, up), lanes_of(up, down), lanes_of(up_on, down)
+
+
 def face_rows(nb):
     wide = jnp.concatenate([nb] * (LANES // SUB), axis=1)
     return [jnp.broadcast_to(wide[j : j + 1], (SUB, LANES)) for j in range(4)]
@@ -87,19 +92,20 @@
     return [t[1] - below, t[2] - t[0], t[3] - t[1], above - t[2]]
 
 
-def x_slopes(columns):
+def x_slopes(columns, runs):
     sub = tile_iota(0)
     first, last = sub == 0, sub == SUB - 1
-    get = [columns(q) for q in range(GROUPS)]
-    easts = [[shifted(x, -1) for x in t] for t in get]
-    wests = [[shifted(x, 1) for x in t] for t in get]
-    for q in range(GROUPS):
-        east, west = easts[q], wests[q]
-        if q + 1 < GROUPS:
-            east = [jnp.where(last, b, a) for a, b in zip(east, easts[q + 1])]
-        if q > 0:
-            west = [jnp.where(first, b, a) for a, b in zip(west, wests[q - 1])]
-        yield [e - w for e, w in zip(east, west)]
+    for run in runs:
+        get = [columns(q) for q in run]
+        easts = [[shifted(x, -1) for x in t] for t in get]
+        wests = [[shifted(x, 1) for x in t] for t in get]
+        for n, q in enumerate(run):
+            east, west = easts[n], wests[n]
+            if n + 1 < len(run):
+                east = [jnp.where(last, b, a) for a, b in zip(east, easts[n + 1])]
+            if n > 0:
+                west = [jnp.where(first, b, a) for a, b in zip(west, wests[n - 1])]
+            yield q, [e - w for e, w in zip(east, west)]
 
 
 def new_level(level, t0, t1, ca, sa, dx, dy, live):
@@ -122,12 +128,13 @@
     }
 
 
-def interior_steps(s, slices, steps, ghosts):
+def interior_steps(s, runs, slices, steps, ghosts, wide):
     sub = tile_iota(0)
+    place = {q: SUB * n for n, q in enumerate(q for run in runs for q in run)}
 
     def tiles(name, q):
         ref, f = s[name]
-        return [ref[f, i, pl.ds(SUB * q, SUB), :] for i in range(ROWS)]
+        return [ref[f, i, pl.ds(place[q], SUB), :] for i in range(ROWS)]
 
     def put(name, q, k, new, old):
         ref, f = s[name]
@@ -138,100 +145,184 @@
             edge = (sub if q < GROUPS // 2 else SUB - 1 - sub) + least
             new = [jnp.where(edge > k, a, b) for a, b in zip(new, old)]
         for i in range(ROWS):
-            ref[f, i, pl.ds(SUB * q, SUB), :] = new[i]
+            ref[f, i, pl.ds(place[q], SUB), :] = new[i]
 
     def product(a, b):
         return [x * y for x, y in zip(a, b)]
 
+    up, up_on, down, down_on = ghosts
+    if wide:
+        back_up, back_up_on, back_down, back_down_on = two_way_ghosts(ghosts)
+    live_over, live_under = {}, {}
+    for q in place if wide else ():
+        live = tiles("live", q)
+        live_over[q] = lanes_of(live[0], up) * up_on
+        live_under[q] = lanes_of(live[3], down) * down_on
     for step in steps:
         ca, sa = phase(slices, step)
-        slope = x_slopes(lambda q: product(tiles("depth", q), tiles("east", q)))
-        for q, dx in enumerate(slope):
-            dy = y_slopes(product(tiles("depth", q), tiles("north", q)), ghosts)
+        slope = x_slopes(lambda q: product(tiles("depth", q), tiles("east", q)), runs)
+        dys = {}
+        for q, dx in slope:
             old = tiles("level", q)
             t0, t1, live = tiles("tide0", q), tiles("tide1", q), tiles("live", q)
-            new = [
-                new_level(old[i], t0[i], t1[i], ca, sa, dx[i], dy[i], live[i]) for i in range(ROWS)
-            ]
+            part = [old[i] + (t0[i] * ca + t1[i] * sa) - dx[i] for i in range(ROWS)]
+            flux = product(tiles("depth", q), tiles("north", q))
+            above, below = lanes_of(flux[0], up) * up_on, lanes_of(flux[3], down) * down_on
+            north = flux[1:] + [above]
+            south = [below] + flux[:3]
+            new = [(part[i] - (north[i] - south[i])) * live[i] for i in range(ROWS)]
             put("level", q, 2 * step + 1, new, old)
-        slope = x_slopes(lambda q: tiles("level", q))
-        for q, dx in enumerate(slope):
-            dy = y_slopes(tiles("level", q), ghosts)
+            if not wide:
+                continue
+            over = lanes_of(flux[1], up) - lanes_of(flux[3], back_up) * back_up_on
+            over = (lanes_of(part[0], up) - over) * live_over[q]
+            under = lanes_of(flux[0], back_down) * back_down_on - lanes_of(flux[2], down)
+            under = (lanes_of(part[3], down) - under) * live_under[q]
+            dys[q] = [new[1] - under, new[2] - new[0], new[3] - new[1], over - new[2]]
+        slope = x_slopes(lambda q: tiles("level", q), runs)
+        for q, dx in slope:
             u, w, cor, live = (tiles(n, q) for n in ("east", "north", "cor", "live"))
+            dy = dys[q] if wide else y_slopes(tiles("level", q), ghosts)
             new = [new_velocity(u[i], w[i], cor[i], dx[i], dy[i], live[i]) for i in range(ROWS)]
             put("east", q, 2 * step + 2, [a for a, _ in new], u)
             put("north", q, 2 * step + 2, [b for _, b in new], w)
 
 
+PARTS = ((0, 1, GROUPS - 2, GROUPS - 1), tuple(range(2, GROUPS - 2)))
+ALL = tuple(range(GROUPS))
+
+
+def started(pairs, sems):
+    loads = [pltpu.make_async_copy(src, dst, sems.at[i]) for i, (src, dst) in enumerate(pairs)]
+    for load in loads:
+        load.start()
+    return loads
+
+
+def prepare(state, still, groups, level_id, table, wet, start, tide, cor, count_ref, wait):
+    tiles = wet.shape[1] // LANES
+    held = tile_iota(0) < count_ref[0]
+
+    def turn(source, put):
+        for i, columns in enumerate(to_columns([source(v) for v in range(tiles)])):
+            for n, q in enumerate(groups):
+                put((i, pl.ds(SUB * n, SUB)), columns[SUB * q : SUB * q + SUB])
+
+    def store(ref, f, source):
+        def put(at, x):
+            ref[f, at[0], at[1], :] = x
+
+        turn(source, put)
+
+    wait(0)
+    levels = table.shape[0]
+    row = F32(0.15) * table[...].reshape(1, levels)
+    row = jnp.concatenate([row, jnp.zeros((1, LANES - levels), F32)], axis=1)
+    row = jnp.broadcast_to(row, (SUB, LANES))
+
+    def coded(v):
+        here = jnp.logical_and(lane_tile(wet, v) > 0, held)
+        return jnp.where(here, lane_tile(level_id, v), levels)
+
+    def store_depth(at, code):
+        still[0, at[0], at[1], :] = lanes_of(row, code)
+        still[1, at[0], at[1], :] = (code < levels).astype(F32)
+
+    turn(coded, store_depth)
+    wait(1)
+
+    def store_state(f):
+        def put(at, x):
+            state[f, at[0], at[1], :] = x * still[1, at[0], at[1], :]
+
+        return put
+
+    for f in range(3):
+        turn(lambda v, f=f: lane_tile(start, v, (0, f)), store_state(f))
+    wait(2)
+    for f in range(2):
+        store(still, 3 + f, lambda v, f=f: lane_tile(tide, v, (f,)))
+    wait(3)
+    store(still, 2, lambda v: F32(0.3) * lane_tile(cor, v))
+
+
 def before_kernel(
     slices, count_ref, level_h, table_h, wet_h, nb_h, start_h, tide_h, cor_h,
-    state, still, begin, face, pe, pw,
-    level_id, table, wet, nb_ref, start, tide, cor, sems,
+    level_id, table, wet, start, tide, cor, face, pe, pw,
+    nb_ref, state, still, sems,
 ):
-    loads = [
-        pltpu.make_async_copy(src, dst, sems.at[i])
-        for i, (src, dst) in enumerate(
-            [
-                (level_h, level_id), (table_h, table), (wet_h, wet), (nb_h, nb_ref),
-                (start_h, start), (tide_h, tide), (cor_h, cor),
-            ]
-        )
-    ]
-    for load in loads:
-        load.start()
-    tiles = wet.shape[1] // LANES
-    held = (tile_iota(0) < count_ref[0]).astype(F32)
-
-    def store(ref, f, columns):
-        for i in range(ROWS):
-            ref[f, i] = columns[i]
-
-    for load in loads[:4]:
-        load.wait()
-    row = F32(0.15) * table[...].reshape(1, table.shape[0])
-    row = jnp.broadcast_to(jnp.concatenate([row] * (LANES // row.shape[1]), axis=1), (SUB, LANES))
-    live = [lane_tile(wet, v).astype(F32) * held for v in range(tiles)]
-    store(still, 1, to_columns(live))
-    store(still, 0, to_columns([lanes_of(row, lane_tile(level_id, v)) for v in range(tiles)]))
+    loads = started(
+        [
+            (level_h, level_id), (table_h, table), (wet_h, wet), (nb_h, nb_ref),
+            (start_h, start), (tide_h, tide), (cor_h, cor),
+        ],
+        sems,
+    )
+
+    def wait(n):
+        for load in (loads[:4], loads[4:5], loads[5:6], loads[6:])[n]:
+            load.wait()
+
+    prepare(state, still, PARTS[0], level_id, table, wet, start, tide, cor, count_ref, wait)
     rows = face_rows(nb_ref[...])
     for j in range(4):
         face[j] = rows[j]
-    loads[4].wait()
-    for f in range(3):
-        own = [lane_tile(start, v, (0, f)) * live[v] for v in range(tiles)]
-        for v in range(tiles):
-            begin[f, :, pl.ds(v * LANES, LANES)] = own[v]
-        store(state, f, to_columns(own))
-    loads[5].wait()
-    for f in range(2):
-        store(still, 3 + f, to_columns([lane_tile(tide, v, (f,)) for v in range(tiles)]))
-    loads[6].wait()
-    store(still, 2, to_columns([F32(0.3) * lane_tile(cor, v) for v in range(tiles)]))
-
     s = fields_of(state, still)
-    interior_steps(s, slices, range(SENT), chunk_ghosts(rows[0], rows[1]))
-
+    runs = (PARTS[0][:2], PARTS[0][2:])
+    interior_steps(s, runs, slices, range(SENT), chunk_ghosts(rows[0], rows[1]), True)
+
+    end = SUB * len(PARTS[0])
     for f, name in enumerate(NAMES):
         ref, at = s[name]
         for i in range(ROWS):
-            pe[i, pl.ds(OUT * f, OUT), :] = ref[at, i, pl.ds(BS - OUT, OUT), :]
+            pe[i, pl.ds(OUT * f, OUT), :] = ref[at, i, pl.ds(end - OUT, OUT), :]
             pw[i, pl.ds(OUT * f, OUT), :] = ref[at, i, pl.ds(0, OUT), :]
     for i in range(ROWS):
-        pe[i, pl.ds(6 * OUT, 1), :] = state[0, i, pl.ds(BS - OUT - 1, 1), :]
+        pe[i, pl.ds(6 * OUT, 1), :] = state[0, i, pl.ds(end - OUT - 1, 1), :]
         pw[i, pl.ds(6 * OUT + OUT - 1, 1), :] = state[0, i, pl.ds(OUT, 1), :]
         entry = rows[i][:1].astype(F32)
         pe[i, pl.ds(7 * OUT, 1), :] = entry
         pw[i, pl.ds(7 * OUT + OUT - 1, 1), :] = entry
 
 
-def during_kernel(slices, state, still, face, last):
-    last[...] = state[...]
+def power(x, n):
+    return functools.reduce(lambda a, b: a * b, [x] * n)
+
+
+def part_tile(ref, f, i, n):
+    return ref[f, i, pl.ds(SUB * n, SUB), :]
+
+
+def during_kernel(
+    slices, level_id, table, wet, start, tide, cor, face, count_ref, gain_h,
+    last, still, inner, inner_gain, edge_gain, edge_base,
+    gain, sems,
+):
+    loads = started([(gain_h, gain)], sems)
+    tiles = wet.shape[1] // LANES
+    prepare(last, still, ALL, level_id, table, wet, start, tide, cor, count_ref, lambda n: None)
     ghosts = chunk_ghosts(face[0], face[1])
-    interior_steps(fields_of(last, still), slices, range(SENT, STEPS), ghosts)
-
-
-def after_kernel(slices, pe, pw, last, still, face, begin, gain, defect, joined):
-    tiles = begin.shape[-1] // LANES
+    interior_steps(fields_of(last, still), (ALL,), slices, range(STEPS), ghosts, False)
+    held = (tile_iota(0) < count_ref[0]).astype(F32)
+    for load in loads:
+        load.wait()
+    for f in range(3):
+        gains = [lane_tile(gain, v, (f,)) for v in range(tiles)]
+        base = [
+            gains[v] * (lane_tile(start, v, (0, f)) * (lane_tile(wet, v).astype(F32) * held))
+            for v in range(tiles)
+        ]
+        gains, base = to_columns(gains), to_columns(base)
+        for i in range(ROWS):
+            for n in range(GROUPS // 2):
+                at, to = [slice(SUB * part[n], SUB * part[n] + SUB) for part in PARTS], pl.ds(SUB * n, SUB)
+                edge_gain[f, i, to, :] = gains[i][at[0]]
+                edge_base[f, i, to, :] = base[i][at[0]]
+                inner_gain[f, i, to, :] = gains[i][at[1]]
+                inner[f, i, to, :] = last[f, i, pl.ds(SUB * PARTS[1][n], SUB), :] - base[i][at[1]]
+
+
+def after_kernel(slices, pe, pw, last, still, face, base, edge, joined):
     sub, lane = tile_iota(0), tile_iota(1)
     s = fields_of(last, still)
 
@@ -358,30 +449,52 @@
                     put("north", side, g, mask, [b for _, b in new])
 
     for f, name in enumerate(NAMES[:3]):
-        fine = []
         for i in range(ROWS):
             a, b, c = (shifted(cells[name, 0, g][i], 2) for g in range(3))
             d, e, h = (shifted(cells[name, 1, g][i], -2) for g in range(3))
-            q = [last[f, i, pl.ds(SUB * n, SUB), :] for n in range(GROUPS)]
-            q[0] = jnp.where(sub < 2, a, b)
-            q[1] = jnp.where(sub < 2, b, jnp.where(sub < 4, c, q[1]))
-            q[6] = jnp.where(sub >= 6, e, jnp.where(sub >= 4, h, q[6]))
-            q[7] = jnp.where(sub >= 6, d, e)
-            fine.append(jnp.concatenate(q, axis=0))
-        for v, x in enumerate(to_tiles(fine)):
-            at = pl.ds(v * LANES, LANES)
-            defect[f, :, at] = x - gain[f, :, at] * begin[f, :, at]
-
-
-def call(kernel, out_shape, operands, spaces=None, scratch=()):
-    vmem = pl.BlockSpec(memory_space=pltpu.VMEM)
+            inside = [last[f, i, pl.ds(SUB * q, SUB), :] for q in PARTS[0][1:3]]
+            fine = [
+                jnp.where(sub < 2, a, b),
+                jnp.where(sub < 2, b, jnp.where(sub < 4, c, inside[0])),
+                jnp.where(sub >= 6, e, jnp.where(sub >= 4, h, inside[1])),
+                jnp.where(sub >= 6, d, e),
+            ]
+            for n, x in enumerate(fine):
+                edge[f, i, pl.ds(SUB * n, SUB), :] = x - part_tile(base, f, i, n)
+
+
+def final_kernel(
+    slices, edge_sum, edge, edge_gain, inner_sum, inner, inner_gain, result, out, sems
+):
+    parts = ((edge_sum, edge, edge_gain), (inner_sum, inner, inner_gain))
+    copies = []
+    for f in range(3):
+        columns = []
+        for i in range(ROWS):
+            q = [None] * GROUPS
+            for groups, (total, own, gain) in zip(PARTS, parts):
+                for n, group in enumerate(groups):
+                    g = part_tile(gain, f, i, n)
+                    most = power(g, slices - 1)
+                    whole = part_tile(total, f, i, n) + most * part_tile(own, f, i, n)
+                    q[group] = whole / (F32(1) - most * g)
+            columns.append(jnp.concatenate(q, axis=0))
+        for v, x in enumerate(to_tiles(columns)):
+            out[0, f, :, pl.ds(v * LANES, LANES)] = x
+        copies.append(pltpu.make_async_copy(out.at[0, f], result.at[0, f], sems.at[f]))
+        copies[-1].start()
+    for copy in copies:
+        copy.wait()
+
+
+def call(kernel, out_shape, operands, spaces=None, out_space=pltpu.VMEM, scratch=()):
     spaces = spaces or [pltpu.VMEM] * len(operands)
     size = sum(4 * x.size for x in operands)
     return pl.pallas_call(
         kernel,
         out_shape=out_shape,
         in_specs=[pl.BlockSpec(memory_space=space) for space in spaces],
-        out_specs=jax.tree.map(lambda _: vmem, out_shape),
+        out_specs=jax.tree.map(lambda _: pl.BlockSpec(memory_space=out_space), out_shape),
         scratch_shapes=scratch,
         cost_estimate=pl.CostEstimate(flops=0, bytes_accessed=2 * size, transcendentals=0),
         compiler_params=pltpu.CompilerParams(vmem_limit_bytes=VMEM_LIMIT),
@@ -392,46 +505,67 @@
     return jax.ShapeDtypeStruct(dims, F32)
 
 
+def in_hbm(arrays):
+    return [pltpu.with_memory_space_constraint(x, pltpu.HBM) for x in arrays]
+
+
 def passed_along(shard, axis, by):
     size = lax.axis_size(axis)
     return lax.ppermute(shard, axis, [(i, (i + by) % size) for i in range(size)])
 
 
+def periodic_sum(defect, gain, slices):
+    total = passed_along(defect, "tm", 1)
+    for _ in range(slices - 2):
+        total = passed_along(defect + gain * total, "tm", 1)
+    return total
+
+
 def body(
     start_states, coarse_gain, depth_level, depth_table, wet, block_count, neighbour, coriolis, tide
 ):
-    slots, cells = wet.shape
     slices = lax.axis_size("tm")
-    loaded = [depth_level, depth_table, wet, neighbour.T, start_states, tide, coriolis]
-    state, still, begin, face, pe, pw = call(
+    loaded = [depth_level, depth_table, wet, start_states, tide, coriolis]
+    faces = neighbour.T
+    whole, half = shape(3, ROWS, BS, LANES), shape(3, ROWS, BS // 2, LANES)
+    *held, face, pe, pw = call(
         functools.partial(before_kernel, slices),
-        [shape(3, ROWS, BS, LANES), shape(5, ROWS, BS, LANES), shape(3, slots, cells)]
+        [jax.ShapeDtypeStruct(x.shape, x.dtype) for x in loaded]
         + [jax.ShapeDtypeStruct((4, SUB, LANES), jnp.int32)]
         + [shape(ROWS, len(NAMES) * OUT, LANES)] * 2,
-        [block_count] + [pltpu.with_memory_space_constraint(x, pltpu.HBM) for x in loaded],
-        spaces=[pltpu.SMEM] + [pltpu.HBM] * len(loaded),
-        scratch=[pltpu.VMEM(x.shape, x.dtype) for x in loaded]
-        + [pltpu.SemaphoreType.DMA((len(loaded),))],
+        [block_count] + in_hbm(loaded[:3] + [faces] + loaded[3:]),
+        spaces=[pltpu.SMEM] + [pltpu.HBM] * (len(loaded) + 1),
+        scratch=[
+            pltpu.VMEM(faces.shape, faces.dtype),
+            pltpu.VMEM(half.shape, F32),
+            pltpu.VMEM((5,) + half.shape[1:], F32),
+            pltpu.SemaphoreType.DMA((len(loaded) + 1,)),
+        ],
     )
     from_west = passed_along(pe, "space", 1)
     from_east = passed_along(pw, "space", -1)
-    last = call(
+    last, still, inner, inner_gain, edge_gain, edge_base = call(
         functools.partial(during_kernel, slices),
-        shape(3, ROWS, BS, LANES),
-        [state, still, face],
-    )
-    defect = call(
+        [whole, shape(5, ROWS, BS, LANES)] + [half] * 4,
+        held + [face, block_count] + in_hbm([coarse_gain]),
+        spaces=[pltpu.VMEM] * (len(held) + 1) + [pltpu.SMEM, pltpu.HBM],
+        scratch=[pltpu.VMEM(coarse_gain.shape, F32), pltpu.SemaphoreType.DMA((1,))],
+    )
+    inner_sum = periodic_sum(inner, inner_gain, slices)
+    edge = call(
         functools.partial(after_kernel, slices),
-        shape(3, slots, cells),
-        [from_west, from_east, last, still, face, begin, coarse_gain],
+        half,
+        [from_west, from_east, last, still, face, edge_base],
         scratch=[pltpu.VMEM((len(NAMES), ROWS, 2, SUB, LANES), F32)],
     )
-    total, power = passed_along(defect, "tm", 1), coarse_gain
-    for _ in range(slices - 2):
-        total = passed_along(defect + coarse_gain * total, "tm", 1)
-        power = power * coarse_gain
-    total = total + power * defect
-    return (total / (1.0 - power * coarse_gain))[None]
+    edge_sum = periodic_sum(edge, edge_gain, slices)
+    return call(
+        functools.partial(final_kernel, slices),
+        shape(*start_states.shape),
+        [edge_sum, edge, edge_gain, inner_sum, inner, inner_gain],
+        out_space=pltpu.HBM,
+        scratch=[pltpu.VMEM(start_states.shape, F32), pltpu.SemaphoreType.DMA((3,))],
+    )
 
 
 def solution(mesh):

time: 16.8 us -> 16.4 us (0.976)
  Pallas kernels: 3.98 us -> 6.02 us
  waiting for transfers between devices: 4.05 us -> 2.32 us
  other arithmetic: 0.85 us -> 0 us
    pallas_call x3 -> x4, Pallas kernels: 3.98 us -> 6.02 us  [call(): pl.pallas_call(kernel, out_shape=out_shape, in_specs=[pl.BlockSpec(memory...]
    ppermute x3 -> x4, waiting for transfers between devices: 4.05 us -> 2.32 us  [passed_along(): lax.ppermute(shard, axis, [(i, (i + by) % size) for i in range(size)])]
    broadcast_in_dim x1 -> x0, other arithmetic: 0.85 us -> none  [body(): return (total / (1.0 - power * coarse_gain))[None]]
    ppermute x3 -> x4, starting transfers between devices: 7.12 us -> 7.19 us  [passed_along(): lax.ppermute(shard, axis, [(i, (i + by) % size) for i in range(size)])]
  transfers between devices with their start and end apart: 3 -> 4, of which waited for: 2 -> 2; matrix products, arithmetic and copies ran while one was open for 0% -> 0% of each run, Pallas kernels for 3% -> 19%
where the time goes in v4:
time: 16.4 us; the launch traced here: 16.2 us
  starting transfers between devices  7.19 us (44%)
  Pallas kernels  6.02 us (37%)
  waiting for transfers between devices  2.32 us (14%)
  between operations  0.7 us (4%)
    ppermute x4, starting transfers between devices, passed_along(): lax.ppermute(shard, axis, [(i, (i + by) % size) for i in range(size)])  7.19 us
    pallas_call x4, Pallas kernels, call(): pl.pallas_call(kernel, out_shape=out_shape, in_specs=[pl.BlockSpec(memory...  6.02 us
    ppermute x4, waiting for transfers between devices, passed_along(): lax.ppermute(shard, axis, [(i, (i + by) % size) for i in range(size)])  2.32 us
  transfers between devices with their start and end apart: 4, of which 2 were waited for; matrix products, arithmetic and copies ran while one was open for 0% of the time, Pallas kernels for 19%

profile of v4, /device:TPU:0, one launch (start us, length us, event | category | flops | bytes accessed | tf_op | source)
XLA Modules:
  0.0 16.2 jit_solution(4442513824469336373)
XLA Ops:
  0.7 2.1 %shard_map.91 = (s32[8,4096]{1,0:T(8,128)S(1)}, f32[64]{0:T(128)S(1)}, s32[8,4096]{1,0:T(8,128)S(1)}, f32[1,3,8,4096]{3,2,1,0:T(8,128)S(1)}, f32[2,8,4096]{2,1,0...) custom-call(s32[1]{0:T(128)S(6)} %copy.10.count_ref, ...), custom_call_target="tpu_custom_call" | custom-call | bytes 2097928 | tf_op jit(solution)/shard_map/pallas_call | solution.py:493
  2.8 3.0 %collective-permute-start = (f32[4,48,128]{2,1,0:T(8,128)S(1)}, f32[4,48,128]{2,1,0:T(8,128)S(1)}, u32[]{:S(2)}, u32[]{:S(2)}) collective-permute-start(f32[4,48,128]{2,1,0:T(8,128)S(1)} %get-tuple-element.20), channel_id=1, source_target_pairs={{0,1},{1,2},{2,3},{3,4},{4,5},{5,6},{6,7},{7,8},{8,9},{9,10},{10,1... | collective-permute-start | bytes 294920 | tf_op jit(solution)/shard_map/ppermute | solution.py:514
  5.8 4.1 %collective-permute-start.1 = (f32[4,48,128]{2,1,0:T(8,128)S(1)}, f32[4,48,128]{2,1,0:T(8,128)S(1)}, u32[]{:S(2)}, u32[]{:S(2)}) collective-permute-start(f32[4,48,128]{2,1,0:T(8,128)S(1)} %get-tuple-element.21), channel_id=1, source_target_pairs={{0,15},{1,0},{2,1},{3,2},{4,3},{5,4},{6,5},{7,6},{8,7},{9,8},{10,9... | collective-permute-start | bytes 294920 | tf_op jit(solution)/shard_map/ppermute | solution.py:514
  9.9 1.9 %shard_map.92 = (f32[3,4,64,128]{3,2,1,0:T(8,128)S(1)}, f32[5,4,64,128]{3,2,1,0:T(8,128)S(1)}, f32[3,4,32,128]{3,2,1,0:T(8,128)S(1)}, f32[3,4,32,128]{3,2,1,0:T(...) custom-call(s32[8,4096]{1,0:T(8,128)S(1)} %get-tuple-element.22.level_id, ...), custom_call_target="tpu_custom_call" | custom-call | bytes 2916872 | tf_op jit(solution)/shard_map/pallas_call | solution.py:493
  11.7 0.1 collective-permute-start.3
  11.8 0.9 %collective-permute-done.pe = f32[4,48,128]{2,1,0:T(8,128)S(1)} collective-permute-done((f32[4,48,128]{2,1,0:T(8,128)S(1)}, f32[4,48,128]{2,1,0:T(8,128)S(1)}, u32[]{:S(2)}, u32[]{:S(2)}) %collective-permute-start) | collective-permute-done | bytes 98336 | tf_op jit(solution)/shard_map/ppermute | solution.py:514
  12.7 0.0 collective-permute-done.1.pw
  12.7 1.1 %shard_map.93.edge = f32[3,4,32,128]{3,2,1,0:T(8,128)S(1)} custom-call(f32[4,48,128]{2,1,0:T(8,128)S(1)} %collective-permute-done.pe, f32[4,48,128]{2,1,0:T(8,128)S(1)} %collective-permute-done.1.pw, f32[3,4,64,128]{3,2,1,0:T(8,128)S(1)} %get-tuple-element.29.last, f32[5,4,64,128]{3,2,1,0:T(8,128)S(1)} %get-tuple-element.30.still, ...), custom_call_target="tpu_custom_call" | custom-call | bytes 2916352 | tf_op jit(solution)/shard_map/pallas_call | solution.py:493
  13.8 0.1 collective-permute-start.2
  13.9 0.0 collective-permute-done.3.inner_sum
  13.9 1.4 %collective-permute-done.2.edge_sum = f32[3,4,32,128]{3,2,1,0:T(8,128)S(1)} collective-permute-done((f32[3,4,32,128]{3,2,1,0:T(8,128)S(1)}, f32[3,4,32,128]{3,2,1,0:T(8,128)S(1)}, u32[]{:S(2)}, u32[]{:S(2)}) %collective-permute-start.2) | collective-permute-done | bytes 196640 | tf_op jit(solution)/shard_map/ppermute | solution.py:514
  15.4 0.9 %shard_map.94 = f32[1,3,8,4096]{3,2,1,0:T(8,128)} custom-call(f32[3,4,32,128]{3,2,1,0:T(8,128)S(1)} %collective-permute-done.2.edge_sum, f32[3,4,32,128]{3,2,1,0:T(8,128)S(1)} %shard_map.93.edge, f32[3,4,32,128]{3,2,1,0:T(8,128)S(1)} %get-tuple-element.32.edge_gain, f32[3,4,32,128]{3,2,1,0:T(8,128)S(1)} %collective-permute-done.3.inner_sum, ...), custom_call_target="tpu_custom_call" | custom-call | bytes 2359296 | tf_op jit(solution)/shard_map/pallas_call | solution.py:493
Async XLA Ops:
  2.8 9.9 %collective-permute-start = (f32[4,48,128]{2,1,0:T(8,128)S(1)}, f32[4,48,128]{2,1,0:T(8,128)S(1)}, u32[]{:S(2)}, u32[]{:S(2)}) collective-permute-start(f32[4,48,128]{2,1,0:T(8,128)S(1)} %get-tuple-element.20), channel_id=1, source_target_pairs={{0,1},{1,2},{2,3},{3,4},{4,5},{5,6},{6,7},{7,8},{8,9},{9,10},{10,1... | collective-permute-start | bytes 294920 | tf_op jit(solution)/shard_map/ppermute | solution.py:514
  5.8 6.9 %collective-permute-start.1 = (f32[4,48,128]{2,1,0:T(8,128)S(1)}, f32[4,48,128]{2,1,0:T(8,128)S(1)}, u32[]{:S(2)}, u32[]{:S(2)}) collective-permute-start(f32[4,48,128]{2,1,0:T(8,128)S(1)} %get-tuple-element.21), channel_id=1, source_target_pairs={{0,15},{1,0},{2,1},{3,2},{4,3},{5,4},{6,5},{7,6},{8,7},{9,8},{10,9... | collective-permute-start | bytes 294920 | tf_op jit(solution)/shard_map/ppermute | solution.py:514
  11.7 2.2 %collective-permute-start.3 = (f32[3,4,32,128]{3,2,1,0:T(8,128)S(1)}, f32[3,4,32,128]{3,2,1,0:T(8,128)S(1)}, u32[]{:S(2)}, u32[]{:S(2)}) collective-permute-start(f32[3,4,32,128]{3,2,1,0:T(8,128)S(1)} %get-tuple-element.33.inner), channel_id=1, source_target_pairs={{0,16},{16,0},{1,17},{17,1},{2,18},{18,2},{3,19},{19,3},{4,20},{20... | collective-permute-start | bytes 589832 | tf_op jit(solution)/shard_map/ppermute | solution.py:514
  13.8 1.5 %collective-permute-start.2 = (f32[3,4,32,128]{3,2,1,0:T(8,128)S(1)}, f32[3,4,32,128]{3,2,1,0:T(8,128)S(1)}, u32[]{:S(2)}, u32[]{:S(2)}) collective-permute-start(f32[3,4,32,128]{3,2,1,0:T(8,128)S(1)} %shard_map.93.edge), channel_id=1, source_target_pairs={{0,16},{16,0},{1,17},{17,1},{2,18},{18,2},{3,19},{19,3},{4,20},{20... | collective-permute-start | bytes 589832 | tf_op jit(solution)/shard_map/ppermute | solution.py:514

commit v5 on v4

--- a/solution.py
+++ b/solution.py
@@ -128,7 +128,7 @@
     }
 
 
-def interior_steps(s, runs, slices, steps, ghosts, wide):
+def interior_steps(s, runs, times, steps, ghosts, wide):
     sub = tile_iota(0)
     place = {q: SUB * n for n, q in enumerate(q for run in runs for q in run)}
 
@@ -159,7 +159,7 @@
         live_over[q] = lanes_of(live[0], up) * up_on
         live_under[q] = lanes_of(live[3], down) * down_on
     for step in steps:
-        ca, sa = phase(slices, step)
+        ca, sa = times[2 * step], times[2 * step + 1]
         slope = x_slopes(lambda q: product(tiles("depth", q), tiles("east", q)), runs)
         dys = {}
         for q, dx in slope:
@@ -199,9 +199,9 @@
     return loads
 
 
-def prepare(state, still, groups, level_id, table, wet, start, tide, cor, count_ref, wait):
+def prepare(state, still, groups, row, held, level_id, wet, start, tide, cor):
     tiles = wet.shape[1] // LANES
-    held = tile_iota(0) < count_ref[0]
+    held = held[...] > 0
 
     def turn(source, put):
         for i, columns in enumerate(to_columns([source(v) for v in range(tiles)])):
@@ -214,11 +214,8 @@
 
         turn(source, put)
 
-    wait(0)
-    levels = table.shape[0]
-    row = F32(0.15) * table[...].reshape(1, levels)
-    row = jnp.concatenate([row, jnp.zeros((1, LANES - levels), F32)], axis=1)
-    row = jnp.broadcast_to(row, (SUB, LANES))
+    levels = LANES - 1
+    row = row[...]
 
     def coded(v):
         here = jnp.logical_and(lane_tile(wet, v) > 0, held)
@@ -229,7 +226,6 @@
         still[1, at[0], at[1], :] = (code < levels).astype(F32)
 
     turn(coded, store_depth)
-    wait(1)
 
     def store_state(f):
         def put(at, x):
@@ -239,37 +235,39 @@
 
     for f in range(3):
         turn(lambda v, f=f: lane_tile(start, v, (0, f)), store_state(f))
-    wait(2)
     for f in range(2):
         store(still, 3 + f, lambda v, f=f: lane_tile(tide, v, (f,)))
-    wait(3)
     store(still, 2, lambda v: F32(0.3) * lane_tile(cor, v))
 
 
+def clock_kernel(slices, times):
+    for step in range(STEPS):
+        for j, x in enumerate(phase(slices, step)):
+            times[2 * step + j] = jnp.full((SUB, LANES), x, F32)
+
+
+def depths_kernel(table, row):
+    levels = table.shape[0]
+    depths = F32(0.15) * table[...].reshape(1, levels)
+    depths = jnp.concatenate([depths, jnp.zeros((1, LANES - levels), F32)], axis=1)
+    row[...] = jnp.broadcast_to(depths, (SUB, LANES))
+
+
+def slots_kernel(count_ref, nb, face, held):
+    for j, x in enumerate(face_rows(nb[...])):
+        face[j] = x
+    held[...] = (tile_iota(0) < count_ref[0]).astype(jnp.int32)
+
+
 def before_kernel(
-    slices, count_ref, level_h, table_h, wet_h, nb_h, start_h, tide_h, cor_h,
-    level_id, table, wet, start, tide, cor, face, pe, pw,
-    nb_ref, state, still, sems,
+    times, face, held, row, level_id, wet, start, tide, cor, pe, pw, state, still
 ):
-    loads = started(
-        [
-            (level_h, level_id), (table_h, table), (wet_h, wet), (nb_h, nb_ref),
-            (start_h, start), (tide_h, tide), (cor_h, cor),
-        ],
-        sems,
-    )
-
-    def wait(n):
-        for load in (loads[:4], loads[4:5], loads[5:6], loads[6:])[n]:
-            load.wait()
-
-    prepare(state, still, PARTS[0], level_id, table, wet, start, tide, cor, count_ref, wait)
-    rows = face_rows(nb_ref[...])
-    for j in range(4):
-        face[j] = rows[j]
+
+    prepare(state, still, PARTS[0], row, held, level_id, wet, start, tide, cor)
+    rows = [face[j] for j in range(4)]
     s = fields_of(state, still)
     runs = (PARTS[0][:2], PARTS[0][2:])
-    interior_steps(s, runs, slices, range(SENT), chunk_ghosts(rows[0], rows[1]), True)
+    interior_steps(s, runs, times, range(SENT), chunk_ghosts(rows[0], rows[1]), True)
 
     end = SUB * len(PARTS[0])
     for f, name in enumerate(NAMES):
@@ -294,16 +292,16 @@
 
 
 def during_kernel(
-    slices, level_id, table, wet, start, tide, cor, face, count_ref, gain_h,
+    times, face, held, row, level_id, wet, start, tide, cor, gain_h,
     last, still, inner, inner_gain, edge_gain, edge_base,
     gain, sems,
 ):
     loads = started([(gain_h, gain)], sems)
     tiles = wet.shape[1] // LANES
-    prepare(last, still, ALL, level_id, table, wet, start, tide, cor, count_ref, lambda n: None)
+    prepare(last, still, ALL, row, held, level_id, wet, start, tide, cor)
     ghosts = chunk_ghosts(face[0], face[1])
-    interior_steps(fields_of(last, still), (ALL,), slices, range(STEPS), ghosts, False)
-    held = (tile_iota(0) < count_ref[0]).astype(F32)
+    interior_steps(fields_of(last, still), (ALL,), times, range(STEPS), ghosts, False)
+    held = held[...].astype(F32)
     for load in loads:
         load.wait()
     for f in range(3):
@@ -322,7 +320,7 @@
                 inner[f, i, to, :] = last[f, i, pl.ds(SUB * PARTS[1][n], SUB), :] - base[i][at[1]]
 
 
-def after_kernel(slices, pe, pw, last, still, face, base, edge, joined):
+def after_kernel(times, pe, pw, last, still, face, base, edge, joined):
     sub, lane = tile_iota(0), tile_iota(1)
     s = fields_of(last, still)
 
@@ -414,7 +412,7 @@
         return [x * y for x, y in zip(a, b)]
 
     for k in range(1, HALF + 1):
-        ca, sa = phase(slices, (k - 1) // 2)
+        ca, sa = times[(k - 1) // 2 * 2], times[(k - 1) // 2 * 2 + 1]
         active = [g for g in range(3) if changed(0, g, k) is not False]
         reach = min(3, len(active) + 1)
         for side in range(2):
@@ -487,16 +485,16 @@
         copy.wait()
 
 
-def call(kernel, out_shape, operands, spaces=None, out_space=pltpu.VMEM, scratch=()):
+def call(kernel, out_shape, operands, spaces=None, out_space=pltpu.VMEM, scratch=(), flops=0):
     spaces = spaces or [pltpu.VMEM] * len(operands)
-    size = sum(4 * x.size for x in operands)
+    size = 2 * sum(4 * x.size for x in operands)
     return pl.pallas_call(
         kernel,
         out_shape=out_shape,
         in_specs=[pl.BlockSpec(memory_space=space) for space in spaces],
         out_specs=jax.tree.map(lambda _: pl.BlockSpec(memory_space=out_space), out_shape),
         scratch_shapes=scratch,
-        cost_estimate=pl.CostEstimate(flops=0, bytes_accessed=2 * size, transcendentals=0),
+        cost_estimate=pl.CostEstimate(flops=flops, bytes_accessed=size, transcendentals=0),
         compiler_params=pltpu.CompilerParams(vmem_limit_bytes=VMEM_LIMIT),
     )(*operands)
 
@@ -525,37 +523,39 @@
     start_states, coarse_gain, depth_level, depth_table, wet, block_count, neighbour, coriolis, tide
 ):
     slices = lax.axis_size("tm")
-    loaded = [depth_level, depth_table, wet, start_states, tide, coriolis]
-    faces = neighbour.T
     whole, half = shape(3, ROWS, BS, LANES), shape(3, ROWS, BS // 2, LANES)
-    *held, face, pe, pw = call(
-        functools.partial(before_kernel, slices),
-        [jax.ShapeDtypeStruct(x.shape, x.dtype) for x in loaded]
-        + [jax.ShapeDtypeStruct((4, SUB, LANES), jnp.int32)]
-        + [shape(ROWS, len(NAMES) * OUT, LANES)] * 2,
-        [block_count] + in_hbm(loaded[:3] + [faces] + loaded[3:]),
-        spaces=[pltpu.SMEM] + [pltpu.HBM] * (len(loaded) + 1),
-        scratch=[
-            pltpu.VMEM(faces.shape, faces.dtype),
-            pltpu.VMEM(half.shape, F32),
-            pltpu.VMEM((5,) + half.shape[1:], F32),
-            pltpu.SemaphoreType.DMA((len(loaded) + 1,)),
-        ],
+    times = call(
+        functools.partial(clock_kernel, slices), shape(2 * STEPS, SUB, LANES), [], flops=10**10
+    )
+    flags = jax.ShapeDtypeStruct((SUB, LANES), jnp.int32)
+    row = call(depths_kernel, shape(SUB, LANES), [depth_table])
+    slot_tiles = call(
+        slots_kernel,
+        [jax.ShapeDtypeStruct((4, SUB, LANES), jnp.int32), flags],
+        [block_count, neighbour.T],
+        spaces=[pltpu.SMEM, pltpu.VMEM],
+    )
+    ready = [times] + list(slot_tiles) + [row, depth_level, wet, start_states, tide, coriolis]
+    pe, pw = call(
+        before_kernel,
+        [shape(ROWS, len(NAMES) * OUT, LANES)] * 2,
+        ready,
+        scratch=[pltpu.VMEM(half.shape, F32), pltpu.VMEM((5,) + half.shape[1:], F32)],
     )
     from_west = passed_along(pe, "space", 1)
     from_east = passed_along(pw, "space", -1)
     last, still, inner, inner_gain, edge_gain, edge_base = call(
-        functools.partial(during_kernel, slices),
+        during_kernel,
         [whole, shape(5, ROWS, BS, LANES)] + [half] * 4,
-        held + [face, block_count] + in_hbm([coarse_gain]),
-        spaces=[pltpu.VMEM] * (len(held) + 1) + [pltpu.SMEM, pltpu.HBM],
+        ready + in_hbm([coarse_gain]),
+        spaces=[pltpu.VMEM] * len(ready) + [pltpu.HBM],
         scratch=[pltpu.VMEM(coarse_gain.shape, F32), pltpu.SemaphoreType.DMA((1,))],
     )
     inner_sum = periodic_sum(inner, inner_gain, slices)
     edge = call(
-        functools.partial(after_kernel, slices),
+        after_kernel,
         half,
-        [from_west, from_east, last, still, face, edge_base],
+        [times, from_west, from_east, last, still, slot_tiles[0], edge_base],
         scratch=[pltpu.VMEM((len(NAMES), ROWS, 2, SUB, LANES), F32)],
     )
     edge_sum = periodic_sum(edge, edge_gain, slices)

time: 16.4 us -> 15.7 us (0.957)
  Pallas kernels: 6.02 us -> 4.84 us
  local copies, waits for them, and re-layouts: 0 us -> 0.38 us
    pallas_call x4 -> x7, Pallas kernels: 6.02 us -> 4.84 us  [call(): pl.pallas_call(kernel, out_shape=out_shape, in_specs=[pl.BlockSpec(memory...]
    unnamed x0 -> x14, local copies, waits for them, and re-layouts: none -> 0.38 us
where the time goes in v5:
time: 15.7 us; the launch traced here: 15.6 us
  starting transfers between devices  7.19 us (46%)
  Pallas kernels  4.84 us (31%)
  waiting for transfers between devices  2.33 us (15%)
  between operations  0.84 us (5%)
  local copies, waits for them, and re-layouts  0.38 us (2%)
    ppermute x4, starting transfers between devices, passed_along(): lax.ppermute(shard, axis, [(i, (i + by) % size) for i in range(size)])  7.19 us
    pallas_call x7, Pallas kernels, call(): pl.pallas_call(kernel, out_shape=out_shape, in_specs=[pl.BlockSpec(memory...  4.84 us
    ppermute x4, waiting for transfers between devices, passed_along(): lax.ppermute(shard, axis, [(i, (i + by) % size) for i in range(size)])  2.33 us
    unnamed x14, local copies, waits for them, and re-layouts  0.38 us
  transfers between devices with their start and end apart: 4, of which 2 were waited for; matrix products, arithmetic and copies ran while one was open for 0% of the time, Pallas kernels for 19%

profile of v5, /device:TPU:0, one launch (start us, length us, event | category | flops | bytes accessed | tf_op | source)
XLA Modules:
  0.0 15.6 jit_solution(4346306463237492638)
XLA Ops:
  0.0 0.0 copy-start.1
  0.0 0.0 copy-start.4
  0.0 0.0 copy-start.3
  0.0 0.0 copy-start.2
  0.0 0.0 copy-start
  0.0 0.0 copy-start.5
  0.1 0.0 copy-start.6
  0.8 0.0 copy-done.6
  0.8 0.0 copy-done.5
  0.8 0.1 shard_map.92
  0.9 0.0 copy-done.1
  1.0 0.1 copy-done.4
  1.0 0.1 copy-done.3
  1.1 0.1 copy-done.2
  1.2 0.1 copy-done
  1.3 0.9 %shard_map.94 = (f32[4,48,128]{2,1,0:T(8,128)S(1)}, f32[4,48,128]{2,1,0:T(8,128)S(1)}) custom-call(f32[12,8,128]{2,1,0:T(8,128)S(1)} %shard_map.91.times, s32[4,8,128]{2,1,0:T(8,128)S(1)} %get-tuple-element.15.face, s32[8,128]{1,0:T(8,128)S(1)} %get-tuple-element.16.held, f32[8,128]{1,0:T(8,128)S(1)} %shard_map.93.row, s32[8,4096]{1,0:T(8,128)S(1)} %copy-done.2, ...), custom_call_target="tpu_custom_call" | custom-call | bytes 2244608 | tf_op jit(solution)/shard_map/pallas_call | solution.py:491
  2.1 3.0 %collective-permute-start = (f32[4,48,128]{2,1,0:T(8,128)S(1)}, f32[4,48,128]{2,1,0:T(8,128)S(1)}, u32[]{:S(2)}, u32[]{:S(2)}) collective-permute-start(f32[4,48,128]{2,1,0:T(8,128)S(1)} %get-tuple-element.17), channel_id=1, source_target_pairs={{0,1},{1,2},{2,3},{3,4},{4,5},{5,6},{6,7},{7,8},{8,9},{9,10},{10,1... | collective-permute-start | bytes 294920 | tf_op jit(solution)/shard_map/ppermute | solution.py:512
  5.1 4.1 %collective-permute-start.1 = (f32[4,48,128]{2,1,0:T(8,128)S(1)}, f32[4,48,128]{2,1,0:T(8,128)S(1)}, u32[]{:S(2)}, u32[]{:S(2)}) collective-permute-start(f32[4,48,128]{2,1,0:T(8,128)S(1)} %get-tuple-element.18), channel_id=1, source_target_pairs={{0,15},{1,0},{2,1},{3,2},{4,3},{5,4},{6,5},{7,6},{8,7},{9,8},{10,9... | collective-permute-start | bytes 294920 | tf_op jit(solution)/shard_map/ppermute | solution.py:512
  9.2 1.8 %shard_map.95 = (f32[3,4,64,128]{3,2,1,0:T(8,128)S(1)}, f32[5,4,64,128]{3,2,1,0:T(8,128)S(1)}, f32[3,4,32,128]{3,2,1,0:T(8,128)S(1)}, f32[3,4,32,128]{3,2,1,0:T(...) custom-call(f32[12,8,128]{2,1,0:T(8,128)S(1)} %shard_map.91.times, ...), custom_call_target="tpu_custom_call" | custom-call | bytes 3031040 | tf_op jit(solution)/shard_map/pallas_call | solution.py:491
  11.0 0.1 collective-permute-start.3
  11.1 0.9 %collective-permute-done.pe = f32[4,48,128]{2,1,0:T(8,128)S(1)} collective-permute-done((f32[4,48,128]{2,1,0:T(8,128)S(1)}, f32[4,48,128]{2,1,0:T(8,128)S(1)}, u32[]{:S(2)}, u32[]{:S(2)}) %collective-permute-start) | collective-permute-done | bytes 98336 | tf_op jit(solution)/shard_map/ppermute | solution.py:512
  12.0 0.0 collective-permute-done.1.pw
  12.0 1.2 %shard_map.96.edge = f32[3,4,32,128]{3,2,1,0:T(8,128)S(1)} custom-call(f32[12,8,128]{2,1,0:T(8,128)S(1)} %shard_map.91.times, f32[4,48,128]{2,1,0:T(8,128)S(1)} %collective-permute-done.pe, f32[4,48,128]{2,1,0:T(8,128)S(1)} %collective-permute-done.1.pw, f32[3,4,64,128]{3,2,1,0:T(8,128)S(1)} %get-tuple-element.19.last, ...), custom_call_target="tpu_custom_call" | custom-call | bytes 3014656 | tf_op jit(solution)/shard_map/pallas_call | solution.py:491
  13.2 0.1 collective-permute-start.2
  13.3 0.0 collective-permute-done.3.inner_sum
  13.3 1.4 %collective-permute-done.2.edge_sum = f32[3,4,32,128]{3,2,1,0:T(8,128)S(1)} collective-permute-done((f32[3,4,32,128]{3,2,1,0:T(8,128)S(1)}, f32[3,4,32,128]{3,2,1,0:T(8,128)S(1)}, u32[]{:S(2)}, u32[]{:S(2)}) %collective-permute-start.2) | collective-permute-done | bytes 196640 | tf_op jit(solution)/shard_map/ppermute | solution.py:512
  14.7 0.9 %shard_map.97 = f32[1,3,8,4096]{3,2,1,0:T(8,128)} custom-call(f32[3,4,32,128]{3,2,1,0:T(8,128)S(1)} %collective-permute-done.2.edge_sum, f32[3,4,32,128]{3,2,1,0:T(8,128)S(1)} %shard_map.96.edge, f32[3,4,32,128]{3,2,1,0:T(8,128)S(1)} %get-tuple-element.22.edge_gain, f32[3,4,32,128]{3,2,1,0:T(8,128)S(1)} %collective-permute-done.3.inner_sum, ...), custom_call_target="tpu_custom_call" | custom-call | bytes 2359296 | tf_op jit(solution)/shard_map/pallas_call | solution.py:491
  (2 shorter events, 0.0 us)
Async XLA Ops:
  0.0 0.9 %copy-start.1 = (f32[2,8,4096]{2,1,0:T(8,128)S(1)}, f32[2,8,4096]{2,1,0:T(8,128)}, u32[]{:S(2)}) copy-start(f32[2,8,4096]{2,1,0:T(8,128)} %tide.3) | copy-start | bytes 786436
  0.0 1.0 %copy-start.4 = (f32[8,4096]{1,0:T(8,128)S(1)}, f32[8,4096]{1,0:T(8,128)}, u32[]{:S(2)}) copy-start(f32[8,4096]{1,0:T(8,128)} %cor.3) | copy-start | bytes 393220
  0.0 1.1 %copy-start.3 = (s32[8,4096]{1,0:T(8,128)S(1)}, s32[8,4096]{1,0:T(8,128)}, u32[]{:S(2)}) copy-start(s32[8,4096]{1,0:T(8,128)} %wet.3) | copy-start | bytes 393220
  0.0 1.1 %copy-start.2 = (s32[8,4096]{1,0:T(8,128)S(1)}, s32[8,4096]{1,0:T(8,128)}, u32[]{:S(2)}) copy-start(s32[8,4096]{1,0:T(8,128)} %level_id.3) | copy-start | bytes 393220
  0.0 1.3 %copy-start = (f32[1,3,8,4096]{3,2,1,0:T(8,128)S(1)}, f32[1,3,8,4096]{3,2,1,0:T(8,128)}, u32[]{:S(2)}) copy-start(f32[1,3,8,4096]{3,2,1,0:T(8,128)} %start.3) | copy-start | bytes 1179652
  0.0 0.8 %copy-start.5 = (s32[8,4]{0,1:T(4,128)S(1)}, s32[8,4]{0,1:T(4,128)}, u32[]{:S(2)}) copy-start(s32[8,4]{0,1:T(4,128)} %param.15) | copy-start | bytes 388
  0.1 0.8 %copy-start.6 = (f32[64]{0:T(128)S(1)}, f32[64]{0:T(128)}, u32[]{:S(2)}) copy-start(f32[64]{0:T(128)} %table.1) | copy-start | bytes 772
  2.1 9.9 %collective-permute-start = (f32[4,48,128]{2,1,0:T(8,128)S(1)}, f32[4,48,128]{2,1,0:T(8,128)S(1)}, u32[]{:S(2)}, u32[]{:S(2)}) collective-permute-start(f32[4,48,128]{2,1,0:T(8,128)S(1)} %get-tuple-element.17), channel_id=1, source_target_pairs={{0,1},{1,2},{2,3},{3,4},{4,5},{5,6},{6,7},{7,8},{8,9},{9,10},{10,1... | collective-permute-start | bytes 294920 | tf_op jit(solution)/shard_map/ppermute | solution.py:512
  5.1 6.9 %collective-permute-start.1 = (f32[4,48,128]{2,1,0:T(8,128)S(1)}, f32[4,48,128]{2,1,0:T(8,128)S(1)}, u32[]{:S(2)}, u32[]{:S(2)}) collective-permute-start(f32[4,48,128]{2,1,0:T(8,128)S(1)} %get-tuple-element.18), channel_id=1, source_target_pairs={{0,15},{1,0},{2,1},{3,2},{4,3},{5,4},{6,5},{7,6},{8,7},{9,8},{10,9... | collective-permute-start | bytes 294920 | tf_op jit(solution)/shard_map/ppermute | solution.py:512
  11.0 2.2 %collective-permute-start.3 = (f32[3,4,32,128]{3,2,1,0:T(8,128)S(1)}, f32[3,4,32,128]{3,2,1,0:T(8,128)S(1)}, u32[]{:S(2)}, u32[]{:S(2)}) collective-permute-start(f32[3,4,32,128]{3,2,1,0:T(8,128)S(1)} %get-tuple-element.23.inner), channel_id=1, source_target_pairs={{0,16},{16,0},{1,17},{17,1},{2,18},{18,2},{3,19},{19,3},{4,20},{20... | collective-permute-start | bytes 589832 | tf_op jit(solution)/shard_map/ppermute | solution.py:512
  13.2 1.5 %collective-permute-start.2 = (f32[3,4,32,128]{3,2,1,0:T(8,128)S(1)}, f32[3,4,32,128]{3,2,1,0:T(8,128)S(1)}, u32[]{:S(2)}, u32[]{:S(2)}) collective-permute-start(f32[3,4,32,128]{3,2,1,0:T(8,128)S(1)} %shard_map.96.edge), channel_id=1, source_target_pairs={{0,16},{16,0},{1,17},{17,1},{2,18},{18,2},{3,19},{19,3},{4,20},{20... | collective-permute-start | bytes 589832 | tf_op jit(solution)/shard_map/ppermute | solution.py:512

commit v6 on v5

--- a/solution.py
+++ b/solution.py
@@ -122,10 +122,9 @@
 NAMES = ("level", "east", "north", "depth", "live", "cor", "tide0", "tide1")
 
 
-def fields_of(state, still):
-    return {
-        name: (state, f) if f < 3 else (still, f - 3) for f, name in enumerate(NAMES)
-    }
+def fields_of(state, land, rest):
+    refs = [(state, 0), (state, 1), (state, 2), (land, 0), (land, 1)]
+    return dict(zip(NAMES, refs + [(rest, f) for f in range(3)]))
 
 
 def interior_steps(s, runs, times, steps, ghosts, wide):
@@ -149,6 +148,9 @@
 
     def product(a, b):
         return [x * y for x, y in zip(a, b)]
+
+    def unneeded(q, k):
+        return wide and min(SUB * q, BS - SUB - SUB * q) > OUT + 2 * SENT - k
 
     up, up_on, down, down_on = ghosts
     if wide:
@@ -163,6 +165,8 @@
         slope = x_slopes(lambda q: product(tiles("depth", q), tiles("east", q)), runs)
         dys = {}
         for q, dx in slope:
+            if unneeded(q, 2 * step + 1):
+                continue
             old = tiles("level", q)
             t0, t1, live = tiles("tide0", q), tiles("tide1", q), tiles("live", q)
             part = [old[i] + (t0[i] * ca + t1[i] * sa) - dx[i] for i in range(ROWS)]
@@ -181,6 +185,8 @@
             dys[q] = [new[1] - under, new[2] - new[0], new[3] - new[1], over - new[2]]
         slope = x_slopes(lambda q: tiles("level", q), runs)
         for q, dx in slope:
+            if unneeded(q, 2 * step + 2):
+                continue
             u, w, cor, live = (tiles(n, q) for n in ("east", "north", "cor", "live"))
             dy = dys[q] if wide else y_slopes(tiles("level", q), ghosts)
             new = [new_velocity(u[i], w[i], cor[i], dx[i], dy[i], live[i]) for i in range(ROWS)]
@@ -188,8 +194,22 @@
             put("north", q, 2 * step + 2, [b for _, b in new], w)
 
 
-PARTS = ((0, 1, GROUPS - 2, GROUPS - 1), tuple(range(2, GROUPS - 2)))
 ALL = tuple(range(GROUPS))
+SIDES = (ALL[:2], ALL[-2:])
+NEAR = SIDES[0] + SIDES[1]
+EDGE, INNER = 2 * HALF, BS - 2 * HALF
+
+
+def parted(q):
+    low = tile_iota(0) < HALF - SUB
+    edge = [q[0], jnp.where(low, q[1], q[-2]), q[-1]]
+    return edge, list(q[2:-2]) + [jnp.where(low, q[-2], q[1])]
+
+
+def joint(edge, inner):
+    low = tile_iota(0) < HALF - SUB
+    second, last_but_one = jnp.where(low, edge[1], inner[-1]), jnp.where(low, inner[-1], edge[1])
+    return [edge[0], second] + inner[:-1] + [last_but_one, edge[2]]
 
 
 def started(pairs, sems):
@@ -199,45 +219,50 @@
     return loads
 
 
-def prepare(state, still, groups, row, held, level_id, wet, start, tide, cor):
-    tiles = wet.shape[1] // LANES
-    held = held[...] > 0
-
-    def turn(source, put):
-        for i, columns in enumerate(to_columns([source(v) for v in range(tiles)])):
-            for n, q in enumerate(groups):
-                put((i, pl.ds(SUB * n, SUB)), columns[SUB * q : SUB * q + SUB])
-
-    def store(ref, f, source):
-        def put(at, x):
-            ref[f, at[0], at[1], :] = x
-
-        turn(source, put)
-
-    levels = LANES - 1
-    row = row[...]
+def turn(groups, source, put):
+    tiles = BS * BS // LANES
+    for i, columns in enumerate(to_columns([source(v) for v in range(tiles)])):
+        for n, q in enumerate(groups):
+            put((i, pl.ds(SUB * n, SUB)), columns[SUB * q : SUB * q + SUB])
+
+
+def storing(ref, f):
+    def put(at, x):
+        ref[f, at[0], at[1], :] = x
+
+    return put
+
+
+def turn_rest(groups, tide, cor, rest):
+    for f in range(2):
+        turn(groups, lambda v, f=f: lane_tile(tide, v, (f,)), storing(rest, 1 + f))
+    turn(groups, lambda v: F32(0.3) * lane_tile(cor, v), storing(rest, 0))
+
+
+def turn_land(groups, held, row, level_id, wet, land):
+    none = LANES - 1
+    held, row = held[...] > 0, row[...]
 
     def coded(v):
         here = jnp.logical_and(lane_tile(wet, v) > 0, held)
-        return jnp.where(here, lane_tile(level_id, v), levels)
-
-    def store_depth(at, code):
-        still[0, at[0], at[1], :] = lanes_of(row, code)
-        still[1, at[0], at[1], :] = (code < levels).astype(F32)
-
-    turn(coded, store_depth)
-
-    def store_state(f):
+        return jnp.where(here, lane_tile(level_id, v), none)
+
+    def put(at, code):
+        land[0, at[0], at[1], :] = lanes_of(row, code)
+        land[1, at[0], at[1], :] = (code < none).astype(F32)
+
+    turn(groups, coded, put)
+
+
+def turn_state(groups, start, land, state):
+    def storing_live(f):
         def put(at, x):
-            state[f, at[0], at[1], :] = x * still[1, at[0], at[1], :]
+            state[f, at[0], at[1], :] = x * land[1, at[0], at[1], :]
 
         return put
 
     for f in range(3):
-        turn(lambda v, f=f: lane_tile(start, v, (0, f)), store_state(f))
-    for f in range(2):
-        store(still, 3 + f, lambda v, f=f: lane_tile(tide, v, (f,)))
-    store(still, 2, lambda v: F32(0.3) * lane_tile(cor, v))
+        turn(groups, lambda v, f=f: lane_tile(start, v, (0, f)), storing_live(f))
 
 
 def clock_kernel(slices, times):
@@ -259,17 +284,18 @@
     held[...] = (tile_iota(0) < count_ref[0]).astype(jnp.int32)
 
 
-def before_kernel(
-    times, face, held, row, level_id, wet, start, tide, cor, pe, pw, state, still
-):
-
-    prepare(state, still, PARTS[0], row, held, level_id, wet, start, tide, cor)
+def still_kernel(held, row, level_id, wet, tide, cor, land, rest):
+    turn_rest(NEAR, tide, cor, rest)
+    turn_land(NEAR, held, row, level_id, wet, land)
+
+
+def before_kernel(times, face, start, land, rest, pe, pw, state):
+    turn_state(NEAR, start, land, state)
     rows = [face[j] for j in range(4)]
-    s = fields_of(state, still)
-    runs = (PARTS[0][:2], PARTS[0][2:])
-    interior_steps(s, runs, times, range(SENT), chunk_ghosts(rows[0], rows[1]), True)
-
-    end = SUB * len(PARTS[0])
+    s = fields_of(state, land, rest)
+    interior_steps(s, SIDES, times, range(SENT), chunk_ghosts(rows[0], rows[1]), True)
+
+    end = SUB * len(NEAR)
     for f, name in enumerate(NAMES):
         ref, at = s[name]
         for i in range(ROWS):
@@ -293,17 +319,24 @@
 
 def during_kernel(
     times, face, held, row, level_id, wet, start, tide, cor, gain_h,
-    last, still, inner, inner_gain, edge_gain, edge_base,
+    last, land, rest, inner, inner_gain, edge_gain, edge_base,
     gain, sems,
 ):
     loads = started([(gain_h, gain)], sems)
     tiles = wet.shape[1] // LANES
-    prepare(last, still, ALL, row, held, level_id, wet, start, tide, cor)
+    turn_land(ALL, held, row, level_id, wet, land)
+    turn_state(ALL, start, land, last)
+    turn_rest(ALL, tide, cor, rest)
     ghosts = chunk_ghosts(face[0], face[1])
-    interior_steps(fields_of(last, still), (ALL,), times, range(STEPS), ghosts, False)
+    interior_steps(fields_of(last, land, rest), (ALL,), times, range(STEPS), ghosts, False)
     held = held[...].astype(F32)
     for load in loads:
         load.wait()
+
+    def store(ref, f, i, parts):
+        for n, x in enumerate(parts):
+            ref[f, i, pl.ds(SUB * n, SUB), :] = x
+
     for f in range(3):
         gains = [lane_tile(gain, v, (f,)) for v in range(tiles)]
         base = [
@@ -312,17 +345,19 @@
         ]
         gains, base = to_columns(gains), to_columns(base)
         for i in range(ROWS):
-            for n in range(GROUPS // 2):
-                at, to = [slice(SUB * part[n], SUB * part[n] + SUB) for part in PARTS], pl.ds(SUB * n, SUB)
-                edge_gain[f, i, to, :] = gains[i][at[0]]
-                edge_base[f, i, to, :] = base[i][at[0]]
-                inner_gain[f, i, to, :] = gains[i][at[1]]
-                inner[f, i, to, :] = last[f, i, pl.ds(SUB * PARTS[1][n], SUB), :] - base[i][at[1]]
-
-
-def after_kernel(times, pe, pw, last, still, face, base, edge, joined):
+            gain_parts, base_parts, last_parts = (
+                parted([x[SUB * q : SUB * q + SUB] for q in ALL])
+                for x in (gains[i], base[i], last[f, i])
+            )
+            store(edge_gain, f, i, gain_parts[0])
+            store(inner_gain, f, i, gain_parts[1])
+            store(edge_base, f, i, base_parts[0])
+            store(inner, f, i, [x - y for x, y in zip(last_parts[1], base_parts[1])])
+
+
+def after_kernel(times, pe, pw, last, land, rest, face, base, edge, joined):
     sub, lane = tile_iota(0), tile_iota(1)
-    s = fields_of(last, still)
+    s = fields_of(last, land, rest)
 
     for f, name in enumerate(NAMES):
         ref, at = s[name]
@@ -450,11 +485,10 @@
         for i in range(ROWS):
             a, b, c = (shifted(cells[name, 0, g][i], 2) for g in range(3))
             d, e, h = (shifted(cells[name, 1, g][i], -2) for g in range(3))
-            inside = [last[f, i, pl.ds(SUB * q, SUB), :] for q in PARTS[0][1:3]]
+            second, last_but_one = jnp.where(sub < 2, b, c), jnp.where(sub >= 6, e, h)
             fine = [
                 jnp.where(sub < 2, a, b),
-                jnp.where(sub < 2, b, jnp.where(sub < 4, c, inside[0])),
-                jnp.where(sub >= 6, e, jnp.where(sub >= 4, h, inside[1])),
+                jnp.where(sub < HALF - SUB, second, last_but_one),
                 jnp.where(sub >= 6, d, e),
             ]
             for n, x in enumerate(fine):
@@ -469,13 +503,15 @@
     for f in range(3):
         columns = []
         for i in range(ROWS):
-            q = [None] * GROUPS
-            for groups, (total, own, gain) in zip(PARTS, parts):
-                for n, group in enumerate(groups):
+            done = []
+            for total, own, gain in parts:
+                done.append([])
+                for n in range(gain.shape[2] // SUB):
                     g = part_tile(gain, f, i, n)
                     most = power(g, slices - 1)
                     whole = part_tile(total, f, i, n) + most * part_tile(own, f, i, n)
-                    q[group] = whole / (F32(1) - most * g)
+                    done[-1].append(whole / (F32(1) - most * g))
+            q = joint(*done)
             columns.append(jnp.concatenate(q, axis=0))
         for v, x in enumerate(to_tiles(columns)):
             out[0, f, :, pl.ds(v * LANES, LANES)] = x
@@ -523,7 +559,10 @@
     start_states, coarse_gain, depth_level, depth_table, wet, block_count, neighbour, coriolis, tide
 ):
     slices = lax.axis_size("tm")
-    whole, half = shape(3, ROWS, BS, LANES), shape(3, ROWS, BS // 2, LANES)
+
+    def columns(fields, size):
+        return shape(fields, ROWS, size, LANES)
+
     times = call(
         functools.partial(clock_kernel, slices), shape(2 * STEPS, SUB, LANES), [], flops=10**10
     )
@@ -535,18 +574,27 @@
         [block_count, neighbour.T],
         spaces=[pltpu.SMEM, pltpu.VMEM],
     )
-    ready = [times] + list(slot_tiles) + [row, depth_level, wet, start_states, tide, coriolis]
+    face, held = slot_tiles
+    ready = [times, face, held, row, depth_level, wet, start_states, tide, coriolis]
+    near = SUB * len(NEAR)
+    land, rest = call(
+        still_kernel,
+        [columns(2, near), columns(3, near)],
+        [held, row, depth_level, wet, tide, coriolis],
+    )
     pe, pw = call(
         before_kernel,
         [shape(ROWS, len(NAMES) * OUT, LANES)] * 2,
-        ready,
-        scratch=[pltpu.VMEM(half.shape, F32), pltpu.VMEM((5,) + half.shape[1:], F32)],
+        [times, face, start_states, land, rest],
+        scratch=[pltpu.VMEM(columns(3, near).shape, F32)],
     )
     from_west = passed_along(pe, "space", 1)
     from_east = passed_along(pw, "space", -1)
-    last, still, inner, inner_gain, edge_gain, edge_base = call(
+    last, land, rest, inner, inner_gain, edge_gain, edge_base = call(
         during_kernel,
-        [whole, shape(5, ROWS, BS, LANES)] + [half] * 4,
+        [columns(3, BS), columns(2, BS), columns(3, BS)]
+        + [columns(3, INNER)] * 2
+        + [columns(3, EDGE)] * 2,
         ready + in_hbm([coarse_gain]),
         spaces=[pltpu.VMEM] * len(ready) + [pltpu.HBM],
         scratch=[pltpu.VMEM(coarse_gain.shape, F32), pltpu.SemaphoreType.DMA((1,))],
@@ -554,8 +602,8 @@
     inner_sum = periodic_sum(inner, inner_gain, slices)
     edge = call(
         after_kernel,
-        half,
-        [times, from_west, from_east, last, still, slot_tiles[0], edge_base],
+        columns(3, EDGE),
+        [times, from_west, from_east, last, land, rest, face, edge_base],
         scratch=[pltpu.VMEM((len(NAMES), ROWS, 2, SUB, LANES), F32)],
     )
     edge_sum = periodic_sum(edge, edge_gain, slices)

time: 15.7 us -> 15.6 us (level)
    pallas_call x7 -> x8, Pallas kernels: 4.84 us -> 4.86 us  [call(): pl.pallas_call(kernel, out_shape=out_shape, in_specs=[pl.BlockSpec(memory...]
  transfers between devices with their start and end apart: 4 -> 4, of which waited for: 2 -> 2; matrix products, arithmetic and copies ran while one was open for 0% -> 0% of each run, Pallas kernels for 19% -> 20%
where the time goes in v6:
time: 15.6 us; the launch traced here: 15.4 us
  starting transfers between devices  7.19 us (46%)
  Pallas kernels  4.86 us (31%)
  waiting for transfers between devices  2.26 us (14%)
  between operations  0.83 us (5%)
  local copies, waits for them, and re-layouts  0.26 us (2%)
    ppermute x4, starting transfers between devices, passed_along(): lax.ppermute(shard, axis, [(i, (i + by) % size) for i in range(size)])  7.19 us
    pallas_call x8, Pallas kernels, call(): pl.pallas_call(kernel, out_shape=out_shape, in_specs=[pl.BlockSpec(memory...  4.86 us
    ppermute x4, waiting for transfers between devices, passed_along(): lax.ppermute(shard, axis, [(i, (i + by) % size) for i in range(size)])  2.26 us
  transfers between devices with their start and end apart: 4, of which 2 were waited for; matrix products, arithmetic and copies ran while one was open for 0% of the time, Pallas kernels for 20%

profile of v6, /device:TPU:0, one launch (start us, length us, event | category | flops | bytes accessed | tf_op | source)
XLA Modules:
  0.0 15.4 jit_solution(9574345340413249074)
XLA Ops:
  0.0 0.0 copy-start.1
  0.0 0.0 copy-start.4
  0.0 0.0 copy-start.3
  0.0 0.0 copy-start.2
  0.0 0.0 copy-start.6
  0.0 0.0 copy-start.5
  0.1 0.0 copy-start
  0.8 0.0 copy-done.6
  0.8 0.0 copy-done.5
  0.8 0.1 shard_map.92
  0.9 0.1 copy-done.1
  1.0 0.0 copy-done.4
  1.0 0.1 copy-done.3
  1.1 0.1 copy-done.2
  1.2 0.3 %shard_map.94 = (f32[2,4,32,128]{3,2,1,0:T(8,128)S(1)}, f32[3,4,32,128]{3,2,1,0:T(8,128)S(1)}) custom-call(s32[8,128]{1,0:T(8,128)S(1)} %get-tuple-element.19.held, f32[8,128]{1,0:T(8,128)S(1)} %shard_map.93.row, s32[8,4096]{1,0:T(8,128)S(1)} %copy-done.2, s32[8,4096]{1,0:T(8,128)S(1)} %copy-done.3, f32[2,8,4096]{2,1,0:T(8,128)S(1)} %copy-done.1, ...), custom_call_target="tpu_custom_call" | custom-call | bytes 1327104 | tf_op jit(solution)/shard_map/pallas_call | solution.py:527
  1.4 0.0 copy-done
  1.4 0.6 %shard_map.95 = (f32[4,48,128]{2,1,0:T(8,128)S(1)}, f32[4,48,128]{2,1,0:T(8,128)S(1)}) custom-call(f32[12,8,128]{2,1,0:T(8,128)S(1)} %shard_map.91.times, s32[4,8,128]{2,1,0:T(8,128)S(1)} %get-tuple-element.18.face, f32[1,3,8,4096]{3,2,1,0:T(8,128)S(1)} %copy-done, f32[2,4,32,128]{3,2,1,0:T(8,128)S(1)} %get-tuple-element.20.land, ...), custom_call_target="tpu_custom_call" | custom-call | bytes 1572864 | tf_op jit(solution)/shard_map/pallas_call | solution.py:527
  2.0 3.0 %collective-permute-start = (f32[4,48,128]{2,1,0:T(8,128)S(1)}, f32[4,48,128]{2,1,0:T(8,128)S(1)}, u32[]{:S(2)}, u32[]{:S(2)}) collective-permute-start(f32[4,48,128]{2,1,0:T(8,128)S(1)} %get-tuple-element.22), channel_id=1, source_target_pairs={{0,1},{1,2},{2,3},{3,4},{4,5},{5,6},{6,7},{7,8},{8,9},{9,10},{10,1... | collective-permute-start | bytes 294920 | tf_op jit(solution)/shard_map/ppermute | solution.py:548
  5.0 4.1 %collective-permute-start.1 = (f32[4,48,128]{2,1,0:T(8,128)S(1)}, f32[4,48,128]{2,1,0:T(8,128)S(1)}, u32[]{:S(2)}, u32[]{:S(2)}) collective-permute-start(f32[4,48,128]{2,1,0:T(8,128)S(1)} %get-tuple-element.23), channel_id=1, source_target_pairs={{0,15},{1,0},{2,1},{3,2},{4,3},{5,4},{6,5},{7,6},{8,7},{9,8},{10,9... | collective-permute-start | bytes 294920 | tf_op jit(solution)/shard_map/ppermute | solution.py:548
  9.1 1.8 %shard_map.96 = (f32[3,4,64,128]{3,2,1,0:T(8,128)S(1)}, f32[2,4,64,128]{3,2,1,0:T(8,128)S(1)}, f32[3,4,64,128]{3,2,1,0:T(8,128)S(1)}, f32[3,4,40,128]{3,2,1,0:T(...) custom-call(f32[12,8,128]{2,1,0:T(8,128)S(1)} %shard_map.91.times, ...), custom_call_target="tpu_custom_call" | custom-call | bytes 3031040 | tf_op jit(solution)/shard_map/pallas_call | solution.py:527
  10.9 0.1 collective-permute-start.3
  11.0 0.9 %collective-permute-done.pe = f32[4,48,128]{2,1,0:T(8,128)S(1)} collective-permute-done((f32[4,48,128]{2,1,0:T(8,128)S(1)}, f32[4,48,128]{2,1,0:T(8,128)S(1)}, u32[]{:S(2)}, u32[]{:S(2)}) %collective-permute-start) | collective-permute-done | bytes 98336 | tf_op jit(solution)/shard_map/ppermute | solution.py:548
  11.9 0.0 collective-permute-done.1.pw
  11.9 1.2 %shard_map.97.edge = f32[3,4,24,128]{3,2,1,0:T(8,128)S(1)} custom-call(f32[12,8,128]{2,1,0:T(8,128)S(1)} %shard_map.91.times, f32[4,48,128]{2,1,0:T(8,128)S(1)} %collective-permute-done.pe, f32[4,48,128]{2,1,0:T(8,128)S(1)} %collective-permute-done.1.pw, f32[3,4,64,128]{3,2,1,0:T(8,128)S(1)} %get-tuple-element.24.last, ...), custom_call_target="tpu_custom_call" | custom-call | bytes 2916352 | tf_op jit(solution)/shard_map/pallas_call | solution.py:527
  13.1 0.1 collective-permute-start.2
  13.2 1.4 %collective-permute-done.2.edge_sum = f32[3,4,24,128]{3,2,1,0:T(8,128)S(1)} collective-permute-done((f32[3,4,24,128]{3,2,1,0:T(8,128)S(1)}, f32[3,4,24,128]{3,2,1,0:T(8,128)S(1)}, u32[]{:S(2)}, u32[]{:S(2)}) %collective-permute-start.2) | collective-permute-done | bytes 147488 | tf_op jit(solution)/shard_map/ppermute | solution.py:548
  14.5 0.0 collective-permute-done.3.inner_sum
  14.5 0.9 %shard_map.98 = f32[1,3,8,4096]{3,2,1,0:T(8,128)} custom-call(f32[3,4,24,128]{3,2,1,0:T(8,128)S(1)} %collective-permute-done.2.edge_sum, f32[3,4,24,128]{3,2,1,0:T(8,128)S(1)} %shard_map.97.edge, f32[3,4,24,128]{3,2,1,0:T(8,128)S(1)} %get-tuple-element.28.edge_gain, f32[3,4,40,128]{3,2,1,0:T(8,128)S(1)} %collective-permute-done.3.inner_sum, ...), custom_call_target="tpu_custom_call" | custom-call | bytes 2359296 | tf_op jit(solution)/shard_map/pallas_call | solution.py:527
  (2 shorter events, 0.0 us)
Async XLA Ops:
  0.0 1.0 %copy-start.1 = (f32[2,8,4096]{2,1,0:T(8,128)S(1)}, f32[2,8,4096]{2,1,0:T(8,128)}, u32[]{:S(2)}) copy-start(f32[2,8,4096]{2,1,0:T(8,128)} %tide.3) | copy-start | bytes 786436
  0.0 1.0 %copy-start.4 = (f32[8,4096]{1,0:T(8,128)S(1)}, f32[8,4096]{1,0:T(8,128)}, u32[]{:S(2)}) copy-start(f32[8,4096]{1,0:T(8,128)} %cor.3) | copy-start | bytes 393220
  0.0 1.1 %copy-start.3 = (s32[8,4096]{1,0:T(8,128)S(1)}, s32[8,4096]{1,0:T(8,128)}, u32[]{:S(2)}) copy-start(s32[8,4096]{1,0:T(8,128)} %wet.3) | copy-start | bytes 393220
  0.0 1.1 %copy-start.2 = (s32[8,4096]{1,0:T(8,128)S(1)}, s32[8,4096]{1,0:T(8,128)}, u32[]{:S(2)}) copy-start(s32[8,4096]{1,0:T(8,128)} %level_id.3) | copy-start | bytes 393220
  0.0 0.8 %copy-start.6 = (f32[64]{0:T(128)S(1)}, f32[64]{0:T(128)}, u32[]{:S(2)}) copy-start(f32[64]{0:T(128)} %table.1) | copy-start | bytes 772
  0.0 0.8 %copy-start.5 = (s32[8,4]{0,1:T(4,128)S(1)}, s32[8,4]{0,1:T(4,128)}, u32[]{:S(2)}) copy-start(s32[8,4]{0,1:T(4,128)} %param.15) | copy-start | bytes 388
  0.1 1.4 %copy-start = (f32[1,3,8,4096]{3,2,1,0:T(8,128)S(1)}, f32[1,3,8,4096]{3,2,1,0:T(8,128)}, u32[]{:S(2)}) copy-start(f32[1,3,8,4096]{3,2,1,0:T(8,128)} %start.3) | copy-start | bytes 1179652
  2.0 9.9 %collective-permute-start = (f32[4,48,128]{2,1,0:T(8,128)S(1)}, f32[4,48,128]{2,1,0:T(8,128)S(1)}, u32[]{:S(2)}, u32[]{:S(2)}) collective-permute-start(f32[4,48,128]{2,1,0:T(8,128)S(1)} %get-tuple-element.22), channel_id=1, source_target_pairs={{0,1},{1,2},{2,3},{3,4},{4,5},{5,6},{6,7},{7,8},{8,9},{9,10},{10,1... | collective-permute-start | bytes 294920 | tf_op jit(solution)/shard_map/ppermute | solution.py:548
  5.0 6.9 %collective-permute-start.1 = (f32[4,48,128]{2,1,0:T(8,128)S(1)}, f32[4,48,128]{2,1,0:T(8,128)S(1)}, u32[]{:S(2)}, u32[]{:S(2)}) collective-permute-start(f32[4,48,128]{2,1,0:T(8,128)S(1)} %get-tuple-element.23), channel_id=1, source_target_pairs={{0,15},{1,0},{2,1},{3,2},{4,3},{5,4},{6,5},{7,6},{8,7},{9,8},{10,9... | collective-permute-start | bytes 294920 | tf_op jit(solution)/shard_map/ppermute | solution.py:548
  10.9 3.6 %collective-permute-start.3 = (f32[3,4,40,128]{3,2,1,0:T(8,128)S(1)}, f32[3,4,40,128]{3,2,1,0:T(8,128)S(1)}, u32[]{:S(2)}, u32[]{:S(2)}) collective-permute-start(f32[3,4,40,128]{3,2,1,0:T(8,128)S(1)} %get-tuple-element.29.inner), channel_id=1, source_target_pairs={{0,16},{16,0},{1,17},{17,1},{2,18},{18,2},{3,19},{19,3},{4,20},{20... | collective-permute-start | bytes 737288 | tf_op jit(solution)/shard_map/ppermute | solution.py:548
  13.1 1.4 %collective-permute-start.2 = (f32[3,4,24,128]{3,2,1,0:T(8,128)S(1)}, f32[3,4,24,128]{3,2,1,0:T(8,128)S(1)}, u32[]{:S(2)}, u32[]{:S(2)}) collective-permute-start(f32[3,4,24,128]{3,2,1,0:T(8,128)S(1)} %shard_map.97.edge), channel_id=1, source_target_pairs={{0,16},{16,0},{1,17},{17,1},{2,18},{18,2},{3,19},{19,3},{4,20},{20... | collective-permute-start | bytes 442376 | tf_op jit(solution)/shard_map/ppermute | solution.py:548

commit v7 on v6

--- a/solution.py
+++ b/solution.py
@@ -233,10 +233,18 @@
     return put
 
 
+def turn_tide(groups, tide, tides):
+    for f in range(2):
+        turn(groups, lambda v, f=f: lane_tile(tide, v, (f,)), storing(tides, f))
+
+
+def turn_cor(groups, cor, out):
+    turn(groups, lambda v: F32(0.3) * lane_tile(cor, v), storing(out, 0))
+
+
 def turn_rest(groups, tide, cor, rest):
-    for f in range(2):
-        turn(groups, lambda v, f=f: lane_tile(tide, v, (f,)), storing(rest, 1 + f))
-    turn(groups, lambda v: F32(0.3) * lane_tile(cor, v), storing(rest, 0))
+    turn_tide(groups, tide, rest.at[pl.ds(1, 2)])
+    turn_cor(groups, cor, rest.at[pl.ds(0, 1)])
 
 
 def turn_land(groups, held, row, level_id, wet, land):
@@ -284,15 +292,17 @@
     held[...] = (tile_iota(0) < count_ref[0]).astype(jnp.int32)
 
 
-def still_kernel(held, row, level_id, wet, tide, cor, land, rest):
-    turn_rest(NEAR, tide, cor, rest)
+def still_kernel(held, row, level_id, wet, cor, land, turned):
     turn_land(NEAR, held, row, level_id, wet, land)
-
-
-def before_kernel(times, face, start, land, rest, pe, pw, state):
+    turn_cor(NEAR, cor, turned)
+
+
+def before_kernel(times, face, start, tide, land, cor, pe, pw, state, tides):
     turn_state(NEAR, start, land, state)
+    turn_tide(NEAR, tide, tides)
     rows = [face[j] for j in range(4)]
-    s = fields_of(state, land, rest)
+    s = fields_of(state, land, tides)
+    s.update(cor=(cor, 0), tide0=(tides, 0), tide1=(tides, 1))
     interior_steps(s, SIDES, times, range(SENT), chunk_ghosts(rows[0], rows[1]), True)
 
     end = SUB * len(NEAR)
@@ -577,16 +587,16 @@
     face, held = slot_tiles
     ready = [times, face, held, row, depth_level, wet, start_states, tide, coriolis]
     near = SUB * len(NEAR)
-    land, rest = call(
+    land, cor = call(
         still_kernel,
-        [columns(2, near), columns(3, near)],
-        [held, row, depth_level, wet, tide, coriolis],
+        [columns(2, near), columns(1, near)],
+        [held, row, depth_level, wet, coriolis],
     )
     pe, pw = call(
         before_kernel,
         [shape(ROWS, len(NAMES) * OUT, LANES)] * 2,
-        [times, face, start_states, land, rest],
-        scratch=[pltpu.VMEM(columns(3, near).shape, F32)],
+        [times, face, start_states, tide, land, cor],
+        scratch=[pltpu.VMEM(columns(n, near).shape, F32) for n in (3, 2)],
     )
     from_west = passed_along(pe, "space", 1)
     from_east = passed_along(pw, "space", -1)

time: 15.6 us -> 15.5 us (level)
  no operation moved by 1% of the time
where the time goes in v7:
time: 15.5 us; the launch traced here: 15.4 us
  starting transfers between devices  7.19 us (46%)
  Pallas kernels  4.88 us (31%)
  waiting for transfers between devices  2.27 us (15%)
  between operations  0.88 us (6%)
    ppermute x4, starting transfers between devices, passed_along(): lax.ppermute(shard, axis, [(i, (i + by) % size) for i in range(size)])  7.19 us
    pallas_call x8, Pallas kernels, call(): pl.pallas_call(kernel, out_shape=out_shape, in_specs=[pl.BlockSpec(memory...  4.88 us
    ppermute x4, waiting for transfers between devices, passed_along(): lax.ppermute(shard, axis, [(i, (i + by) % size) for i in range(size)])  2.27 us
  transfers between devices with their start and end apart: 4, of which 2 were waited for; matrix products, arithmetic and copies ran while one was open for 0% of the time, Pallas kernels for 20%

profile of v7, /device:TPU:0, one launch (start us, length us, event | category | flops | bytes accessed | tf_op | source)
XLA Modules:
  0.0 15.4 jit_solution(12196408886089301760)
XLA Ops:
  0.0 0.0 copy-start.4
  0.0 0.0 copy-start.3
  0.0 0.0 copy-start.2
  0.0 0.0 copy-start.6
  0.0 0.0 copy-start.5
  0.0 0.0 copy-start.1
  0.1 0.0 copy-start
  0.8 0.0 copy-done.6
  0.8 0.0 copy-done.5
  0.9 0.1 shard_map.92
  0.9 0.0 copy-done.4
  1.0 0.0 copy-done.3
  1.0 0.1 copy-done.2
  1.1 0.2 %shard_map.94 = (f32[2,4,32,128]{3,2,1,0:T(8,128)S(1)}, f32[1,4,32,128]{3,2,1,0:T(8,128)S(1)}) custom-call(s32[8,128]{1,0:T(8,128)S(1)} %get-tuple-element.19.held, f32[8,128]{1,0:T(8,128)S(1)} %shard_map.93.row, s32[8,4096]{1,0:T(8,128)S(1)} %copy-done.2, s32[8,4096]{1,0:T(8,128)S(1)} %copy-done.3, f32[8,4096]{1,0:T(8,128)S(1)} %copy-done.4), custom_call_target="tpu_custom_call" | custom-call | bytes 802816 | tf_op jit(solution)/shard_map/pallas_call | solution.py:537
  1.3 0.0 copy-done.1
  1.3 0.0 copy-done
  1.3 0.7 %shard_map.95 = (f32[4,48,128]{2,1,0:T(8,128)S(1)}, f32[4,48,128]{2,1,0:T(8,128)S(1)}) custom-call(f32[12,8,128]{2,1,0:T(8,128)S(1)} %shard_map.91.times, s32[4,8,128]{2,1,0:T(8,128)S(1)} %get-tuple-element.18.face, f32[1,3,8,4096]{3,2,1,0:T(8,128)S(1)} %copy-done, f32[2,8,4096]{2,1,0:T(8,128)S(1)} %copy-done.1, ...), custom_call_target="tpu_custom_call" | custom-call | bytes 1835008 | tf_op jit(solution)/shard_map/pallas_call | solution.py:537
  2.0 3.0 %collective-permute-start = (f32[4,48,128]{2,1,0:T(8,128)S(1)}, f32[4,48,128]{2,1,0:T(8,128)S(1)}, u32[]{:S(2)}, u32[]{:S(2)}) collective-permute-start(f32[4,48,128]{2,1,0:T(8,128)S(1)} %get-tuple-element.22), channel_id=1, source_target_pairs={{0,1},{1,2},{2,3},{3,4},{4,5},{5,6},{6,7},{7,8},{8,9},{9,10},{10,1... | collective-permute-start | bytes 294920 | tf_op jit(solution)/shard_map/ppermute | solution.py:558
  5.0 4.1 %collective-permute-start.1 = (f32[4,48,128]{2,1,0:T(8,128)S(1)}, f32[4,48,128]{2,1,0:T(8,128)S(1)}, u32[]{:S(2)}, u32[]{:S(2)}) collective-permute-start(f32[4,48,128]{2,1,0:T(8,128)S(1)} %get-tuple-element.23), channel_id=1, source_target_pairs={{0,15},{1,0},{2,1},{3,2},{4,3},{5,4},{6,5},{7,6},{8,7},{9,8},{10,9... | collective-permute-start | bytes 294920 | tf_op jit(solution)/shard_map/ppermute | solution.py:558
  9.0 1.8 %shard_map.96 = (f32[3,4,64,128]{3,2,1,0:T(8,128)S(1)}, f32[2,4,64,128]{3,2,1,0:T(8,128)S(1)}, f32[3,4,64,128]{3,2,1,0:T(8,128)S(1)}, f32[3,4,40,128]{3,2,1,0:T(...) custom-call(f32[12,8,128]{2,1,0:T(8,128)S(1)} %shard_map.91.times, ...), custom_call_target="tpu_custom_call" | custom-call | bytes 3031040 | tf_op jit(solution)/shard_map/pallas_call | solution.py:537
  10.9 0.1 collective-permute-start.3
  11.0 0.9 %collective-permute-done.pe = f32[4,48,128]{2,1,0:T(8,128)S(1)} collective-permute-done((f32[4,48,128]{2,1,0:T(8,128)S(1)}, f32[4,48,128]{2,1,0:T(8,128)S(1)}, u32[]{:S(2)}, u32[]{:S(2)}) %collective-permute-start) | collective-permute-done | bytes 98336 | tf_op jit(solution)/shard_map/ppermute | solution.py:558
  11.9 0.0 collective-permute-done.1.pw
  11.9 1.2 %shard_map.97.edge = f32[3,4,24,128]{3,2,1,0:T(8,128)S(1)} custom-call(f32[12,8,128]{2,1,0:T(8,128)S(1)} %shard_map.91.times, f32[4,48,128]{2,1,0:T(8,128)S(1)} %collective-permute-done.pe, f32[4,48,128]{2,1,0:T(8,128)S(1)} %collective-permute-done.1.pw, f32[3,4,64,128]{3,2,1,0:T(8,128)S(1)} %get-tuple-element.24.last, ...), custom_call_target="tpu_custom_call" | custom-call | bytes 2916352 | tf_op jit(solution)/shard_map/pallas_call | solution.py:537
  13.0 0.1 collective-permute-start.2
  13.1 1.4 %collective-permute-done.2.edge_sum = f32[3,4,24,128]{3,2,1,0:T(8,128)S(1)} collective-permute-done((f32[3,4,24,128]{3,2,1,0:T(8,128)S(1)}, f32[3,4,24,128]{3,2,1,0:T(8,128)S(1)}, u32[]{:S(2)}, u32[]{:S(2)}) %collective-permute-start.2) | collective-permute-done | bytes 147488 | tf_op jit(solution)/shard_map/ppermute | solution.py:558
  14.5 0.0 collective-permute-done.3.inner_sum
  14.5 0.9 %shard_map.98 = f32[1,3,8,4096]{3,2,1,0:T(8,128)} custom-call(f32[3,4,24,128]{3,2,1,0:T(8,128)S(1)} %collective-permute-done.2.edge_sum, f32[3,4,24,128]{3,2,1,0:T(8,128)S(1)} %shard_map.97.edge, f32[3,4,24,128]{3,2,1,0:T(8,128)S(1)} %get-tuple-element.28.edge_gain, f32[3,4,40,128]{3,2,1,0:T(8,128)S(1)} %collective-permute-done.3.inner_sum, ...), custom_call_target="tpu_custom_call" | custom-call | bytes 2359296 | tf_op jit(solution)/shard_map/pallas_call | solution.py:537
  (2 shorter events, 0.0 us)
Async XLA Ops:
  0.0 0.9 %copy-start.4 = (f32[8,4096]{1,0:T(8,128)S(1)}, f32[8,4096]{1,0:T(8,128)}, u32[]{:S(2)}) copy-start(f32[8,4096]{1,0:T(8,128)} %cor.3) | copy-start | bytes 393220
  0.0 1.0 %copy-start.3 = (s32[8,4096]{1,0:T(8,128)S(1)}, s32[8,4096]{1,0:T(8,128)}, u32[]{:S(2)}) copy-start(s32[8,4096]{1,0:T(8,128)} %wet.3) | copy-start | bytes 393220
  0.0 1.1 %copy-start.2 = (s32[8,4096]{1,0:T(8,128)S(1)}, s32[8,4096]{1,0:T(8,128)}, u32[]{:S(2)}) copy-start(s32[8,4096]{1,0:T(8,128)} %level_id.3) | copy-start | bytes 393220
  0.0 0.8 %copy-start.6 = (f32[64]{0:T(128)S(1)}, f32[64]{0:T(128)}, u32[]{:S(2)}) copy-start(f32[64]{0:T(128)} %table.1) | copy-start | bytes 772
  0.0 0.8 %copy-start.5 = (s32[8,4]{0,1:T(4,128)S(1)}, s32[8,4]{0,1:T(4,128)}, u32[]{:S(2)}) copy-start(s32[8,4]{0,1:T(4,128)} %param.15) | copy-start | bytes 388
  0.0 1.3 %copy-start.1 = (f32[2,8,4096]{2,1,0:T(8,128)S(1)}, f32[2,8,4096]{2,1,0:T(8,128)}, u32[]{:S(2)}) copy-start(f32[2,8,4096]{2,1,0:T(8,128)} %tide.3) | copy-start | bytes 786436
  0.1 1.3 %copy-start = (f32[1,3,8,4096]{3,2,1,0:T(8,128)S(1)}, f32[1,3,8,4096]{3,2,1,0:T(8,128)}, u32[]{:S(2)}) copy-start(f32[1,3,8,4096]{3,2,1,0:T(8,128)} %start.3) | copy-start | bytes 1179652
  2.0 9.9 %collective-permute-start = (f32[4,48,128]{2,1,0:T(8,128)S(1)}, f32[4,48,128]{2,1,0:T(8,128)S(1)}, u32[]{:S(2)}, u32[]{:S(2)}) collective-permute-start(f32[4,48,128]{2,1,0:T(8,128)S(1)} %get-tuple-element.22), channel_id=1, source_target_pairs={{0,1},{1,2},{2,3},{3,4},{4,5},{5,6},{6,7},{7,8},{8,9},{9,10},{10,1... | collective-permute-start | bytes 294920 | tf_op jit(solution)/shard_map/ppermute | solution.py:558
  5.0 6.9 %collective-permute-start.1 = (f32[4,48,128]{2,1,0:T(8,128)S(1)}, f32[4,48,128]{2,1,0:T(8,128)S(1)}, u32[]{:S(2)}, u32[]{:S(2)}) collective-permute-start(f32[4,48,128]{2,1,0:T(8,128)S(1)} %get-tuple-element.23), channel_id=1, source_target_pairs={{0,15},{1,0},{2,1},{3,2},{4,3},{5,4},{6,5},{7,6},{8,7},{9,8},{10,9... | collective-permute-start | bytes 294920 | tf_op jit(solution)/shard_map/ppermute | solution.py:558
  10.9 3.6 %collective-permute-start.3 = (f32[3,4,40,128]{3,2,1,0:T(8,128)S(1)}, f32[3,4,40,128]{3,2,1,0:T(8,128)S(1)}, u32[]{:S(2)}, u32[]{:S(2)}) collective-permute-start(f32[3,4,40,128]{3,2,1,0:T(8,128)S(1)} %get-tuple-element.29.inner), channel_id=1, source_target_pairs={{0,16},{16,0},{1,17},{17,1},{2,18},{18,2},{3,19},{19,3},{4,20},{20... | collective-permute-start | bytes 737288 | tf_op jit(solution)/shard_map/ppermute | solution.py:558
  13.0 1.4 %collective-permute-start.2 = (f32[3,4,24,128]{3,2,1,0:T(8,128)S(1)}, f32[3,4,24,128]{3,2,1,0:T(8,128)S(1)}, u32[]{:S(2)}, u32[]{:S(2)}) collective-permute-start(f32[3,4,24,128]{3,2,1,0:T(8,128)S(1)} %shard_map.97.edge), channel_id=1, source_target_pairs={{0,16},{16,0},{1,17},{17,1},{2,18},{18,2},{3,19},{19,3},{4,20},{20... | collective-permute-start | bytes 442376 | tf_op jit(solution)/shard_map/ppermute | solution.py:558

commit v8 on v7

--- a/solution.py
+++ b/solution.py
@@ -113,10 +113,8 @@
 
 
 def new_velocity(u, w, cor, dx, dy, live):
-    return (
-        (F32(0.985) * u + cor * w - F32(0.15) * dx) * live,
-        (F32(0.985) * w - cor * u - F32(0.15) * dy) * live,
-    )
+    push = F32(0.15) * live
+    return (F32(0.985) * u + cor * w) - push * dx, (F32(0.985) * w - cor * u) - push * dy
 
 
 NAMES = ("level", "east", "north", "depth", "live", "cor", "tide0", "tide1")

time: 15.5 us -> 15.5 us (level)
  no operation moved by 1% of the time
where the time goes in v8:
time: 15.5 us; the launch traced here: 15.4 us
  starting transfers between devices  7.19 us (46%)
  Pallas kernels  4.92 us (32%)
  waiting for transfers between devices  2.22 us (14%)
  between operations  0.88 us (6%)
    ppermute x4, starting transfers between devices, passed_along(): lax.ppermute(shard, axis, [(i, (i + by) % size) for i in range(size)])  7.19 us
    pallas_call x8, Pallas kernels, call(): pl.pallas_call(kernel, out_shape=out_shape, in_specs=[pl.BlockSpec(memory...  4.92 us
    ppermute x4, waiting for transfers between devices, passed_along(): lax.ppermute(shard, axis, [(i, (i + by) % size) for i in range(size)])  2.22 us
  transfers between devices with their start and end apart: 4, of which 2 were waited for; matrix products, arithmetic and copies ran while one was open for 0% of the time, Pallas kernels for 20%

profile of v8, /device:TPU:0, one launch (start us, length us, event | category | flops | bytes accessed | tf_op | source)
XLA Modules:
  0.0 15.4 jit_solution(8373759166973015120)
XLA Ops:
  0.0 0.0 copy-start.4
  0.0 0.0 copy-start.3
  0.0 0.0 copy-start.2
  0.0 0.0 copy-start.6
  0.0 0.0 copy-start.5
  0.0 0.0 copy-start.1
  0.1 0.0 copy-start
  0.8 0.0 copy-done.6
  0.8 0.0 copy-done.5
  0.9 0.1 shard_map.92
  0.9 0.0 copy-done.4
  1.0 0.0 copy-done.3
  1.0 0.1 copy-done.2
  1.1 0.2 %shard_map.94 = (f32[2,4,32,128]{3,2,1,0:T(8,128)S(1)}, f32[1,4,32,128]{3,2,1,0:T(8,128)S(1)}) custom-call(s32[8,128]{1,0:T(8,128)S(1)} %get-tuple-element.19.held, f32[8,128]{1,0:T(8,128)S(1)} %shard_map.93.row, s32[8,4096]{1,0:T(8,128)S(1)} %copy-done.2, s32[8,4096]{1,0:T(8,128)S(1)} %copy-done.3, f32[8,4096]{1,0:T(8,128)S(1)} %copy-done.4), custom_call_target="tpu_custom_call" | custom-call | bytes 802816 | tf_op jit(solution)/shard_map/pallas_call | solution.py:535
  1.3 0.0 copy-done.1
  1.3 0.0 copy-done
  1.3 0.7 %shard_map.95 = (f32[4,48,128]{2,1,0:T(8,128)S(1)}, f32[4,48,128]{2,1,0:T(8,128)S(1)}) custom-call(f32[12,8,128]{2,1,0:T(8,128)S(1)} %shard_map.91.times, s32[4,8,128]{2,1,0:T(8,128)S(1)} %get-tuple-element.18.face, f32[1,3,8,4096]{3,2,1,0:T(8,128)S(1)} %copy-done, f32[2,8,4096]{2,1,0:T(8,128)S(1)} %copy-done.1, ...), custom_call_target="tpu_custom_call" | custom-call | bytes 1835008 | tf_op jit(solution)/shard_map/pallas_call | solution.py:535
  2.0 3.0 %collective-permute-start = (f32[4,48,128]{2,1,0:T(8,128)S(1)}, f32[4,48,128]{2,1,0:T(8,128)S(1)}, u32[]{:S(2)}, u32[]{:S(2)}) collective-permute-start(f32[4,48,128]{2,1,0:T(8,128)S(1)} %get-tuple-element.22), channel_id=1, source_target_pairs={{0,1},{1,2},{2,3},{3,4},{4,5},{5,6},{6,7},{7,8},{8,9},{9,10},{10,1... | collective-permute-start | bytes 294920 | tf_op jit(solution)/shard_map/ppermute | solution.py:556
  5.0 4.1 %collective-permute-start.1 = (f32[4,48,128]{2,1,0:T(8,128)S(1)}, f32[4,48,128]{2,1,0:T(8,128)S(1)}, u32[]{:S(2)}, u32[]{:S(2)}) collective-permute-start(f32[4,48,128]{2,1,0:T(8,128)S(1)} %get-tuple-element.23), channel_id=1, source_target_pairs={{0,15},{1,0},{2,1},{3,2},{4,3},{5,4},{6,5},{7,6},{8,7},{9,8},{10,9... | collective-permute-start | bytes 294920 | tf_op jit(solution)/shard_map/ppermute | solution.py:556
  9.0 1.9 %shard_map.96 = (f32[3,4,64,128]{3,2,1,0:T(8,128)S(1)}, f32[2,4,64,128]{3,2,1,0:T(8,128)S(1)}, f32[3,4,64,128]{3,2,1,0:T(8,128)S(1)}, f32[3,4,40,128]{3,2,1,0:T(...) custom-call(f32[12,8,128]{2,1,0:T(8,128)S(1)} %shard_map.91.times, ...), custom_call_target="tpu_custom_call" | custom-call | bytes 3031040 | tf_op jit(solution)/shard_map/pallas_call | solution.py:535
  10.9 0.1 collective-permute-start.3
  11.0 0.9 %collective-permute-done.pe = f32[4,48,128]{2,1,0:T(8,128)S(1)} collective-permute-done((f32[4,48,128]{2,1,0:T(8,128)S(1)}, f32[4,48,128]{2,1,0:T(8,128)S(1)}, u32[]{:S(2)}, u32[]{:S(2)}) %collective-permute-start) | collective-permute-done | bytes 98336 | tf_op jit(solution)/shard_map/ppermute | solution.py:556
  11.9 0.0 collective-permute-done.1.pw
  11.9 1.2 %shard_map.97.edge = f32[3,4,24,128]{3,2,1,0:T(8,128)S(1)} custom-call(f32[12,8,128]{2,1,0:T(8,128)S(1)} %shard_map.91.times, f32[4,48,128]{2,1,0:T(8,128)S(1)} %collective-permute-done.pe, f32[4,48,128]{2,1,0:T(8,128)S(1)} %collective-permute-done.1.pw, f32[3,4,64,128]{3,2,1,0:T(8,128)S(1)} %get-tuple-element.24.last, ...), custom_call_target="tpu_custom_call" | custom-call | bytes 2916352 | tf_op jit(solution)/shard_map/pallas_call | solution.py:535
  13.0 0.1 collective-permute-start.2
  13.1 1.4 %collective-permute-done.2.edge_sum = f32[3,4,24,128]{3,2,1,0:T(8,128)S(1)} collective-permute-done((f32[3,4,24,128]{3,2,1,0:T(8,128)S(1)}, f32[3,4,24,128]{3,2,1,0:T(8,128)S(1)}, u32[]{:S(2)}, u32[]{:S(2)}) %collective-permute-start.2) | collective-permute-done | bytes 147488 | tf_op jit(solution)/shard_map/ppermute | solution.py:556
  14.5 0.0 collective-permute-done.3.inner_sum
  14.5 0.9 %shard_map.98 = f32[1,3,8,4096]{3,2,1,0:T(8,128)} custom-call(f32[3,4,24,128]{3,2,1,0:T(8,128)S(1)} %collective-permute-done.2.edge_sum, f32[3,4,24,128]{3,2,1,0:T(8,128)S(1)} %shard_map.97.edge, f32[3,4,24,128]{3,2,1,0:T(8,128)S(1)} %get-tuple-element.28.edge_gain, f32[3,4,40,128]{3,2,1,0:T(8,128)S(1)} %collective-permute-done.3.inner_sum, ...), custom_call_target="tpu_custom_call" | custom-call | bytes 2359296 | tf_op jit(solution)/shard_map/pallas_call | solution.py:535
  (2 shorter events, 0.0 us)
Async XLA Ops:
  0.0 0.9 %copy-start.4 = (f32[8,4096]{1,0:T(8,128)S(1)}, f32[8,4096]{1,0:T(8,128)}, u32[]{:S(2)}) copy-start(f32[8,4096]{1,0:T(8,128)} %cor.3) | copy-start | bytes 393220
  0.0 1.0 %copy-start.3 = (s32[8,4096]{1,0:T(8,128)S(1)}, s32[8,4096]{1,0:T(8,128)}, u32[]{:S(2)}) copy-start(s32[8,4096]{1,0:T(8,128)} %wet.3) | copy-start | bytes 393220
  0.0 1.1 %copy-start.2 = (s32[8,4096]{1,0:T(8,128)S(1)}, s32[8,4096]{1,0:T(8,128)}, u32[]{:S(2)}) copy-start(s32[8,4096]{1,0:T(8,128)} %level_id.3) | copy-start | bytes 393220
  0.0 0.8 %copy-start.6 = (f32[64]{0:T(128)S(1)}, f32[64]{0:T(128)}, u32[]{:S(2)}) copy-start(f32[64]{0:T(128)} %table.1) | copy-start | bytes 772
  0.0 0.8 %copy-start.5 = (s32[8,4]{0,1:T(4,128)S(1)}, s32[8,4]{0,1:T(4,128)}, u32[]{:S(2)}) copy-start(s32[8,4]{0,1:T(4,128)} %param.15) | copy-start | bytes 388
  0.0 1.3 %copy-start.1 = (f32[2,8,4096]{2,1,0:T(8,128)S(1)}, f32[2,8,4096]{2,1,0:T(8,128)}, u32[]{:S(2)}) copy-start(f32[2,8,4096]{2,1,0:T(8,128)} %tide.3) | copy-start | bytes 786436
  0.1 1.3 %copy-start = (f32[1,3,8,4096]{3,2,1,0:T(8,128)S(1)}, f32[1,3,8,4096]{3,2,1,0:T(8,128)}, u32[]{:S(2)}) copy-start(f32[1,3,8,4096]{3,2,1,0:T(8,128)} %start.3) | copy-start | bytes 1179652
  2.0 9.9 %collective-permute-start = (f32[4,48,128]{2,1,0:T(8,128)S(1)}, f32[4,48,128]{2,1,0:T(8,128)S(1)}, u32[]{:S(2)}, u32[]{:S(2)}) collective-permute-start(f32[4,48,128]{2,1,0:T(8,128)S(1)} %get-tuple-element.22), channel_id=1, source_target_pairs={{0,1},{1,2},{2,3},{3,4},{4,5},{5,6},{6,7},{7,8},{8,9},{9,10},{10,1... | collective-permute-start | bytes 294920 | tf_op jit(solution)/shard_map/ppermute | solution.py:556
  5.0 6.9 %collective-permute-start.1 = (f32[4,48,128]{2,1,0:T(8,128)S(1)}, f32[4,48,128]{2,1,0:T(8,128)S(1)}, u32[]{:S(2)}, u32[]{:S(2)}) collective-permute-start(f32[4,48,128]{2,1,0:T(8,128)S(1)} %get-tuple-element.23), channel_id=1, source_target_pairs={{0,15},{1,0},{2,1},{3,2},{4,3},{5,4},{6,5},{7,6},{8,7},{9,8},{10,9... | collective-permute-start | bytes 294920 | tf_op jit(solution)/shard_map/ppermute | solution.py:556
  10.9 3.5 %collective-permute-start.3 = (f32[3,4,40,128]{3,2,1,0:T(8,128)S(1)}, f32[3,4,40,128]{3,2,1,0:T(8,128)S(1)}, u32[]{:S(2)}, u32[]{:S(2)}) collective-permute-start(f32[3,4,40,128]{3,2,1,0:T(8,128)S(1)} %get-tuple-element.29.inner), channel_id=1, source_target_pairs={{0,16},{16,0},{1,17},{17,1},{2,18},{18,2},{3,19},{19,3},{4,20},{20... | collective-permute-start | bytes 737288 | tf_op jit(solution)/shard_map/ppermute | solution.py:556
  13.0 1.4 %collective-permute-start.2 = (f32[3,4,24,128]{3,2,1,0:T(8,128)S(1)}, f32[3,4,24,128]{3,2,1,0:T(8,128)S(1)}, u32[]{:S(2)}, u32[]{:S(2)}) collective-permute-start(f32[3,4,24,128]{3,2,1,0:T(8,128)S(1)} %shard_map.97.edge), channel_id=1, source_target_pairs={{0,16},{16,0},{1,17},{17,1},{2,18},{18,2},{3,19},{19,3},{4,20},{20... | collective-permute-start | bytes 442376 | tf_op jit(solution)/shard_map/ppermute | solution.py:556

commit v9 on v7

--- a/solution.py
+++ b/solution.py
@@ -523,10 +523,14 @@
                     done[-1].append(whole / (F32(1) - most * g))
             q = joint(*done)
             columns.append(jnp.concatenate(q, axis=0))
-        for v, x in enumerate(to_tiles(columns)):
-            out[0, f, :, pl.ds(v * LANES, LANES)] = x
-        copies.append(pltpu.make_async_copy(out.at[0, f], result.at[0, f], sems.at[f]))
-        copies[-1].start()
+        tiles = to_tiles(columns)
+        half = len(tiles) // 2
+        for n in range(2):
+            for v in range(half * n, half * n + half):
+                out[0, f, :, pl.ds(v * LANES, LANES)] = tiles[v]
+            at = (0, f, slice(None), pl.ds(half * n * LANES, half * LANES))
+            copies.append(pltpu.make_async_copy(out.at[at], result.at[at], sems.at[2 * f + n]))
+            copies[-1].start()
     for copy in copies:
         copy.wait()
 
@@ -622,7 +626,7 @@
         shape(*start_states.shape),
         [edge_sum, edge, edge_gain, inner_sum, inner, inner_gain],
         out_space=pltpu.HBM,
-        scratch=[pltpu.VMEM(start_states.shape, F32), pltpu.SemaphoreType.DMA((3,))],
+        scratch=[pltpu.VMEM(start_states.shape, F32), pltpu.SemaphoreType.DMA((6,))],
     )
 
 

time: 15.5 us -> 15.5 us (level)
  no operation moved by 1% of the time
where the time goes in v9:
time: 15.5 us; the launch traced here: 15.4 us
  starting transfers between devices  7.19 us (46%)
  Pallas kernels  4.88 us (31%)
  waiting for transfers between devices  2.27 us (15%)
  between operations  0.88 us (6%)
    ppermute x4, starting transfers between devices, passed_along(): lax.ppermute(shard, axis, [(i, (i + by) % size) for i in range(size)])  7.19 us
    pallas_call x8, Pallas kernels, call(): pl.pallas_call(kernel, out_shape=out_shape, in_specs=[pl.BlockSpec(memory...  4.88 us
    ppermute x4, waiting for transfers between devices, passed_along(): lax.ppermute(shard, axis, [(i, (i + by) % size) for i in range(size)])  2.27 us
  transfers between devices with their start and end apart: 4, of which 2 were waited for; matrix products, arithmetic and copies ran while one was open for 0% of the time, Pallas kernels for 20%

profile of v9, /device:TPU:0, one launch (start us, length us, event | category | flops | bytes accessed | tf_op | source)
XLA Modules:
  0.0 15.4 jit_solution(10876943252072199645)
XLA Ops:
  0.0 0.0 copy-start.4
  0.0 0.0 copy-start.3
  0.0 0.0 copy-start.2
  0.0 0.0 copy-start.6
  0.0 0.0 copy-start.5
  0.0 0.0 copy-start.1
  0.1 0.0 copy-start
  0.8 0.0 copy-done.6
  0.8 0.0 copy-done.5
  0.9 0.1 shard_map.92
  0.9 0.0 copy-done.4
  1.0 0.0 copy-done.3
  1.0 0.1 copy-done.2
  1.1 0.2 %shard_map.94 = (f32[2,4,32,128]{3,2,1,0:T(8,128)S(1)}, f32[1,4,32,128]{3,2,1,0:T(8,128)S(1)}) custom-call(s32[8,128]{1,0:T(8,128)S(1)} %get-tuple-element.19.held, f32[8,128]{1,0:T(8,128)S(1)} %shard_map.93.row, s32[8,4096]{1,0:T(8,128)S(1)} %copy-done.2, s32[8,4096]{1,0:T(8,128)S(1)} %copy-done.3, f32[8,4096]{1,0:T(8,128)S(1)} %copy-done.4), custom_call_target="tpu_custom_call" | custom-call | bytes 802816 | tf_op jit(solution)/shard_map/pallas_call | solution.py:541
  1.3 0.0 copy-done.1
  1.3 0.0 copy-done
  1.3 0.7 %shard_map.95 = (f32[4,48,128]{2,1,0:T(8,128)S(1)}, f32[4,48,128]{2,1,0:T(8,128)S(1)}) custom-call(f32[12,8,128]{2,1,0:T(8,128)S(1)} %shard_map.91.times, s32[4,8,128]{2,1,0:T(8,128)S(1)} %get-tuple-element.18.face, f32[1,3,8,4096]{3,2,1,0:T(8,128)S(1)} %copy-done, f32[2,8,4096]{2,1,0:T(8,128)S(1)} %copy-done.1, ...), custom_call_target="tpu_custom_call" | custom-call | bytes 1835008 | tf_op jit(solution)/shard_map/pallas_call | solution.py:541
  2.0 3.0 %collective-permute-start = (f32[4,48,128]{2,1,0:T(8,128)S(1)}, f32[4,48,128]{2,1,0:T(8,128)S(1)}, u32[]{:S(2)}, u32[]{:S(2)}) collective-permute-start(f32[4,48,128]{2,1,0:T(8,128)S(1)} %get-tuple-element.22), channel_id=1, source_target_pairs={{0,1},{1,2},{2,3},{3,4},{4,5},{5,6},{6,7},{7,8},{8,9},{9,10},{10,1... | collective-permute-start | bytes 294920 | tf_op jit(solution)/shard_map/ppermute | solution.py:562
  5.0 4.1 %collective-permute-start.1 = (f32[4,48,128]{2,1,0:T(8,128)S(1)}, f32[4,48,128]{2,1,0:T(8,128)S(1)}, u32[]{:S(2)}, u32[]{:S(2)}) collective-permute-start(f32[4,48,128]{2,1,0:T(8,128)S(1)} %get-tuple-element.23), channel_id=1, source_target_pairs={{0,15},{1,0},{2,1},{3,2},{4,3},{5,4},{6,5},{7,6},{8,7},{9,8},{10,9... | collective-permute-start | bytes 294920 | tf_op jit(solution)/shard_map/ppermute | solution.py:562
  9.0 1.8 %shard_map.96 = (f32[3,4,64,128]{3,2,1,0:T(8,128)S(1)}, f32[2,4,64,128]{3,2,1,0:T(8,128)S(1)}, f32[3,4,64,128]{3,2,1,0:T(8,128)S(1)}, f32[3,4,40,128]{3,2,1,0:T(...) custom-call(f32[12,8,128]{2,1,0:T(8,128)S(1)} %shard_map.91.times, ...), custom_call_target="tpu_custom_call" | custom-call | bytes 3031040 | tf_op jit(solution)/shard_map/pallas_call | solution.py:541
  10.9 0.1 collective-permute-start.3
  11.0 0.9 %collective-permute-done.pe = f32[4,48,128]{2,1,0:T(8,128)S(1)} collective-permute-done((f32[4,48,128]{2,1,0:T(8,128)S(1)}, f32[4,48,128]{2,1,0:T(8,128)S(1)}, u32[]{:S(2)}, u32[]{:S(2)}) %collective-permute-start) | collective-permute-done | bytes 98336 | tf_op jit(solution)/shard_map/ppermute | solution.py:562
  11.9 0.0 collective-permute-done.1.pw
  11.9 1.2 %shard_map.97.edge = f32[3,4,24,128]{3,2,1,0:T(8,128)S(1)} custom-call(f32[12,8,128]{2,1,0:T(8,128)S(1)} %shard_map.91.times, f32[4,48,128]{2,1,0:T(8,128)S(1)} %collective-permute-done.pe, f32[4,48,128]{2,1,0:T(8,128)S(1)} %collective-permute-done.1.pw, f32[3,4,64,128]{3,2,1,0:T(8,128)S(1)} %get-tuple-element.24.last, ...), custom_call_target="tpu_custom_call" | custom-call | bytes 2916352 | tf_op jit(solution)/shard_map/pallas_call | solution.py:541
  13.0 0.1 collective-permute-start.2
  13.1 1.4 %collective-permute-done.2.edge_sum = f32[3,4,24,128]{3,2,1,0:T(8,128)S(1)} collective-permute-done((f32[3,4,24,128]{3,2,1,0:T(8,128)S(1)}, f32[3,4,24,128]{3,2,1,0:T(8,128)S(1)}, u32[]{:S(2)}, u32[]{:S(2)}) %collective-permute-start.2) | collective-permute-done | bytes 147488 | tf_op jit(solution)/shard_map/ppermute | solution.py:562
  14.5 0.0 collective-permute-done.3.inner_sum
  14.5 0.9 %shard_map.98 = f32[1,3,8,4096]{3,2,1,0:T(8,128)} custom-call(f32[3,4,24,128]{3,2,1,0:T(8,128)S(1)} %collective-permute-done.2.edge_sum, f32[3,4,24,128]{3,2,1,0:T(8,128)S(1)} %shard_map.97.edge, f32[3,4,24,128]{3,2,1,0:T(8,128)S(1)} %get-tuple-element.28.edge_gain, f32[3,4,40,128]{3,2,1,0:T(8,128)S(1)} %collective-permute-done.3.inner_sum, ...), custom_call_target="tpu_custom_call" | custom-call | bytes 2359296 | tf_op jit(solution)/shard_map/pallas_call | solution.py:541
  (2 shorter events, 0.0 us)
Async XLA Ops:
  0.0 0.9 %copy-start.4 = (f32[8,4096]{1,0:T(8,128)S(1)}, f32[8,4096]{1,0:T(8,128)}, u32[]{:S(2)}) copy-start(f32[8,4096]{1,0:T(8,128)} %cor.3) | copy-start | bytes 393220
  0.0 1.0 %copy-start.3 = (s32[8,4096]{1,0:T(8,128)S(1)}, s32[8,4096]{1,0:T(8,128)}, u32[]{:S(2)}) copy-start(s32[8,4096]{1,0:T(8,128)} %wet.3) | copy-start | bytes 393220
  0.0 1.1 %copy-start.2 = (s32[8,4096]{1,0:T(8,128)S(1)}, s32[8,4096]{1,0:T(8,128)}, u32[]{:S(2)}) copy-start(s32[8,4096]{1,0:T(8,128)} %level_id.3) | copy-start | bytes 393220
  0.0 0.8 %copy-start.6 = (f32[64]{0:T(128)S(1)}, f32[64]{0:T(128)}, u32[]{:S(2)}) copy-start(f32[64]{0:T(128)} %table.1) | copy-start | bytes 772
  0.0 0.8 %copy-start.5 = (s32[8,4]{0,1:T(4,128)S(1)}, s32[8,4]{0,1:T(4,128)}, u32[]{:S(2)}) copy-start(s32[8,4]{0,1:T(4,128)} %param.15) | copy-start | bytes 388
  0.0 1.3 %copy-start.1 = (f32[2,8,4096]{2,1,0:T(8,128)S(1)}, f32[2,8,4096]{2,1,0:T(8,128)}, u32[]{:S(2)}) copy-start(f32[2,8,4096]{2,1,0:T(8,128)} %tide.3) | copy-start | bytes 786436
  0.1 1.3 %copy-start = (f32[1,3,8,4096]{3,2,1,0:T(8,128)S(1)}, f32[1,3,8,4096]{3,2,1,0:T(8,128)}, u32[]{:S(2)}) copy-start(f32[1,3,8,4096]{3,2,1,0:T(8,128)} %start.3) | copy-start | bytes 1179652
  2.0 9.9 %collective-permute-start = (f32[4,48,128]{2,1,0:T(8,128)S(1)}, f32[4,48,128]{2,1,0:T(8,128)S(1)}, u32[]{:S(2)}, u32[]{:S(2)}) collective-permute-start(f32[4,48,128]{2,1,0:T(8,128)S(1)} %get-tuple-element.22), channel_id=1, source_target_pairs={{0,1},{1,2},{2,3},{3,4},{4,5},{5,6},{6,7},{7,8},{8,9},{9,10},{10,1... | collective-permute-start | bytes 294920 | tf_op jit(solution)/shard_map/ppermute | solution.py:562
  5.0 6.9 %collective-permute-start.1 = (f32[4,48,128]{2,1,0:T(8,128)S(1)}, f32[4,48,128]{2,1,0:T(8,128)S(1)}, u32[]{:S(2)}, u32[]{:S(2)}) collective-permute-start(f32[4,48,128]{2,1,0:T(8,128)S(1)} %get-tuple-element.23), channel_id=1, source_target_pairs={{0,15},{1,0},{2,1},{3,2},{4,3},{5,4},{6,5},{7,6},{8,7},{9,8},{10,9... | collective-permute-start | bytes 294920 | tf_op jit(solution)/shard_map/ppermute | solution.py:562
  10.9 3.6 %collective-permute-start.3 = (f32[3,4,40,128]{3,2,1,0:T(8,128)S(1)}, f32[3,4,40,128]{3,2,1,0:T(8,128)S(1)}, u32[]{:S(2)}, u32[]{:S(2)}) collective-permute-start(f32[3,4,40,128]{3,2,1,0:T(8,128)S(1)} %get-tuple-element.29.inner), channel_id=1, source_target_pairs={{0,16},{16,0},{1,17},{17,1},{2,18},{18,2},{3,19},{19,3},{4,20},{20... | collective-permute-start | bytes 737288 | tf_op jit(solution)/shard_map/ppermute | solution.py:562
  13.0 1.4 %collective-permute-start.2 = (f32[3,4,24,128]{3,2,1,0:T(8,128)S(1)}, f32[3,4,24,128]{3,2,1,0:T(8,128)S(1)}, u32[]{:S(2)}, u32[]{:S(2)}) collective-permute-start(f32[3,4,24,128]{3,2,1,0:T(8,128)S(1)} %shard_map.97.edge), channel_id=1, source_target_pairs={{0,16},{16,0},{1,17},{17,1},{2,18},{18,2},{3,19},{19,3},{4,20},{20... | collective-permute-start | bytes 442376 | tf_op jit(solution)/shard_map/ppermute | solution.py:562
